TPU v7x, 32 devices: a whole 2x2x4 slice. The times are simulated.
32 devices in a mesh: grp: 2 (over x), slot: 4 (over y, core), site: 4 (over z).
Axes of the slice: x: 2, y: 2, z: 4, core: 2. Of those that a mesh axis runs over, the one named last changes fastest.
Arguments:
- field: bfloat16 [8, 2048, 4096], P('grp', 'slot', 'site'), parts along dimension 0, may hold values from -6 to 6
- time_row: bfloat16 [2048], replicated, may hold values from -0.125 to 0.125
- sp_weight: bfloat16 [4096, 2048], P('site'), may hold values from -0.1875 to 0.1875
- offsets: int32 [4096], P('site'), may hold values from 0 to 1024
- noise: float32 [4096], P('site'), may hold values from 0.1 to 1
Outputs:
- image: bfloat16 [8, 2048, 4096], P('grp', 'slot', 'site'), parts along dimension 0
There are 2 independent parts, one for each index of `grp`. A program takes and returns all parts, laid end to end along the dimension named above; an argument that names none is the same for every part. Nothing has to cross between parts.
All inputs are finite; a program needn't handle non-finite values.
Results may differ from a plain program's by a relative error of at most 0.0048.
Values may be sent and summed in bfloat16 or wider, within the bound.
No kernel may reach another device: no remote copies, remote signals or barrier semaphores. Data moves between devices by JAX's collectives and lax.ppermute only.
A program may use at most 128 MiB of HBM per device.

v0:
```python
import jax
import jax.numpy as jnp
from jax import lax
from jax.sharding import PartitionSpec as P


def with_halo(block, sides, width):
    for axis, dim in sides:
        count = lax.axis_size(axis)
        forward = [(i, i + 1) for i in range(count - 1)]
        backward = [(target, source) for source, target in forward]
        low = lax.ppermute(
            lax.slice_in_dim(block, block.shape[dim] - width, None, axis=dim), axis, forward
        )
        high = lax.ppermute(lax.slice_in_dim(block, 0, width, axis=dim), axis, backward)
        block = jnp.concatenate([low, block, high], axis=dim)
    return block


def circulant_rows(row, count):
    length = row.shape[0]
    shifted = jnp.concatenate([row[1:], row[:1]])
    tiled = jnp.tile(shifted, count + 1)[: count * (length + 1)]
    table = tiled.reshape(count, length + 1)[:, :length]
    return table[:, ::-1]


def on_device(field, time_row, sp_weight, offsets, noise):
    probes, slot_dev, site_dev = field.shape
    slots = time_row.shape[0]
    first_slot = lax.axis_index("slot") * slot_dev
    doubled = jnp.concatenate([time_row, time_row])
    rolled = lax.dynamic_slice_in_dim(doubled, first_slot, slots, 0)
    own_rows = circulant_rows(rolled, slot_dev)
    mixed = jnp.einsum(
        "ab,pbs->pas",
        own_rows,
        lax.all_gather(field, "slot", axis=1, tiled=True),
        preferred_element_type=jnp.float32,
    ).astype(jnp.bfloat16)
    padded = with_halo(mixed, (("site", 2),), site_dev // 2)
    patch = padded.shape[2]
    col_patch = jnp.arange(patch, dtype=jnp.int32)
    band_mask = (col_patch[None, :] >= offsets[:, None]) & (
        col_patch[None, :] < offsets[:, None] + site_dev
    )
    band = jnp.where(band_mask, sp_weight, jnp.zeros_like(sp_weight))
    spatial = jnp.einsum("ptj,sj->pts", padded, band, preferred_element_type=jnp.float32)
    image = spatial + noise[None, None, :] * field.astype(jnp.float32)
    return image.astype(jnp.bfloat16)


def solution(mesh):
    in_specs = (P("grp", "slot", "site"), P(), P("site", None), P("site"), P("site"))
    out_specs = P("grp", "slot", "site")
    return jax.shard_map(
        on_device, mesh=mesh, in_specs=in_specs, out_specs=out_specs, check_vma=False
    )
```

profile of v0, /device:TPU:0, one launch (start us, length us, event | category | flops | bytes accessed | tf_op | source)
XLA Modules:
  0.0 207.6 jit_solution(17185582052407370592)
XLA Ops:
  6.5 0.0 copy-start.1
  6.5 0.0 all-gather.2.cloned.1.call-start
  6.5 0.7 all-gather.2.cloned.1.call-update
  7.3 0.0 copy-done.1
  7.3 0.1 fusion.18
  7.4 0.1 slice.24
  7.5 0.5 slice.25
  8.0 0.7 pad_maximum_fusion
  8.7 0.3 tile.4
  9.0 2.3 %tile.10 = bf16[1050624]{0:T(1024)(128)(2,1)} reshape(bf16[513,2048]{1,0:T(8,128)(2,1)S(1)} %tile.4) | data formatting | bytes 4202496 | tf_op jit(solution)/shard_map/tile | solution.py:23
  11.2 0.0 slice-start
  11.2 1.6 slice-done
  12.8 4.9 %reshape.8 = bf16[512,2049]{1,0:T(8,128)(2,1)} reshape(bf16[1049088]{0:T(1024)(128)(2,1)S(1)} %slice-done) | data formatting | bytes 4196352 | tf_op jit(solution)/shard_map/reshape | solution.py:24
  17.7 0.0 slice-start.1
  17.7 1.9 slice-done.1
  19.6 22.5 %rev.3 = bf16[512,2048]{1,0:T(8,128)(2,1)} reverse(bf16[512,2048]{1,0:T(8,128)(2,1)S(1)} %slice-done.1), dimensions={1} | reverse | bytes 4194304 | tf_op jit(solution)/shard_map/rev | solution.py:25
  42.2 75.4 %all-gather.2.cloned.1.call-done = bf16[4,2048,1024]{2,1,0:T(8,128)(2,1)} async-done(((bf16[4,512,1024]{2,1,0:T(8,128)(2,1)}), bf16[4,2048,1024]{2,1,0:T(8,128)(2,1)}) %all-gather.2.cloned.1.call-update) | async-done | bytes 16777232 | tf_op jit(solution)/shard_map/all_gather | solution.py:38
  117.6 13.0 %convert_bitcast_fusion = bf16[4,512,1024]{2,1,0:T(8,128)(2,1)S(1)} fusion(bf16[4,2048,1024]{2,1,0:T(8,128)(2,1)} %all-gather.2.cloned.1.call-done, bf16[512,2048]{1,0:T(8,128)(2,1)} %rev.3), kind=kOutput, calls=%fused_computation.14 | convolution fusion | flops 8592031744 | bytes 23068672 | tf_op jit(solution)/shard_map/ab,pbs->pas/dot_general | solution.py:35
  130.7 0.0 copy-start.2
  130.7 0.0 copy-start
  130.7 0.0 copy-start.4
  130.7 0.4 fusion.21
  131.1 3.8 %collective-permute-start = (bf16[4,512,512]{2,1,0:T(8,128)(2,1)S(1)}, bf16[4,512,512]{2,1,0:T(8,128)(2,1)S(1)}, u32[]{:S(2)}, u32[]{:S(2)}) collective-permute-start(bf16[4,512,512]{2,1,0:T(8,128)(2,1)S(1)} %get-tuple-element.5), channel_id=1, source_target_pairs={{0,1},{1,2},{2,3},{4,5},{5,6},{6,7},{8,9},{9,10},{10,11},{12,13},{... | collective-permute-start | bytes 6291464 | tf_op jit(solution)/shard_map/ppermute | solution.py:12
  134.9 1.5 collective-permute-start.1
  136.4 0.0 copy-done.2
  136.4 43.7 %collective-permute-done = bf16[4,512,512]{2,1,0:T(8,128)(2,1)S(1)} collective-permute-done((bf16[4,512,512]{2,1,0:T(8,128)(2,1)S(1)}, bf16[4,512,512]{2,1,0:T(8,128)(2,1)S(1)}, u32[]{:S(2)}, u32[]{:S(2)}) %collective-permute-start) | collective-permute-done | bytes 2097184 | tf_op jit(solution)/shard_map/ppermute | solution.py:12
  180.1 0.0 copy-start.3
  180.1 1.3 copy-done.3
  181.4 3.0 %collective-permute-done.1 = bf16[4,512,512]{2,1,0:T(8,128)(2,1)} collective-permute-done((bf16[4,512,512]{2,1,0:T(8,128)(2,1)S(1)}, bf16[4,512,512]{2,1,0:T(8,128)(2,1)}, u32[]{:S(2)}, u32[]{:S(2)}) %collective-permute-start.1) | collective-permute-done | bytes 2097184 | tf_op jit(solution)/shard_map/ppermute | solution.py:15
  184.4 0.0 copy-done
  184.4 0.0 copy-done.4
  184.4 16.4 %add_convert_fusion = bf16[4,512,1024]{2,1,0:T(8,128)(2,1)} fusion(bf16[4,512,1024]{2,1,0:T(8,128)(2,1)S(1)} %copy-done, f32[1024]{0:T(1024)S(1)} %copy-done.4, bf16[1024,2048]{1,0:T(8,128)(2,1)} %param.7, s32[1024]{0:T(1024)S(1)} %broadcast_add_fusion, s32[1024]{0:T(1024)S(1)} %copy-done.2, bf16[4,512,512]{2,1,0:T(8,128)(2,1)} %collective-permute-done.1, ...), kind=kOutput, calls=%fused_computation.6 | convolution fusion | flops 8631877632 | bytes 20983808 | tf_op jit(solution)/shard_map/ptj,sj->pts/dot_general | solution.py:48
  (1 shorter events, 0.0 us)
Async XLA Ops:
  6.5 0.7 copy-start.1
  6.5 111.1 %all-gather.2.cloned.1.call-start = ((), (), s32[]{:S(2)}) async-start(), calls=%async_computation | async-start | bytes 20971520 | tf_op jit(solution)/shard_map/all_gather | solution.py:38
  11.2 1.6 slice-start
  17.7 1.9 slice-start.1
  130.7 5.7 %copy-start.2 = (s32[1024]{0:T(1024)S(1)}, s32[1024]{0:T(1024)}, u32[]{:S(2)}) copy-start(s32[1024]{0:T(1024)} %param.8) | copy-start | bytes 12292
  130.7 53.7 %copy-start = (bf16[4,512,1024]{2,1,0:T(8,128)(2,1)S(1)}, bf16[4,512,1024]{2,1,0:T(8,128)(2,1)}, u32[]{:S(2)}) copy-start(bf16[4,512,1024]{2,1,0:T(8,128)(2,1)} %param.5) | copy-start | bytes 12582916
  130.7 53.7 %copy-start.4 = (f32[1024]{0:T(1024)S(1)}, f32[1024]{0:T(1024)}, u32[]{:S(2)}) copy-start(f32[1024]{0:T(1024)} %param.9) | copy-start | bytes 12292
  131.1 49.0 %collective-permute-start = (bf16[4,512,512]{2,1,0:T(8,128)(2,1)S(1)}, bf16[4,512,512]{2,1,0:T(8,128)(2,1)S(1)}, u32[]{:S(2)}, u32[]{:S(2)}) collective-permute-start(bf16[4,512,512]{2,1,0:T(8,128)(2,1)S(1)} %get-tuple-element.5), channel_id=1, source_target_pairs={{0,1},{1,2},{2,3},{4,5},{5,6},{6,7},{8,9},{9,10},{10,11},{12,13},{... | collective-permute-start | bytes 6291464 | tf_op jit(solution)/shard_map/ppermute | solution.py:12
  134.9 49.5 %collective-permute-start.1 = (bf16[4,512,512]{2,1,0:T(8,128)(2,1)S(1)}, bf16[4,512,512]{2,1,0:T(8,128)(2,1)}, u32[]{:S(2)}, u32[]{:S(2)}) collective-permute-start(bf16[4,512,512]{2,1,0:T(8,128)(2,1)S(1)} %get-tuple-element.6), channel_id=1, source_target_pairs={{1,0},{2,1},{3,2},{5,4},{6,5},{7,6},{9,8},{10,9},{11,10},{13,12},{... | collective-permute-start | bytes 6291464 | tf_op jit(solution)/shard_map/ppermute | solution.py:15
  180.1 1.3 copy-start.3
Sparse Core Ops, SparseCore 0:
  8.9 108.6 all-gather.1
where the time goes:
time: 208 us
  waiting for transfers between devices  123 us (59%)
  local copies, waits for them, and re-layouts  35.8 us (17%)
  matrix products  29.4 us (14%)
  between operations  13.5 us (6%)
  starting transfers between devices  5.26 us (3%)
    all_gather x1, waiting for transfers between devices, on_device(): lax.all_gather(field, 'slot', axis=1, tiled=True)  75.4 us
    ppermute x1, waiting for transfers between devices, with_halo(): lax.ppermute(lax.slice_in_dim(block, block.shape[dim] - width, None, axis...  43.7 us
    rev x1, local copies, waits for them, and re-layouts, circulant_rows(): return table[:, ::-1]  22.5 us
    dot_general x1, matrix products, on_device(): jnp.einsum('ptj,sj->pts', padded, band, preferred_element_type=jnp.float32)  16.4 us
    dot_general x1, matrix products, on_device(): jnp.einsum('ab,pbs->pas', own_rows, lax.all_gather(field, 'slot', axis=1,...  13 us
    reshape x1, local copies, waits for them, and re-layouts, circulant_rows(): table = tiled.reshape(count, length + 1)[:, :length]  4.87 us
  transfers between devices with their start and end apart: 3, of which 3 were waited for; matrix products, arithmetic and copies ran while one was open for 15% of the time, Pallas kernels for 0%

commit v1 on v0

v1 whole, which is shorter than its diff:
```python
import functools

import jax
import jax.numpy as jnp
from jax import lax
from jax.experimental import pallas as pl
from jax.experimental.pallas import tpu as pltpu
from jax.sharding import PartitionSpec as P

F32 = jnp.float32
BF16 = jnp.bfloat16
VMEM_BYTES = 24 * 1024 * 1024


def dot(a, b):
    return lax.dot_general(a, b, (((1,), (0,)), ((), ())), preferred_element_type=F32)


def dot_t(a, b):
    return lax.dot_general(a, b, (((1,), (1,)), ((), ())), preferred_element_type=F32)


def params():
    return pltpu.CompilerParams(vmem_limit_bytes=VMEM_BYTES)


BRIEF = pl.CostEstimate(flops=0, bytes_accessed=0, transcendentals=0)


def table_kernel(order, rows, core_ref, row_ref, out_ref):
    first = core_ref[0] == 0
    length = row_ref.shape[1]
    lags = pltpu.roll(jnp.broadcast_to(row_ref[...], (16, length)), 0, 1, stride=1, stride_axis=0)

    def group(g, carry):
        base = g * 16
        whole = pltpu.roll(lags, base, 1)
        for m, (a, b) in enumerate(zip(*order)):
            left = whole[:, a * rows : (a + 1) * rows]
            right = whole[:, b * rows : (b + 1) * rows]
            picked = left if a == b else jnp.where(first, left, right)
            out_ref[pl.ds(pl.multiple_of(base, 16), 16), m * rows : (m + 1) * rows] = picked.astype(BF16)
        return carry

    lax.fori_loop(0, rows // 16, group, 0)


def time_table(time_row, core, order, rows):
    reversed_row = jnp.concatenate([time_row[:1], time_row[1:][::-1]]).astype(F32)[None, :]
    length = time_row.shape[0]
    return pl.pallas_call(
        functools.partial(table_kernel, order, rows),
        out_shape=jax.ShapeDtypeStruct((rows, length), BF16),
        in_specs=[
            pl.BlockSpec(memory_space=pltpu.SMEM),
            pl.BlockSpec(memory_space=pltpu.VMEM),
        ],
        out_specs=pl.BlockSpec(memory_space=pltpu.VMEM),
        compiler_params=params(),
        cost_estimate=BRIEF,
        name="time_table",
    )(core, reversed_row)


ANY = pl.BlockSpec(memory_space=pl.ANY)


def space_kernel(half, noisy, *refs):
    low, mid, high, band = refs[:4]
    out = refs[-1]
    width = mid.shape[2]
    total = dot_t(mid[0], band[:, half : half + width])
    total += dot_t(low[0], band[:, :half])
    total += dot_t(high[0], band[:, half + width :])
    if noisy:
        noise, own = refs[4:6]
        total += noise[...] * own[0].astype(F32)
        out[0] = total.astype(BF16)
    else:
        out[...] = total.astype(BF16)


def space(low, mid, high, band, base, start, size, image=None):
    rows, width = mid.shape[1:]
    half = low.shape[2]
    step = min(256, size)
    skip, per = start // step, width // step

    def probe(j):
        return lax.div(j + skip, per)

    def site(j):
        return lax.rem(j + skip, per)

    args = [low, mid, high, band]
    specs = [
        pl.BlockSpec((1, rows, half), lambda j: (probe(j), 0, 0)),
        pl.BlockSpec((1, rows, width), lambda j: (probe(j) + base, 0, 0)),
        pl.BlockSpec((1, rows, half), lambda j: (probe(j), 0, 0)),
        pl.BlockSpec((step, band.shape[1]), lambda j: (site(j), 0)),
    ]
    aliases = {}
    if image is not None:
        noise, field, first, old = image
        args += [noise, field]
        out_spec = pl.BlockSpec((1, rows, step), lambda j: (probe(j) + first, 0, site(j)))
        specs += [pl.BlockSpec((1, step), lambda j: (0, site(j))), out_spec]
        if old is not None:
            args.append(old)
            specs.append(ANY)
            aliases = {len(args) - 1: 0}
        out_shape = jax.ShapeDtypeStruct(field.shape, BF16)
    else:
        out_shape = jax.ShapeDtypeStruct((rows, size), BF16)
        out_spec = pl.BlockSpec((rows, step), lambda j: (0, j))
    return pl.pallas_call(
        functools.partial(space_kernel, half, image is not None),
        grid=(size // step,),
        out_shape=out_shape,
        in_specs=specs,
        out_specs=out_spec,
        input_output_aliases=aliases,
        compiler_params=params(),
        cost_estimate=BRIEF,
        name="space",
    )(*args)


def mix_kernel(count, noisy, *refs):
    table = refs[0]
    blocks = refs[1 : 1 + count]
    out = refs[-1]
    rows = blocks[0].shape[0]
    total = dot(table[:, :rows], blocks[0][...])
    for m in range(1, count):
        total += dot(table[:, m * rows : (m + 1) * rows], blocks[m][...])
    if noisy:
        noise, own = refs[1 + count : 3 + count]
        total += noise[...] * own[0].astype(F32)
    out[0] = total.astype(BF16)


def mix(table, blocks, image=None):
    rows, width = blocks[0].shape
    step = min(512, width)
    args = [table] + list(blocks)
    specs = [pl.BlockSpec(table.shape, lambda j: (0, 0))]
    specs += [pl.BlockSpec((rows, step), lambda j: (0, j))] * len(blocks)
    aliases = {}
    if image is not None:
        noise, field, base, start, old = image
        skip, per = start // step, field.shape[2] // step

        def probe(j):
            return lax.div(j + skip, per) + base

        def site(j):
            return lax.rem(j + skip, per)

        args += [noise, field, old]
        out_spec = pl.BlockSpec((1, rows, step), lambda j: (probe(j), 0, site(j)))
        specs += [pl.BlockSpec((1, step), lambda j: (0, site(j))), out_spec, ANY]
        aliases = {len(args) - 1: 0}
        out_shape = jax.ShapeDtypeStruct(field.shape, BF16)
    else:
        out_shape = jax.ShapeDtypeStruct((1, rows, width), BF16)
        out_spec = pl.BlockSpec((1, rows, step), lambda j: (0, 0, j))
    return pl.pallas_call(
        functools.partial(mix_kernel, len(blocks), image is not None),
        grid=(width // step,),
        out_shape=out_shape,
        in_specs=specs,
        out_specs=out_spec,
        input_output_aliases=aliases,
        compiler_params=params(),
        cost_estimate=BRIEF,
        name="mix",
    )(*args)


def after(value, *others):
    return lax.optimization_barrier((value,) + others)[0]


def on_device(field, time_row, sp_weight, offsets, noise):
    probes, rows, width = field.shape
    half = width // 2
    count = lax.axis_size("slot")
    sites = lax.axis_size("site")
    core = (lax.axis_index("slot") % 2).astype(jnp.int32).reshape(1)
    noise = noise[None, :]

    swap = [(i, i ^ 1) for i in range(count)]
    shifts = range(2, count, 2)
    up = [(i, i + 1) for i in range(sites - 1)]
    down = [(i + 1, i) for i in range(sites - 1)]

    def to_core(block):
        return lax.ppermute(block, "slot", swap)

    def to_chips(block):
        return [lax.ppermute(block, "slot", [(i, (i + s) % count) for i in range(count)]) for s in shifts]

    def halo(block):
        return (
            lax.ppermute(block[:, :, width - half :], "site", up),
            lax.ppermute(block[:, :, :half], "site", down),
        )

    order = ([0, 1], [0, count - 1])
    for s in shifts:
        order[0].extend([(-s) % count, (1 - s) % count])
        order[1].extend([(-s) % count, (-1 - s) % count])

    def gathered(own, far, *others):
        blocks = [own, to_core(own)]
        for got in far:
            got = after(got, *others)
            blocks += [got, to_core(got)]
        return blocks

    firsts = probes // 2
    own, far = [], []
    rest = field
    for p in range(firsts):
        own.append(rest[p])
        far.append(to_chips(own[p]))
        rest = after(field, own[p])
        if p == 0:
            low, high = halo(rest[firsts:])

    table = time_table(time_row, core, order, rows)
    col = jnp.arange(sp_weight.shape[1], dtype=jnp.int32)
    mask = (col[None, :] >= offsets[:, None]) & (col[None, :] < offsets[:, None] + width)
    band = jnp.where(mask, sp_weight, jnp.zeros_like(sp_weight))

    mixed = [mix(table, gathered(own[0], far[0]))]
    columns = (probes - firsts) * width
    chunks = [(0, columns - half), (columns - half, half)]
    sent = []
    weights = band
    for start, size in chunks:
        block = space(low, field, high, weights, firsts, start, size)
        sent.append((block, to_chips(block)))
        weights = after(band, block)
    for p in range(1, firsts):
        mixed.append(mix(table, gathered(own[p], far[p], mixed[-1], block)))

    image = None
    for p in range(firsts):
        got_low, got_high = halo(mixed[p])
        image = space(got_low, mixed[p], got_high, band, 0, 0, width, image=(noise, field, p, image))
    for (start, _), (block, got) in zip(chunks, sent):
        image = mix(table, gathered(block, got, image), image=(noise, field, firsts, start, image))
    return image


def solution(mesh):
    in_specs = (P("grp", "slot", "site"), P(), P("site", None), P("site"), P("site"))
    out_specs = P("grp", "slot", "site")
    return jax.shard_map(
        on_device, mesh=mesh, in_specs=in_specs, out_specs=out_specs, check_vma=False
    )
```

time: 208 us -> 107 us (0.51)
  waiting for transfers between devices: 123 us -> 35.9 us
  Pallas kernels: 0 us -> 35 us
  matrix products: 29.4 us -> 0 us
  local copies, waits for them, and re-layouts: 35.8 us -> 6.6 us
  starting transfers between devices: 5.26 us -> 23.1 us
  between operations: 13.5 us -> 0.23 us
  other arithmetic: 0.83 us -> 5.18 us
    all_gather x1 -> x0, waiting for transfers between devices: 75.4 us -> none  [on_device(): lax.all_gather(field, 'slot', axis=1, tiled=True)]
    pallas_call x0 -> x9, Pallas kernels: none -> 35 us  [the longest x4 16.6 us: space(): pl.pallas_call(functools.partial(space_kernel, half, image is not None),...]
    dot_general x2 -> x0, matrix products: 29.4 us -> none  [the longest x1 16.4 us: on_device(): jnp.einsum('ptj,sj->pts', padded, band, preferred_element_type=jnp.float32)]
    rev x1 -> x0, local copies, waits for them, and re-layouts: 22.5 us -> none  [circulant_rows(): return table[:, ::-1]]
    ppermute x2 -> x18, starting transfers between devices: 5.26 us -> 23.1 us  [the longest x3 11.6 us: halo(): lax.ppermute(block[:, :, width - half:], 'site', up)]
    ppermute x2 -> x18, waiting for transfers between devices: 46.7 us -> 35.9 us  [the longest x4 20 us: to_chips(): lax.ppermute(block, 'slot', [(i, (i + s) % count) for i in range(count)])]
    reshape x1 -> x0, local copies, waits for them, and re-layouts: 4.87 us -> none  [circulant_rows(): table = tiled.reshape(count, length + 1)[:, :length]]
    select_n x0 -> x1, other arithmetic: none -> 4.41 us  [on_device(): band = jnp.where(mask, sp_weight, jnp.zeros_like(sp_weight))]
  transfers between devices with their start and end apart: 3 -> 18, of which waited for: 3 -> 10; matrix products, arithmetic and copies ran while one was open for 15% -> 10% of each run, Pallas kernels for 0% -> 31%
where the time goes in v1:
time: 107 us; the launch traced here: 106 us
  waiting for transfers between devices  35.9 us (34%)
  Pallas kernels  35 us (33%)
  starting transfers between devices  23.1 us (22%)
  local copies, waits for them, and re-layouts  6.6 us (6%)
  other arithmetic  5.18 us (5%)
    ppermute x4, waiting for transfers between devices, to_chips(): lax.ppermute(block, 'slot', [(i, (i + s) % count) for i in range(count)])  20 us
    pallas_call x4, Pallas kernels, space(): pl.pallas_call(functools.partial(space_kernel, half, image is not None),...  16.6 us
    pallas_call x4, Pallas kernels, mix(): pl.pallas_call(functools.partial(mix_kernel, len(blocks), image is not No...  14.8 us
    ppermute x3, starting transfers between devices, halo(): lax.ppermute(block[:, :, width - half:], 'site', up)  11.6 us
    ppermute x3, waiting for transfers between devices, halo(): lax.ppermute(block[:, :, :half], 'site', down)  9.16 us
    ppermute x4, starting transfers between devices, to_chips(): lax.ppermute(block, 'slot', [(i, (i + s) % count) for i in range(count)])  6.73 us
    select_n x1, other arithmetic, on_device(): band = jnp.where(mask, sp_weight, jnp.zeros_like(sp_weight))  4.41 us
    ppermute x3, starting transfers between devices, halo(): lax.ppermute(block[:, :, :half], 'site', down)  3.88 us
  transfers between devices with their start and end apart: 18, of which 10 were waited for; matrix products, arithmetic and copies ran while one was open for 10% of the time, Pallas kernels for 31%

profile of v1, /device:TPU:0, one launch (start us, length us, event | category | flops | bytes accessed | tf_op | source)
XLA Modules:
  0.0 106.1 jit_solution(6992631057989381753)
XLA Ops:
  0.0 0.0 copy-start.3
  0.0 1.3 %slice_bitcast_fusion.1.refs_1_ = bf16[512,1024]{1,0:T(8,128)(2,1)S(1)} fusion(bf16[4,512,1024]{2,1,0:T(8,128)(2,1)} %refs_6_.3), kind=kLoop, calls=%fused_computation.5 | loop fusion | bytes 2097152 | tf_op jit(solution)/shard_map/squeeze | solution.py:226
  1.3 0.0 copy-start.2
  1.3 3.0 %collective-permute-start.9 = (bf16[512,1024]{1,0:T(8,128)(2,1)S(1)}, bf16[512,1024]{1,0:T(8,128)(2,1)}, u32[]{:S(2)}, u32[]{:S(2)}) collective-permute-start(bf16[512,1024]{1,0:T(8,128)(2,1)S(1)} %slice_bitcast_fusion.1.refs_1_), channel_id=1, source_target_pairs={{0,8},{4,12},{8,0},{12,4},{1,9},{5,13},{9,1},{13,5},{2,10},{6,14},... | collective-permute-start | bytes 3145736 | tf_op jit(solution)/shard_map/ppermute | solution.py:202
  4.4 0.0 collective-permute-start.8
  4.4 3.0 %fusion.2 = (bf16[2,512,512]{2,1,0:T(8,128)(2,1)}, bf16[2,512,512]{2,1,0:T(8,128)(2,1)}) fusion(bf16[4,512,1024]{2,1,0:T(8,128)(2,1)} %refs_6_.3), kind=kLoop, calls=%fused_computation.8 | loop fusion | bytes 4194304 | tf_op jit(solution)/shard_map/slice | solution.py:207
  7.4 3.5 %collective-permute-start = (bf16[2,512,512]{2,1,0:T(8,128)(2,1)}, bf16[2,512,512]{2,1,0:T(8,128)(2,1)S(1)}, u32[]{:S(2)}, u32[]{:S(2)}) collective-permute-start(bf16[2,512,512]{2,1,0:T(8,128)(2,1)} %get-tuple-element.16), channel_id=1, source_target_pairs={{0,1},{1,2},{2,3},{4,5},{5,6},{6,7},{8,9},{9,10},{10,11},{12,13},{... | collective-permute-start | bytes 3145736 | tf_op jit(solution)/shard_map/ppermute | solution.py:206
  10.9 1.3 %collective-permute-start.1 = (bf16[2,512,512]{2,1,0:T(8,128)(2,1)}, bf16[2,512,512]{2,1,0:T(8,128)(2,1)}, u32[]{:S(2)}, u32[]{:S(2)}) collective-permute-start(bf16[2,512,512]{2,1,0:T(8,128)(2,1)} %get-tuple-element.15), channel_id=1, source_target_pairs={{1,0},{2,1},{3,2},{5,4},{6,5},{7,6},{9,8},{10,9},{11,10},{13,12},{... | collective-permute-start | bytes 3145736 | tf_op jit(solution)/shard_map/ppermute | solution.py:207
  12.2 1.3 %slice_bitcast_fusion.refs_1_ = bf16[512,1024]{1,0:T(8,128)(2,1)S(1)} fusion(bf16[4,512,1024]{2,1,0:T(8,128)(2,1)} %refs_6_.3), kind=kLoop, calls=%fused_computation.4 | loop fusion | bytes 2097152 | tf_op jit(solution)/shard_map/squeeze | solution.py:226
  13.5 0.6 collective-permute-start.7
  14.1 0.0 copy-done.3
  14.1 0.1 slice.34
  14.2 0.6 slice.33
  14.7 0.1 reverse
  14.8 0.1 slice.49
  14.9 13.5 %collective-permute-done.9.refs_3_ = bf16[512,1024]{1,0:T(8,128)(2,1)} collective-permute-done((bf16[512,1024]{1,0:T(8,128)(2,1)S(1)}, bf16[512,1024]{1,0:T(8,128)(2,1)}, u32[]{:S(2)}, u32[]{:S(2)}) %collective-permute-start.9) | collective-permute-done | bytes 1048608 | tf_op jit(solution)/shard_map/ppermute | solution.py:202
  28.5 0.0 collective-permute-start.10
  28.5 0.8 maximum_convert_fusion.row_ref
  29.2 3.6 %time_table.1.refs_0_ = bf16[512,2048]{1,0:T(8,128)(2,1)S(1)} custom-call(s32[1]{0:T(128)} %bitcast.core_ref, f32[1,2048]{1,0:T(1,128)S(1)} %maximum_convert_fusion.row_ref), custom_call_target="tpu_custom_call" | custom-call | tf_op jit(solution)/shard_map/time_table/pallas_call | solution.py:51
  32.8 0.0 copy-done.2
  32.9 0.0 copy-start
  32.9 4.4 %fusion.1.refs_3_ = bf16[1024,2048]{1,0:T(8,128)(2,1)S(1)} fusion(bf16[1024,2048]{1,0:T(8,128)(2,1)} %param.7, s32[1024]{0:T(1024)S(1)} %broadcast_add_fusion, s32[1024]{0:T(1024)S(1)} %copy-done.2), kind=kLoop, calls=%fused_computation.3 | loop fusion | flops 8388608 | bytes 8396800 | tf_op jit(solution)/shard_map/jit(_where)/select_n | solution.py:235
  37.3 0.0 collective-permute-done.refs_0_
  37.3 0.6 collective-permute-start.6
  37.9 0.5 collective-permute-done.1.refs_2_
  38.4 0.0 copy-done
  38.4 6.0 %space.4.refs_1_ = bf16[512,1536]{1,0:T(8,128)(2,1)S(1)} custom-call(bf16[2,512,512]{2,1,0:T(8,128)(2,1)S(1)} %collective-permute-done.refs_0_, bf16[4,512,1024]{2,1,0:T(8,128)(2,1)S(1)} %copy-done, bf16[2,512,512]{2,1,0:T(8,128)(2,1)} %collective-permute-done.1.refs_2_, bf16[1024,2048]{1,0:T(8,128)(2,1)S(1)} %fusion.1.refs_3_), custom_call_target="tpu_custom_call" | custom-call | tf_op jit(solution)/shard_map/space/pallas_call | solution.py:116
  44.4 2.6 %space.5.refs_1_ = bf16[512,512]{1,0:T(8,128)(2,1)S(1)} custom-call(bf16[2,512,512]{2,1,0:T(8,128)(2,1)S(1)} %collective-permute-done.refs_0_, bf16[4,512,1024]{2,1,0:T(8,128)(2,1)S(1)} %copy-done, bf16[2,512,512]{2,1,0:T(8,128)(2,1)} %collective-permute-done.1.refs_2_, bf16[1024,2048]{1,0:T(8,128)(2,1)S(1)} %fusion.1.refs_3_), custom_call_target="tpu_custom_call" | custom-call | tf_op jit(solution)/shard_map/space/pallas_call | solution.py:116
  47.0 0.0 collective-permute-done.8.refs_2_
  47.0 0.0 collective-permute-done.10.refs_4_
  47.0 3.8 %mix.4.refs_1_ = bf16[1,512,1024]{2,1,0:T(8,128)(2,1)S(1)} custom-call(bf16[512,2048]{1,0:T(8,128)(2,1)S(1)} %time_table.1.refs_0_, bf16[512,1024]{1,0:T(8,128)(2,1)S(1)} %slice_bitcast_fusion.1.refs_1_, bf16[512,1024]{1,0:T(8,128)(2,1)} %collective-permute-done.8.refs_2_, bf16[512,1024]{1,0:T(8,128)(2,1)} %collective-permute-done.9.refs_3_, ...), custom_call_target="tpu_custom_call" | custom-call | tf_op jit(solution)/shard_map/mix/pallas_call | solution.py:168
  50.9 0.0 collective-permute-done.7.refs_3_
  50.9 0.1 collective-permute-start.11
  51.0 1.6 %collective-permute-start.5 = (bf16[512,1536]{1,0:T(8,128)(2,1)S(1)}, bf16[512,1536]{1,0:T(8,128)(2,1)S(1)}, u32[]{:S(2)}, u32[]{:S(2)}) collective-permute-start(bf16[512,1536]{1,0:T(8,128)(2,1)S(1)} %space.4.refs_1_), channel_id=1, source_target_pairs={{0,8},{4,12},{8,0},{12,4},{1,9},{5,13},{9,1},{13,5},{2,10},{6,14},... | collective-permute-start | bytes 4718600 | tf_op jit(solution)/shard_map/ppermute | solution.py:202
  52.6 0.1 fusion.3
  52.6 3.5 %collective-permute-start.14 = (bf16[1,512,512]{2,1,0:T(8,128)(2,1)S(1)}, bf16[1,512,512]{2,1,0:T(8,128)(2,1)S(1)}, u32[]{:S(2)}, u32[]{:S(2)}) collective-permute-start(bf16[1,512,512]{2,1,0:T(8,128)(2,1)S(1)} %get-tuple-element.18), channel_id=1, source_target_pairs={{0,1},{1,2},{2,3},{4,5},{5,6},{6,7},{8,9},{9,10},{10,11},{12,13},{... | collective-permute-start | bytes 1572872 | tf_op jit(solution)/shard_map/ppermute | solution.py:206
  56.1 0.0 copy-start.1
  56.2 1.3 %collective-permute-start.15 = (bf16[1,512,512]{2,1,0:T(8,128)(2,1)S(1)}, bf16[1,512,512]{2,1,0:T(8,128)(2,1)S(1)}, u32[]{:S(2)}, u32[]{:S(2)}) collective-permute-start(bf16[1,512,512]{2,1,0:T(8,128)(2,1)S(1)} %get-tuple-element.17), channel_id=1, source_target_pairs={{1,0},{2,1},{3,2},{5,4},{6,5},{7,6},{9,8},{10,9},{11,10},{13,12},{... | collective-permute-start | bytes 1572872 | tf_op jit(solution)/shard_map/ppermute | solution.py:207
  57.5 0.0 collective-permute-done.6.refs_2_
  57.5 0.0 collective-permute-done.11.refs_4_
  57.5 3.7 %mix.5.refs_1_ = bf16[1,512,1024]{2,1,0:T(8,128)(2,1)S(1)} custom-call(bf16[512,2048]{1,0:T(8,128)(2,1)S(1)} %time_table.1.refs_0_, bf16[512,1024]{1,0:T(8,128)(2,1)S(1)} %slice_bitcast_fusion.refs_1_, bf16[512,1024]{1,0:T(8,128)(2,1)S(1)} %collective-permute-done.6.refs_2_, bf16[512,1024]{1,0:T(8,128)(2,1)} %collective-permute-done.7.refs_3_, ...), custom_call_target="tpu_custom_call" | custom-call | tf_op jit(solution)/shard_map/mix/pallas_call | solution.py:168
  61.2 0.1 fusion.4
  61.3 4.6 %collective-permute-start.12 = (bf16[1,512,512]{2,1,0:T(8,128)(2,1)S(1)}, bf16[1,512,512]{2,1,0:T(8,128)(2,1)S(1)}, u32[]{:S(2)}, u32[]{:S(2)}) collective-permute-start(bf16[1,512,512]{2,1,0:T(8,128)(2,1)S(1)} %get-tuple-element.20), channel_id=1, source_target_pairs={{0,1},{1,2},{2,3},{4,5},{5,6},{6,7},{8,9},{9,10},{10,11},{12,13},{... | collective-permute-start | bytes 1572872 | tf_op jit(solution)/shard_map/ppermute | solution.py:206
  65.9 1.3 %collective-permute-start.13 = (bf16[1,512,512]{2,1,0:T(8,128)(2,1)S(1)}, bf16[1,512,512]{2,1,0:T(8,128)(2,1)S(1)}, u32[]{:S(2)}, u32[]{:S(2)}) collective-permute-start(bf16[1,512,512]{2,1,0:T(8,128)(2,1)S(1)} %get-tuple-element.19), channel_id=1, source_target_pairs={{1,0},{2,1},{3,2},{5,4},{6,5},{7,6},{9,8},{10,9},{11,10},{13,12},{... | collective-permute-start | bytes 1572872 | tf_op jit(solution)/shard_map/ppermute | solution.py:207
  67.2 1.2 %collective-permute-done.14.refs_0_ = bf16[1,512,512]{2,1,0:T(8,128)(2,1)S(1)} collective-permute-done((bf16[1,512,512]{2,1,0:T(8,128)(2,1)S(1)}, bf16[1,512,512]{2,1,0:T(8,128)(2,1)S(1)}, u32[]{:S(2)}, u32[]{:S(2)}) %collective-permute-start.14) | collective-permute-done | bytes 524320 | tf_op jit(solution)/shard_map/ppermute | solution.py:206
  68.4 0.0 collective-permute-start.4
  68.4 4.5 %collective-permute-done.15.refs_2_ = bf16[1,512,512]{2,1,0:T(8,128)(2,1)S(1)} collective-permute-done((bf16[1,512,512]{2,1,0:T(8,128)(2,1)S(1)}, bf16[1,512,512]{2,1,0:T(8,128)(2,1)S(1)}, u32[]{:S(2)}, u32[]{:S(2)}) %collective-permute-start.15) | collective-permute-done | bytes 524320 | tf_op jit(solution)/shard_map/ppermute | solution.py:207
  72.9 0.0 copy-done.1
  72.9 4.0 %space.6.refs_6_ = bf16[4,512,1024]{2,1,0:T(8,128)(2,1)} custom-call(bf16[1,512,512]{2,1,0:T(8,128)(2,1)S(1)} %collective-permute-done.14.refs_0_, bf16[1,512,1024]{2,1,0:T(8,128)(2,1)S(1)} %mix.4.refs_1_, bf16[1,512,512]{2,1,0:T(8,128)(2,1)S(1)} %collective-permute-done.15.refs_2_, bf16[1024,2048]{1,0:T(8,128)(2,1)S(1)} %fusion.1.refs_3_, ...), custom_call_target="tpu_custom_call" | custom-call | tf_op jit(solution)/shard_map/space/pallas_call | solution.py:116
  76.9 2.0 %collective-permute-done.12.refs_0_ = bf16[1,512,512]{2,1,0:T(8,128)(2,1)S(1)} collective-permute-done((bf16[1,512,512]{2,1,0:T(8,128)(2,1)S(1)}, bf16[1,512,512]{2,1,0:T(8,128)(2,1)S(1)}, u32[]{:S(2)}, u32[]{:S(2)}) %collective-permute-start.12) | collective-permute-done | bytes 524320 | tf_op jit(solution)/shard_map/ppermute | solution.py:206
  78.8 4.2 %collective-permute-done.13.refs_2_ = bf16[1,512,512]{2,1,0:T(8,128)(2,1)S(1)} collective-permute-done((bf16[1,512,512]{2,1,0:T(8,128)(2,1)S(1)}, bf16[1,512,512]{2,1,0:T(8,128)(2,1)S(1)}, u32[]{:S(2)}, u32[]{:S(2)}) %collective-permute-start.13) | collective-permute-done | bytes 524320 | tf_op jit(solution)/shard_map/ppermute | solution.py:207
  83.0 4.0 %space.7.refs_7_ = bf16[4,512,1024]{2,1,0:T(8,128)(2,1)} custom-call(bf16[1,512,512]{2,1,0:T(8,128)(2,1)S(1)} %collective-permute-done.12.refs_0_, bf16[1,512,1024]{2,1,0:T(8,128)(2,1)S(1)} %mix.5.refs_1_, bf16[1,512,512]{2,1,0:T(8,128)(2,1)S(1)} %collective-permute-done.13.refs_2_, ...), custom_call_target="tpu_custom_call", output_to_operand_aliasing={{}: (6, {})} | custom-call | tf_op jit(solution)/shard_map/space/pallas_call | solution.py:116
  87.0 0.8 collective-permute-done.5.refs_3_
  87.8 0.0 collective-permute-start.16
  87.8 1.5 %collective-permute-start.3 = (bf16[512,512]{1,0:T(8,128)(2,1)S(1)}, bf16[512,512]{1,0:T(8,128)(2,1)S(1)}, u32[]{:S(2)}, u32[]{:S(2)}) collective-permute-start(bf16[512,512]{1,0:T(8,128)(2,1)S(1)} %space.5.refs_1_), channel_id=1, source_target_pairs={{0,8},{4,12},{8,0},{12,4},{1,9},{5,13},{9,1},{13,5},{2,10},{6,14},... | collective-permute-start | bytes 1572872 | tf_op jit(solution)/shard_map/ppermute | solution.py:202
  89.3 0.2 collective-permute-start.2
  89.5 0.0 collective-permute-done.4.refs_2_
  89.5 1.6 %collective-permute-done.16.refs_4_ = bf16[512,1536]{1,0:T(8,128)(2,1)S(1)} collective-permute-done((bf16[512,1536]{1,0:T(8,128)(2,1)S(1)}, bf16[512,1536]{1,0:T(8,128)(2,1)S(1)}, u32[]{:S(2)}, u32[]{:S(2)}) %collective-permute-start.16) | collective-permute-done | bytes 1572896 | tf_op jit(solution)/shard_map/ppermute | solution.py:199
  91.2 5.2 %mix.6.refs_7_ = bf16[4,512,1024]{2,1,0:T(8,128)(2,1)} custom-call(bf16[512,2048]{1,0:T(8,128)(2,1)S(1)} %time_table.1.refs_0_, bf16[512,1536]{1,0:T(8,128)(2,1)S(1)} %space.4.refs_1_, bf16[512,1536]{1,0:T(8,128)(2,1)S(1)} %collective-permute-done.4.refs_2_, bf16[512,1536]{1,0:T(8,128)(2,1)S(1)} %collective-permute-done.5.refs_3_, ...), custom_call_target="tpu_custom_call", output_to_operand_aliasing={{}: (7, {})} | custom-call | tf_op jit(solution)/shard_map/mix/pallas_call | solution.py:168
  96.4 5.7 %collective-permute-done.3.refs_3_ = bf16[512,512]{1,0:T(8,128)(2,1)S(1)} collective-permute-done((bf16[512,512]{1,0:T(8,128)(2,1)S(1)}, bf16[512,512]{1,0:T(8,128)(2,1)S(1)}, u32[]{:S(2)}, u32[]{:S(2)}) %collective-permute-start.3) | collective-permute-done | bytes 524320 | tf_op jit(solution)/shard_map/ppermute | solution.py:202
  102.1 0.0 collective-permute-start.17
  102.1 0.0 collective-permute-done.2.refs_2_
  102.1 1.9 %collective-permute-done.17.refs_4_ = bf16[512,512]{1,0:T(8,128)(2,1)S(1)} collective-permute-done((bf16[512,512]{1,0:T(8,128)(2,1)S(1)}, bf16[512,512]{1,0:T(8,128)(2,1)S(1)}, u32[]{:S(2)}, u32[]{:S(2)}) %collective-permute-start.17) | collective-permute-done | bytes 524320 | tf_op jit(solution)/shard_map/ppermute | solution.py:199
  104.0 2.1 %mix.7 = bf16[4,512,1024]{2,1,0:T(8,128)(2,1)} custom-call(bf16[512,2048]{1,0:T(8,128)(2,1)S(1)} %time_table.1.refs_0_, bf16[512,512]{1,0:T(8,128)(2,1)S(1)} %space.5.refs_1_, bf16[512,512]{1,0:T(8,128)(2,1)S(1)} %collective-permute-done.2.refs_2_, bf16[512,512]{1,0:T(8,128)(2,1)S(1)} %collective-permute-done.3.refs_3_, ...), custom_call_target="tpu_custom_call", output_to_operand_aliasing={{}: (7, {})} | custom-call | tf_op jit(solution)/shard_map/mix/pallas_call | solution.py:168
  (2 shorter events, 0.0 us)
Async XLA Ops:
  0.0 14.1 %copy-start.3 = (bf16[2048]{0:T(1024)(128)(2,1)S(1)}, bf16[2048]{0:T(1024)(128)(2,1)}, u32[]{:S(2)}) copy-start(bf16[2048]{0:T(1024)(128)(2,1)} %param.6) | copy-start | bytes 12292
  1.3 31.5 %copy-start.2 = (s32[1024]{0:T(1024)S(1)}, s32[1024]{0:T(1024)}, u32[]{:S(2)}) copy-start(s32[1024]{0:T(1024)} %param.8) | copy-start | bytes 12292
  1.3 27.1 %collective-permute-start.9 = (bf16[512,1024]{1,0:T(8,128)(2,1)S(1)}, bf16[512,1024]{1,0:T(8,128)(2,1)}, u32[]{:S(2)}, u32[]{:S(2)}) collective-permute-start(bf16[512,1024]{1,0:T(8,128)(2,1)S(1)} %slice_bitcast_fusion.1.refs_1_), channel_id=1, source_target_pairs={{0,8},{4,12},{8,0},{12,4},{1,9},{5,13},{9,1},{13,5},{2,10},{6,14},... | collective-permute-start | bytes 3145736 | tf_op jit(solution)/shard_map/ppermute | solution.py:202
  4.4 42.6 %collective-permute-start.8 = (bf16[512,1024]{1,0:T(8,128)(2,1)S(1)}, bf16[512,1024]{1,0:T(8,128)(2,1)}, u32[]{:S(2)}, u32[]{:S(2)}) collective-permute-start(bf16[512,1024]{1,0:T(8,128)(2,1)S(1)} %slice_bitcast_fusion.1.refs_1_), channel_id=1, source_target_pairs={{0,4},{4,0},{8,12},{12,8},{1,5},{5,1},{9,13},{13,9},{2,6},{6,2},{1... | collective-permute-start | bytes 3145736 | tf_op jit(solution)/shard_map/ppermute | solution.py:199
  7.4 29.9 %collective-permute-start = (bf16[2,512,512]{2,1,0:T(8,128)(2,1)}, bf16[2,512,512]{2,1,0:T(8,128)(2,1)S(1)}, u32[]{:S(2)}, u32[]{:S(2)}) collective-permute-start(bf16[2,512,512]{2,1,0:T(8,128)(2,1)} %get-tuple-element.16), channel_id=1, source_target_pairs={{0,1},{1,2},{2,3},{4,5},{5,6},{6,7},{8,9},{9,10},{10,11},{12,13},{... | collective-permute-start | bytes 3145736 | tf_op jit(solution)/shard_map/ppermute | solution.py:206
  10.9 27.5 %collective-permute-start.1 = (bf16[2,512,512]{2,1,0:T(8,128)(2,1)}, bf16[2,512,512]{2,1,0:T(8,128)(2,1)}, u32[]{:S(2)}, u32[]{:S(2)}) collective-permute-start(bf16[2,512,512]{2,1,0:T(8,128)(2,1)} %get-tuple-element.15), channel_id=1, source_target_pairs={{1,0},{2,1},{3,2},{5,4},{6,5},{7,6},{9,8},{10,9},{11,10},{13,12},{... | collective-permute-start | bytes 3145736 | tf_op jit(solution)/shard_map/ppermute | solution.py:207
  13.5 37.4 %collective-permute-start.7 = (bf16[512,1024]{1,0:T(8,128)(2,1)S(1)}, bf16[512,1024]{1,0:T(8,128)(2,1)}, u32[]{:S(2)}, u32[]{:S(2)}) collective-permute-start(bf16[512,1024]{1,0:T(8,128)(2,1)S(1)} %slice_bitcast_fusion.refs_1_), channel_id=1, source_target_pairs={{0,8},{4,12},{8,0},{12,4},{1,9},{5,13},{9,1},{13,5},{2,10},{6,14},... | collective-permute-start | bytes 3145736 | tf_op jit(solution)/shard_map/ppermute | solution.py:202
  28.5 18.6 %collective-permute-start.10 = (bf16[512,1024]{1,0:T(8,128)(2,1)}, bf16[512,1024]{1,0:T(8,128)(2,1)S(1)}, u32[]{:S(2)}, u32[]{:S(2)}) collective-permute-start(bf16[512,1024]{1,0:T(8,128)(2,1)} %collective-permute-done.9.refs_3_), channel_id=1, source_target_pairs={{0,4},{4,0},{8,12},{12,8},{1,5},{5,1},{9,13},{13,9},{2,6},{6,2},{1... | collective-permute-start | bytes 3145736 | tf_op jit(solution)/shard_map/ppermute | solution.py:199
  32.9 5.5 %copy-start = (bf16[4,512,1024]{2,1,0:T(8,128)(2,1)S(1)}, bf16[4,512,1024]{2,1,0:T(8,128)(2,1)}, u32[]{:S(2)}) copy-start(bf16[4,512,1024]{2,1,0:T(8,128)(2,1)} %refs_6_.3) | copy-start | bytes 12582916
  37.3 20.2 %collective-permute-start.6 = (bf16[512,1024]{1,0:T(8,128)(2,1)S(1)}, bf16[512,1024]{1,0:T(8,128)(2,1)S(1)}, u32[]{:S(2)}, u32[]{:S(2)}) collective-permute-start(bf16[512,1024]{1,0:T(8,128)(2,1)S(1)} %slice_bitcast_fusion.refs_1_), channel_id=1, source_target_pairs={{0,4},{4,0},{8,12},{12,8},{1,5},{5,1},{9,13},{13,9},{2,6},{6,2},{1... | collective-permute-start | bytes 3145736 | tf_op jit(solution)/shard_map/ppermute | solution.py:199
  50.9 6.6 %collective-permute-start.11 = (bf16[512,1024]{1,0:T(8,128)(2,1)}, bf16[512,1024]{1,0:T(8,128)(2,1)S(1)}, u32[]{:S(2)}, u32[]{:S(2)}) collective-permute-start(bf16[512,1024]{1,0:T(8,128)(2,1)} %collective-permute-done.7.refs_3_), channel_id=1, source_target_pairs={{0,4},{4,0},{8,12},{12,8},{1,5},{5,1},{9,13},{13,9},{2,6},{6,2},{1... | collective-permute-start | bytes 3145736 | tf_op jit(solution)/shard_map/ppermute | solution.py:199
  51.0 36.8 %collective-permute-start.5 = (bf16[512,1536]{1,0:T(8,128)(2,1)S(1)}, bf16[512,1536]{1,0:T(8,128)(2,1)S(1)}, u32[]{:S(2)}, u32[]{:S(2)}) collective-permute-start(bf16[512,1536]{1,0:T(8,128)(2,1)S(1)} %space.4.refs_1_), channel_id=1, source_target_pairs={{0,8},{4,12},{8,0},{12,4},{1,9},{5,13},{9,1},{13,5},{2,10},{6,14},... | collective-permute-start | bytes 4718600 | tf_op jit(solution)/shard_map/ppermute | solution.py:202
  52.6 15.8 %collective-permute-start.14 = (bf16[1,512,512]{2,1,0:T(8,128)(2,1)S(1)}, bf16[1,512,512]{2,1,0:T(8,128)(2,1)S(1)}, u32[]{:S(2)}, u32[]{:S(2)}) collective-permute-start(bf16[1,512,512]{2,1,0:T(8,128)(2,1)S(1)} %get-tuple-element.18), channel_id=1, source_target_pairs={{0,1},{1,2},{2,3},{4,5},{5,6},{6,7},{8,9},{9,10},{10,11},{12,13},{... | collective-permute-start | bytes 1572872 | tf_op jit(solution)/shard_map/ppermute | solution.py:206
  56.1 16.7 %copy-start.1 = (f32[1024]{0:T(1024)S(1)}, f32[1024]{0:T(1024)}, u32[]{:S(2)}) copy-start(f32[1024]{0:T(1024)} %param.9) | copy-start | bytes 12292
  56.2 16.7 %collective-permute-start.15 = (bf16[1,512,512]{2,1,0:T(8,128)(2,1)S(1)}, bf16[1,512,512]{2,1,0:T(8,128)(2,1)S(1)}, u32[]{:S(2)}, u32[]{:S(2)}) collective-permute-start(bf16[1,512,512]{2,1,0:T(8,128)(2,1)S(1)} %get-tuple-element.17), channel_id=1, source_target_pairs={{1,0},{2,1},{3,2},{5,4},{6,5},{7,6},{9,8},{10,9},{11,10},{13,12},{... | collective-permute-start | bytes 1572872 | tf_op jit(solution)/shard_map/ppermute | solution.py:207
  61.3 17.6 %collective-permute-start.12 = (bf16[1,512,512]{2,1,0:T(8,128)(2,1)S(1)}, bf16[1,512,512]{2,1,0:T(8,128)(2,1)S(1)}, u32[]{:S(2)}, u32[]{:S(2)}) collective-permute-start(bf16[1,512,512]{2,1,0:T(8,128)(2,1)S(1)} %get-tuple-element.20), channel_id=1, source_target_pairs={{0,1},{1,2},{2,3},{4,5},{5,6},{6,7},{8,9},{9,10},{10,11},{12,13},{... | collective-permute-start | bytes 1572872 | tf_op jit(solution)/shard_map/ppermute | solution.py:206
  65.9 17.1 %collective-permute-start.13 = (bf16[1,512,512]{2,1,0:T(8,128)(2,1)S(1)}, bf16[1,512,512]{2,1,0:T(8,128)(2,1)S(1)}, u32[]{:S(2)}, u32[]{:S(2)}) collective-permute-start(bf16[1,512,512]{2,1,0:T(8,128)(2,1)S(1)} %get-tuple-element.19), channel_id=1, source_target_pairs={{1,0},{2,1},{3,2},{5,4},{6,5},{7,6},{9,8},{10,9},{11,10},{13,12},{... | collective-permute-start | bytes 1572872 | tf_op jit(solution)/shard_map/ppermute | solution.py:207
  68.4 21.1 %collective-permute-start.4 = (bf16[512,1536]{1,0:T(8,128)(2,1)S(1)}, bf16[512,1536]{1,0:T(8,128)(2,1)S(1)}, u32[]{:S(2)}, u32[]{:S(2)}) collective-permute-start(bf16[512,1536]{1,0:T(8,128)(2,1)S(1)} %space.4.refs_1_), channel_id=1, source_target_pairs={{0,4},{4,0},{8,12},{12,8},{1,5},{5,1},{9,13},{13,9},{2,6},{6,2},{1... | collective-permute-start | bytes 4718600 | tf_op jit(solution)/shard_map/ppermute | solution.py:199
  87.8 3.4 %collective-permute-start.16 = (bf16[512,1536]{1,0:T(8,128)(2,1)S(1)}, bf16[512,1536]{1,0:T(8,128)(2,1)S(1)}, u32[]{:S(2)}, u32[]{:S(2)}) collective-permute-start(bf16[512,1536]{1,0:T(8,128)(2,1)S(1)} %collective-permute-done.5.refs_3_), channel_id=1, source_target_pairs={{0,4},{4,0},{8,12},{12,8},{1,5},{5,1},{9,13},{13,9},{2,6},{6,2},{1... | collective-permute-start | bytes 4718600 | tf_op jit(solution)/shard_map/ppermute | solution.py:199
  87.8 14.3 %collective-permute-start.3 = (bf16[512,512]{1,0:T(8,128)(2,1)S(1)}, bf16[512,512]{1,0:T(8,128)(2,1)S(1)}, u32[]{:S(2)}, u32[]{:S(2)}) collective-permute-start(bf16[512,512]{1,0:T(8,128)(2,1)S(1)} %space.5.refs_1_), channel_id=1, source_target_pairs={{0,8},{4,12},{8,0},{12,4},{1,9},{5,13},{9,1},{13,5},{2,10},{6,14},... | collective-permute-start | bytes 1572872 | tf_op jit(solution)/shard_map/ppermute | solution.py:202
  89.3 12.8 %collective-permute-start.2 = (bf16[512,512]{1,0:T(8,128)(2,1)S(1)}, bf16[512,512]{1,0:T(8,128)(2,1)S(1)}, u32[]{:S(2)}, u32[]{:S(2)}) collective-permute-start(bf16[512,512]{1,0:T(8,128)(2,1)S(1)} %space.5.refs_1_), channel_id=1, source_target_pairs={{0,4},{4,0},{8,12},{12,8},{1,5},{5,1},{9,13},{13,9},{2,6},{6,2},{1... | collective-permute-start | bytes 1572872 | tf_op jit(solution)/shard_map/ppermute | solution.py:199
  102.1 1.9 %collective-permute-start.17 = (bf16[512,512]{1,0:T(8,128)(2,1)S(1)}, bf16[512,512]{1,0:T(8,128)(2,1)S(1)}, u32[]{:S(2)}, u32[]{:S(2)}) collective-permute-start(bf16[512,512]{1,0:T(8,128)(2,1)S(1)} %collective-permute-done.3.refs_3_), channel_id=1, source_target_pairs={{0,4},{4,0},{8,12},{12,8},{1,5},{5,1},{9,13},{13,9},{2,6},{6,2},{1... | collective-permute-start | bytes 1572872 | tf_op jit(solution)/shard_map/ppermute | solution.py:199

commit v2 on v1

--- a/solution.py
+++ b/solution.py
@@ -126,26 +126,30 @@
     )(*args)
 
 
-def mix_kernel(count, noisy, *refs):
+def mix_kernel(pieces, noisy, *refs):
     table = refs[0]
-    blocks = refs[1 : 1 + count]
     out = refs[-1]
-    rows = blocks[0].shape[0]
-    total = dot(table[:, :rows], blocks[0][...])
-    for m in range(1, count):
-        total += dot(table[:, m * rows : (m + 1) * rows], blocks[m][...])
+    taken = 1
+    total = None
+    for m, count in enumerate(pieces):
+        block = jnp.concatenate([ref[...] for ref in refs[taken : taken + count]], axis=0)
+        taken += count
+        rows = block.shape[0]
+        term = dot(table[:, m * rows : (m + 1) * rows], block)
+        total = term if total is None else total + term
     if noisy:
-        noise, own = refs[1 + count : 3 + count]
+        noise, own = refs[taken : taken + 2]
         total += noise[...] * own[0].astype(F32)
     out[0] = total.astype(BF16)
 
 
 def mix(table, blocks, image=None):
-    rows, width = blocks[0].shape
+    rows, width = blocks[0][0].shape
     step = min(512, width)
-    args = [table] + list(blocks)
+    flat = [piece for block in blocks for piece in block]
+    args = [table] + flat
     specs = [pl.BlockSpec(table.shape, lambda j: (0, 0))]
-    specs += [pl.BlockSpec((rows, step), lambda j: (0, j))] * len(blocks)
+    specs += [pl.BlockSpec((piece.shape[0], step), lambda j: (0, j)) for piece in flat]
     aliases = {}
     if image is not None:
         noise, field, base, start, old = image
@@ -166,7 +170,7 @@
         out_shape = jax.ShapeDtypeStruct((1, rows, width), BF16)
         out_spec = pl.BlockSpec((1, rows, step), lambda j: (0, 0, j))
     return pl.pallas_call(
-        functools.partial(mix_kernel, len(blocks), image is not None),
+        functools.partial(mix_kernel, [len(block) for block in blocks], image is not None),
         grid=(width // step,),
         out_shape=out_shape,
         in_specs=specs,
@@ -212,11 +216,11 @@
         order[0].extend([(-s) % count, (1 - s) % count])
         order[1].extend([(-s) % count, (-1 - s) % count])
 
-    def gathered(own, far, *others):
-        blocks = [own, to_core(own)]
+    def gathered(own, far, pieces, *others):
+        blocks = [[own], [to_core(own)]]
         for got in far:
             got = after(got, *others)
-            blocks += [got, to_core(got)]
+            blocks += [[got], [to_core(part) for part in jnp.split(got, pieces, axis=0)]]
         return blocks
 
     firsts = probes // 2
@@ -234,24 +238,22 @@
     mask = (col[None, :] >= offsets[:, None]) & (col[None, :] < offsets[:, None] + width)
     band = jnp.where(mask, sp_weight, jnp.zeros_like(sp_weight))
 
-    mixed = [mix(table, gathered(own[0], far[0]))]
     columns = (probes - firsts) * width
-    chunks = [(0, columns - half), (columns - half, half)]
-    sent = []
-    weights = band
-    for start, size in chunks:
-        block = space(low, field, high, weights, firsts, start, size)
-        sent.append((block, to_chips(block)))
-        weights = after(band, block)
+    mixed = [mix(table, gathered(own[0], far[0], 2, table, band))]
+    long = space(low, field, high, after(band, mixed[0]), firsts, 0, columns - half)
+    sent = [(0, long, to_chips(long), 4)]
     for p in range(1, firsts):
-        mixed.append(mix(table, gathered(own[p], far[p], mixed[-1], block)))
+        mixed.append(mix(table, gathered(own[p], far[p], 2, mixed[-1], long)))
 
     image = None
     for p in range(firsts):
         got_low, got_high = halo(mixed[p])
         image = space(got_low, mixed[p], got_high, band, 0, 0, width, image=(noise, field, p, image))
-    for (start, _), (block, got) in zip(chunks, sent):
-        image = mix(table, gathered(block, got, image), image=(noise, field, firsts, start, image))
+        if p == 0:
+            short = space(low, field, high, after(band, image), firsts, columns - half, half)
+            sent.append((columns - half, short, to_chips(short), 1))
+    for start, block, got, pieces in sent:
+        image = mix(table, gathered(block, got, pieces, image), image=(noise, field, firsts, start, image))
     return image
 
 

time: 107 us -> 100 us (0.935)
  waiting for transfers between devices: 35.9 us -> 24.7 us
  starting transfers between devices: 23.1 us -> 27.2 us
  local copies, waits for them, and re-layouts: 6.6 us -> 8.27 us
    ppermute x4, waiting for transfers between devices: 20 us -> 8.7 us  [to_chips(): lax.ppermute(block, 'slot', [(i, (i + s) % count) for i in range(count)])]
    ppermute x3, waiting for transfers between devices: 9.16 us -> 6.62 us  [halo(): lax.ppermute(block[:, :, :half], 'site', down)]
    ppermute x8 -> x13, waiting for transfers between devices: 3.56 us -> 6.04 us  [to_core(): return lax.ppermute(block, 'slot', swap)]
    ppermute x3, starting transfers between devices: 11.6 us -> 14.1 us  [halo(): lax.ppermute(block[:, :, width - half:], 'site', up)]
    ppermute x8 -> x13, starting transfers between devices: 0.88 us -> 2.7 us  [to_core(): return lax.ppermute(block, 'slot', swap)]
    split x0 -> x3, local copies, waits for them, and re-layouts: none -> 1.59 us  [gathered(): jnp.split(got, pieces, axis=0)]
  transfers between devices with their start and end apart: 18 -> 23, of which waited for: 10 -> 13; matrix products, arithmetic and copies ran while one was open for 10% -> 11% of each run, Pallas kernels for 31% -> 33%
where the time goes in v2:
time: 100 us; the launch traced here: 99.7 us
  Pallas kernels  34.7 us (35%)
  starting transfers between devices  27.2 us (27%)
  waiting for transfers between devices  24.7 us (25%)
  local copies, waits for them, and re-layouts  8.27 us (8%)
  other arithmetic  4.65 us (5%)
    pallas_call x4, Pallas kernels, space(): pl.pallas_call(functools.partial(space_kernel, half, image is not None),...  17.1 us
    ppermute x3, starting transfers between devices, halo(): lax.ppermute(block[:, :, width - half:], 'site', up)  14.1 us
    pallas_call x4, Pallas kernels, mix(): pl.pallas_call(functools.partial(mix_kernel, [len(block) for block in blo...  14 us
    ppermute x4, waiting for transfers between devices, to_chips(): lax.ppermute(block, 'slot', [(i, (i + s) % count) for i in range(count)])  8.7 us
    ppermute x3, waiting for transfers between devices, halo(): lax.ppermute(block[:, :, :half], 'site', down)  6.62 us
    ppermute x4, starting transfers between devices, to_chips(): lax.ppermute(block, 'slot', [(i, (i + s) % count) for i in range(count)])  6.52 us
    ppermute x13, waiting for transfers between devices, to_core(): return lax.ppermute(block, 'slot', swap)  6.04 us
    select_n x1, other arithmetic, on_device(): band = jnp.where(mask, sp_weight, jnp.zeros_like(sp_weight))  4.01 us
  transfers between devices with their start and end apart: 23, of which 13 were waited for; matrix products, arithmetic and copies ran while one was open for 11% of the time, Pallas kernels for 33%

profile of v2, /device:TPU:0, one launch (start us, length us, event | category | flops | bytes accessed | tf_op | source)
XLA Modules:
  0.0 99.7 jit_solution(8447314649341912386)
XLA Ops:
  0.0 1.4 %slice_bitcast_fusion.1.refs_1_ = bf16[512,1024]{1,0:T(8,128)(2,1)S(1)} fusion(bf16[4,512,1024]{2,1,0:T(8,128)(2,1)} %refs_6_.1), kind=kLoop, calls=%fused_computation.5 | loop fusion | bytes 2097152 | tf_op jit(solution)/shard_map/squeeze | solution.py:230
  1.5 3.0 %collective-permute-start.3 = (bf16[512,1024]{1,0:T(8,128)(2,1)S(1)}, bf16[512,1024]{1,0:T(8,128)(2,1)}, u32[]{:S(2)}, u32[]{:S(2)}) collective-permute-start(bf16[512,1024]{1,0:T(8,128)(2,1)S(1)} %slice_bitcast_fusion.1.refs_1_), channel_id=1, source_target_pairs={{0,8},{4,12},{8,0},{12,4},{1,9},{5,13},{9,1},{13,5},{2,10},{6,14},... | collective-permute-start | bytes 3145736 | tf_op jit(solution)/shard_map/ppermute | solution.py:206
  4.5 0.0 collective-permute-start.2
  4.5 1.3 %slice_bitcast_fusion.refs_1_ = bf16[512,1024]{1,0:T(8,128)(2,1)S(1)} fusion(bf16[4,512,1024]{2,1,0:T(8,128)(2,1)} %refs_6_.1), kind=kLoop, calls=%fused_computation.4 | loop fusion | bytes 2097152 | tf_op jit(solution)/shard_map/squeeze | solution.py:230
  5.8 0.2 collective-permute-start.13
  5.9 3.0 %fusion.2 = (bf16[2,512,512]{2,1,0:T(8,128)(2,1)}, bf16[2,512,512]{2,1,0:T(8,128)(2,1)}) fusion(bf16[4,512,1024]{2,1,0:T(8,128)(2,1)} %refs_6_.1), kind=kLoop, calls=%fused_computation.8 | loop fusion | bytes 4194304 | tf_op jit(solution)/shard_map/slice | solution.py:211
  9.0 1.3 %collective-permute-start.1 = (bf16[2,512,512]{2,1,0:T(8,128)(2,1)}, bf16[2,512,512]{2,1,0:T(8,128)(2,1)}, u32[]{:S(2)}, u32[]{:S(2)}) collective-permute-start(bf16[2,512,512]{2,1,0:T(8,128)(2,1)} %get-tuple-element.19), channel_id=1, source_target_pairs={{1,0},{2,1},{3,2},{5,4},{6,5},{7,6},{9,8},{10,9},{11,10},{13,12},{... | collective-permute-start | bytes 3145736 | tf_op jit(solution)/shard_map/ppermute | solution.py:211
  10.3 5.6 %collective-permute-start = (bf16[2,512,512]{2,1,0:T(8,128)(2,1)}, bf16[2,512,512]{2,1,0:T(8,128)(2,1)}, u32[]{:S(2)}, u32[]{:S(2)}) collective-permute-start(bf16[2,512,512]{2,1,0:T(8,128)(2,1)} %get-tuple-element.20), channel_id=1, source_target_pairs={{0,1},{1,2},{2,3},{4,5},{5,6},{6,7},{8,9},{9,10},{10,11},{12,13},{... | collective-permute-start | bytes 3145736 | tf_op jit(solution)/shard_map/ppermute | solution.py:210
  15.8 4.0 %fusion.1.refs_3_ = bf16[1024,2048]{1,0:T(8,128)(2,1)} fusion(bf16[1024,2048]{1,0:T(8,128)(2,1)S(1)} %copy-done.3, s32[1024]{0:T(1024)S(1)} %broadcast_add_fusion, s32[1024]{0:T(1024)S(1)} %copy-done.4), kind=kLoop, calls=%fused_computation.3 | loop fusion | flops 8388608 | bytes 8396800 | tf_op jit(solution)/shard_map/jit(_where)/select_n | solution.py:239
  19.9 0.5 slice.33
  20.4 0.1 slice.34
  20.4 0.1 reverse
  20.5 0.1 slice.49
  20.6 0.6 maximum_convert_fusion.row_ref
  21.2 3.6 %time_table.1.refs_0_ = bf16[512,2048]{1,0:T(8,128)(2,1)S(1)} custom-call(s32[1]{0:T(128)} %bitcast.core_ref, f32[1,2048]{1,0:T(1,128)S(1)} %maximum_convert_fusion.row_ref), custom_call_target="tpu_custom_call" | custom-call | tf_op jit(solution)/shard_map/time_table/pallas_call | solution.py:51
  24.9 3.7 %collective-permute-done.3.refs_3_ = bf16[512,1024]{1,0:T(8,128)(2,1)} collective-permute-done((bf16[512,1024]{1,0:T(8,128)(2,1)S(1)}, bf16[512,1024]{1,0:T(8,128)(2,1)}, u32[]{:S(2)}, u32[]{:S(2)}) %collective-permute-start.3) | collective-permute-done | bytes 1048608 | tf_op jit(solution)/shard_map/ppermute | solution.py:206
  28.6 1.4 %fusion.7 = (bf16[256,1024]{1,0:T(8,128)(2,1)S(1)}, bf16[256,1024]{1,0:T(8,128)(2,1)S(1)}) fusion(bf16[512,1024]{1,0:T(8,128)(2,1)} %collective-permute-done.3.refs_3_), kind=kLoop, calls=%fused_computation.13 | loop fusion | bytes 2097152 | tf_op jit(solution)/shard_map/split | solution.py:223
  30.0 0.0 copy-start
  30.0 0.1 collective-permute-start.5
  30.1 0.0 collective-permute-done.2.refs_2_
  30.1 0.5 collective-permute-start.4
  30.6 1.4 %collective-permute-done.5.refs_5_ = bf16[256,1024]{1,0:T(8,128)(2,1)S(1)} collective-permute-done((bf16[256,1024]{1,0:T(8,128)(2,1)S(1)}, bf16[256,1024]{1,0:T(8,128)(2,1)S(1)}, u32[]{:S(2)}, u32[]{:S(2)}) %collective-permute-start.5) | collective-permute-done | bytes 524320 | tf_op jit(solution)/shard_map/ppermute | solution.py:203
  32.0 0.1 collective-permute-start.12
  32.1 0.6 collective-permute-done.4.refs_4_
  32.7 3.8 %mix.4.refs_1_ = bf16[1,512,1024]{2,1,0:T(8,128)(2,1)S(1)} custom-call(bf16[512,2048]{1,0:T(8,128)(2,1)S(1)} %time_table.1.refs_0_, bf16[512,1024]{1,0:T(8,128)(2,1)S(1)} %slice_bitcast_fusion.1.refs_1_, bf16[512,1024]{1,0:T(8,128)(2,1)} %collective-permute-done.2.refs_2_, bf16[512,1024]{1,0:T(8,128)(2,1)} %collective-permute-done.3.refs_3_, ...), custom_call_target="tpu_custom_call" | custom-call | tf_op jit(solution)/shard_map/mix/pallas_call | solution.py:172
  36.6 0.1 collective-permute-done.1.refs_2_
  36.7 1.2 %collective-permute-done.refs_0_ = bf16[2,512,512]{2,1,0:T(8,128)(2,1)} collective-permute-done((bf16[2,512,512]{2,1,0:T(8,128)(2,1)}, bf16[2,512,512]{2,1,0:T(8,128)(2,1)}, u32[]{:S(2)}, u32[]{:S(2)}) %collective-permute-start) | collective-permute-done | bytes 1048608 | tf_op jit(solution)/shard_map/ppermute | solution.py:210
  37.9 6.3 %space.6.refs_1_ = bf16[512,1536]{1,0:T(8,128)(2,1)S(1)} custom-call(bf16[2,512,512]{2,1,0:T(8,128)(2,1)} %collective-permute-done.refs_0_, bf16[4,512,1024]{2,1,0:T(8,128)(2,1)S(1)} %copy-done, bf16[2,512,512]{2,1,0:T(8,128)(2,1)} %collective-permute-done.1.refs_2_, bf16[1024,2048]{1,0:T(8,128)(2,1)S(1)} %copy-done.1), custom_call_target="tpu_custom_call" | custom-call | tf_op jit(solution)/shard_map/space/pallas_call | solution.py:116
  44.2 1.7 %collective-permute-start.11 = (bf16[512,1536]{1,0:T(8,128)(2,1)S(1)}, bf16[512,1536]{1,0:T(8,128)(2,1)S(1)}, u32[]{:S(2)}, u32[]{:S(2)}) collective-permute-start(bf16[512,1536]{1,0:T(8,128)(2,1)S(1)} %space.6.refs_1_), channel_id=1, source_target_pairs={{0,8},{4,12},{8,0},{12,4},{1,9},{5,13},{9,1},{13,5},{2,10},{6,14},... | collective-permute-start | bytes 4718600 | tf_op jit(solution)/shard_map/ppermute | solution.py:206
  46.0 5.0 %collective-permute-done.13.refs_3_ = bf16[512,1024]{1,0:T(8,128)(2,1)S(1)} collective-permute-done((bf16[512,1024]{1,0:T(8,128)(2,1)S(1)}, bf16[512,1024]{1,0:T(8,128)(2,1)S(1)}, u32[]{:S(2)}, u32[]{:S(2)}) %collective-permute-start.13) | collective-permute-done | bytes 1048608 | tf_op jit(solution)/shard_map/ppermute | solution.py:206
  50.9 0.1 fusion.5
  51.0 0.1 collective-permute-start.15
  51.1 0.5 collective-permute-start.14
  51.6 0.1 collective-permute-start.10
  51.7 0.1 fusion.6
  51.7 0.0 collective-permute-done.12.refs_2_
  51.8 1.3 %collective-permute-start.7 = (bf16[1,512,512]{2,1,0:T(8,128)(2,1)S(1)}, bf16[1,512,512]{2,1,0:T(8,128)(2,1)S(1)}, u32[]{:S(2)}, u32[]{:S(2)}) collective-permute-start(bf16[1,512,512]{2,1,0:T(8,128)(2,1)S(1)} %get-tuple-element.29), channel_id=1, source_target_pairs={{1,0},{2,1},{3,2},{5,4},{6,5},{7,6},{9,8},{10,9},{11,10},{13,12},{... | collective-permute-start | bytes 1572872 | tf_op jit(solution)/shard_map/ppermute | solution.py:211
  53.1 0.0 collective-permute-done.15.refs_5_
  53.1 0.0 copy-start.2
  53.1 4.7 %collective-permute-start.6 = (bf16[1,512,512]{2,1,0:T(8,128)(2,1)S(1)}, bf16[1,512,512]{2,1,0:T(8,128)(2,1)S(1)}, u32[]{:S(2)}, u32[]{:S(2)}) collective-permute-start(bf16[1,512,512]{2,1,0:T(8,128)(2,1)S(1)} %get-tuple-element.30), channel_id=1, source_target_pairs={{0,1},{1,2},{2,3},{4,5},{5,6},{6,7},{8,9},{9,10},{10,11},{12,13},{... | collective-permute-start | bytes 1572872 | tf_op jit(solution)/shard_map/ppermute | solution.py:210
  57.8 2.9 %mix.5.refs_1_ = bf16[1,512,1024]{2,1,0:T(8,128)(2,1)S(1)} custom-call(bf16[512,2048]{1,0:T(8,128)(2,1)S(1)} %time_table.1.refs_0_, bf16[512,1024]{1,0:T(8,128)(2,1)S(1)} %slice_bitcast_fusion.refs_1_, bf16[512,1024]{1,0:T(8,128)(2,1)S(1)} %collective-permute-done.12.refs_2_, bf16[512,1024]{1,0:T(8,128)(2,1)S(1)} %collective-permute-done.13.refs_3_, ...), custom_call_target="tpu_custom_call" | custom-call | tf_op jit(solution)/shard_map/mix/pallas_call | solution.py:172
  60.7 0.1 fusion.4
  60.8 1.3 %collective-permute-start.17 = (bf16[1,512,512]{2,1,0:T(8,128)(2,1)S(1)}, bf16[1,512,512]{2,1,0:T(8,128)(2,1)S(1)}, u32[]{:S(2)}, u32[]{:S(2)}) collective-permute-start(bf16[1,512,512]{2,1,0:T(8,128)(2,1)S(1)} %get-tuple-element.25), channel_id=1, source_target_pairs={{1,0},{2,1},{3,2},{5,4},{6,5},{7,6},{9,8},{10,9},{11,10},{13,12},{... | collective-permute-start | bytes 1572872 | tf_op jit(solution)/shard_map/ppermute | solution.py:211
  62.1 6.5 %collective-permute-done.7.refs_2_ = bf16[1,512,512]{2,1,0:T(8,128)(2,1)S(1)} collective-permute-done((bf16[1,512,512]{2,1,0:T(8,128)(2,1)S(1)}, bf16[1,512,512]{2,1,0:T(8,128)(2,1)S(1)}, u32[]{:S(2)}, u32[]{:S(2)}) %collective-permute-start.7) | collective-permute-done | bytes 524320 | tf_op jit(solution)/shard_map/ppermute | solution.py:211
  68.5 3.9 %collective-permute-start.16 = (bf16[1,512,512]{2,1,0:T(8,128)(2,1)S(1)}, bf16[1,512,512]{2,1,0:T(8,128)(2,1)S(1)}, u32[]{:S(2)}, u32[]{:S(2)}) collective-permute-start(bf16[1,512,512]{2,1,0:T(8,128)(2,1)S(1)} %get-tuple-element.26), channel_id=1, source_target_pairs={{0,1},{1,2},{2,3},{4,5},{5,6},{6,7},{8,9},{9,10},{10,11},{12,13},{... | collective-permute-start | bytes 1572872 | tf_op jit(solution)/shard_map/ppermute | solution.py:210
  72.4 4.0 %space.4.refs_6_ = bf16[4,512,1024]{2,1,0:T(8,128)(2,1)} custom-call(bf16[1,512,512]{2,1,0:T(8,128)(2,1)S(1)} %collective-permute-done.6.refs_0_, bf16[1,512,1024]{2,1,0:T(8,128)(2,1)S(1)} %mix.4.refs_1_, bf16[1,512,512]{2,1,0:T(8,128)(2,1)S(1)} %collective-permute-done.7.refs_2_, bf16[1024,2048]{1,0:T(8,128)(2,1)S(1)} %copy-done.1, f32[1,1024]{1,0:T(1,128)S(1)} %bitcast.8, ...), custom_call_target="tpu_custom_call" | custom-call | tf_op jit(solution)/shard_map/space/pallas_call | solution.py:116
  76.5 2.8 %space.5.refs_1_ = bf16[512,512]{1,0:T(8,128)(2,1)S(1)} custom-call(bf16[2,512,512]{2,1,0:T(8,128)(2,1)} %collective-permute-done.refs_0_, bf16[4,512,1024]{2,1,0:T(8,128)(2,1)S(1)} %copy-done, bf16[2,512,512]{2,1,0:T(8,128)(2,1)} %collective-permute-done.1.refs_2_, bf16[1024,2048]{1,0:T(8,128)(2,1)S(1)} %copy-done.1), custom_call_target="tpu_custom_call" | custom-call | tf_op jit(solution)/shard_map/space/pallas_call | solution.py:116
  79.2 1.6 %collective-permute-start.9 = (bf16[512,512]{1,0:T(8,128)(2,1)S(1)}, bf16[512,512]{1,0:T(8,128)(2,1)S(1)}, u32[]{:S(2)}, u32[]{:S(2)}) collective-permute-start(bf16[512,512]{1,0:T(8,128)(2,1)S(1)} %space.5.refs_1_), channel_id=1, source_target_pairs={{0,8},{4,12},{8,0},{12,4},{1,9},{5,13},{9,1},{13,5},{2,10},{6,14},... | collective-permute-start | bytes 1572872 | tf_op jit(solution)/shard_map/ppermute | solution.py:206
  80.8 2.1 %collective-permute-done.16.refs_0_ = bf16[1,512,512]{2,1,0:T(8,128)(2,1)S(1)} collective-permute-done((bf16[1,512,512]{2,1,0:T(8,128)(2,1)S(1)}, bf16[1,512,512]{2,1,0:T(8,128)(2,1)S(1)}, u32[]{:S(2)}, u32[]{:S(2)}) %collective-permute-start.16) | collective-permute-done | bytes 524320 | tf_op jit(solution)/shard_map/ppermute | solution.py:210
  82.9 4.0 %space.7.refs_10_ = bf16[4,512,1024]{2,1,0:T(8,128)(2,1)} custom-call(bf16[1,512,512]{2,1,0:T(8,128)(2,1)S(1)} %collective-permute-done.16.refs_0_, bf16[1,512,1024]{2,1,0:T(8,128)(2,1)S(1)} %mix.5.refs_1_, bf16[1,512,512]{2,1,0:T(8,128)(2,1)S(1)} %collective-permute-done.17.refs_2_, ...), custom_call_target="tpu_custom_call", output_to_operand_aliasing={{}: (6, {})} | custom-call | tf_op jit(solution)/shard_map/space/pallas_call | solution.py:116
  86.9 0.1 fusion.3
  87.0 0.1 collective-permute-start.21
  87.1 0.5 collective-permute-start.20
  87.6 0.1 collective-permute-start.19
  87.7 0.4 collective-permute-start.18
  88.1 0.7 collective-permute-done.21.refs_7_
  88.8 0.1 collective-permute-start.8
  88.9 0.4 collective-permute-done.20.refs_6_
  89.4 0.6 collective-permute-done.19.refs_5_
  89.9 0.6 collective-permute-done.18.refs_4_
  90.5 5.2 %mix.6.refs_7_ = bf16[4,512,1024]{2,1,0:T(8,128)(2,1)} custom-call(bf16[512,2048]{1,0:T(8,128)(2,1)S(1)} %time_table.1.refs_0_, bf16[512,1536]{1,0:T(8,128)(2,1)S(1)} %space.6.refs_1_, bf16[512,1536]{1,0:T(8,128)(2,1)S(1)} %collective-permute-done.10.refs_2_, bf16[512,1536]{1,0:T(8,128)(2,1)S(1)} %collective-permute-done.11.refs_3_, ...), custom_call_target="tpu_custom_call", output_to_operand_aliasing={{}: (10, {})} | custom-call | tf_op jit(solution)/shard_map/mix/pallas_call | solution.py:172
  95.7 0.1 collective-permute-start.22
  95.9 1.8 %collective-permute-done.22.refs_4_ = bf16[512,512]{1,0:T(8,128)(2,1)S(1)} collective-permute-done((bf16[512,512]{1,0:T(8,128)(2,1)S(1)}, bf16[512,512]{1,0:T(8,128)(2,1)S(1)}, u32[]{:S(2)}, u32[]{:S(2)}) %collective-permute-start.22) | collective-permute-done | bytes 524320 | tf_op jit(solution)/shard_map/ppermute | solution.py:203
  97.6 2.0 %mix.7 = bf16[4,512,1024]{2,1,0:T(8,128)(2,1)} custom-call(bf16[512,2048]{1,0:T(8,128)(2,1)S(1)} %time_table.1.refs_0_, bf16[512,512]{1,0:T(8,128)(2,1)S(1)} %space.5.refs_1_, bf16[512,512]{1,0:T(8,128)(2,1)S(1)} %collective-permute-done.8.refs_2_, bf16[512,512]{1,0:T(8,128)(2,1)S(1)} %collective-permute-done.9.refs_3_, ...), custom_call_target="tpu_custom_call", output_to_operand_aliasing={{}: (7, {})} | custom-call | tf_op jit(solution)/shard_map/mix/pallas_call | solution.py:172
  (19 shorter events, 0.1 us)
Async XLA Ops:
  0.0 15.8 %copy-start.4 = (s32[1024]{0:T(1024)S(1)}, s32[1024]{0:T(1024)}, u32[]{:S(2)}) copy-start(s32[1024]{0:T(1024)} %param.8) | copy-start | bytes 12292
  0.0 15.8 %copy-start.3 = (bf16[1024,2048]{1,0:T(8,128)(2,1)S(1)}, bf16[1024,2048]{1,0:T(8,128)(2,1)}, u32[]{:S(2)}) copy-start(bf16[1024,2048]{1,0:T(8,128)(2,1)} %param.7) | copy-start | bytes 12582916
  1.5 27.1 %collective-permute-start.3 = (bf16[512,1024]{1,0:T(8,128)(2,1)S(1)}, bf16[512,1024]{1,0:T(8,128)(2,1)}, u32[]{:S(2)}, u32[]{:S(2)}) collective-permute-start(bf16[512,1024]{1,0:T(8,128)(2,1)S(1)} %slice_bitcast_fusion.1.refs_1_), channel_id=1, source_target_pairs={{0,8},{4,12},{8,0},{12,4},{1,9},{5,13},{9,1},{13,5},{2,10},{6,14},... | collective-permute-start | bytes 3145736 | tf_op jit(solution)/shard_map/ppermute | solution.py:206
  4.5 25.6 %collective-permute-start.2 = (bf16[512,1024]{1,0:T(8,128)(2,1)S(1)}, bf16[512,1024]{1,0:T(8,128)(2,1)}, u32[]{:S(2)}, u32[]{:S(2)}) collective-permute-start(bf16[512,1024]{1,0:T(8,128)(2,1)S(1)} %slice_bitcast_fusion.1.refs_1_), channel_id=1, source_target_pairs={{0,4},{4,0},{8,12},{12,8},{1,5},{5,1},{9,13},{13,9},{2,6},{6,2},{1... | collective-permute-start | bytes 3145736 | tf_op jit(solution)/shard_map/ppermute | solution.py:203
  5.8 45.2 %collective-permute-start.13 = (bf16[512,1024]{1,0:T(8,128)(2,1)S(1)}, bf16[512,1024]{1,0:T(8,128)(2,1)S(1)}, u32[]{:S(2)}, u32[]{:S(2)}) collective-permute-start(bf16[512,1024]{1,0:T(8,128)(2,1)S(1)} %slice_bitcast_fusion.refs_1_), channel_id=1, source_target_pairs={{0,8},{4,12},{8,0},{12,4},{1,9},{5,13},{9,1},{13,5},{2,10},{6,14},... | collective-permute-start | bytes 3145736 | tf_op jit(solution)/shard_map/ppermute | solution.py:206
  9.0 27.7 %collective-permute-start.1 = (bf16[2,512,512]{2,1,0:T(8,128)(2,1)}, bf16[2,512,512]{2,1,0:T(8,128)(2,1)}, u32[]{:S(2)}, u32[]{:S(2)}) collective-permute-start(bf16[2,512,512]{2,1,0:T(8,128)(2,1)} %get-tuple-element.19), channel_id=1, source_target_pairs={{1,0},{2,1},{3,2},{5,4},{6,5},{7,6},{9,8},{10,9},{11,10},{13,12},{... | collective-permute-start | bytes 3145736 | tf_op jit(solution)/shard_map/ppermute | solution.py:211
  10.3 27.6 %collective-permute-start = (bf16[2,512,512]{2,1,0:T(8,128)(2,1)}, bf16[2,512,512]{2,1,0:T(8,128)(2,1)}, u32[]{:S(2)}, u32[]{:S(2)}) collective-permute-start(bf16[2,512,512]{2,1,0:T(8,128)(2,1)} %get-tuple-element.20), channel_id=1, source_target_pairs={{0,1},{1,2},{2,3},{4,5},{5,6},{6,7},{8,9},{9,10},{10,11},{12,13},{... | collective-permute-start | bytes 3145736 | tf_op jit(solution)/shard_map/ppermute | solution.py:210
  15.8 4.0 %copy-start.5 = (bf16[2048]{0:T(1024)(128)(2,1)S(1)}, bf16[2048]{0:T(1024)(128)(2,1)}, u32[]{:S(2)}) copy-start(bf16[2048]{0:T(1024)(128)(2,1)} %param.6) | copy-start | bytes 12292
  28.6 9.3 %copy-start.1 = (bf16[1024,2048]{1,0:T(8,128)(2,1)S(1)}, bf16[1024,2048]{1,0:T(8,128)(2,1)}, u32[]{:S(2)}) copy-start(bf16[1024,2048]{1,0:T(8,128)(2,1)} %fusion.1.refs_3_) | copy-start | bytes 12582916
  30.0 7.9 %copy-start = (bf16[4,512,1024]{2,1,0:T(8,128)(2,1)S(1)}, bf16[4,512,1024]{2,1,0:T(8,128)(2,1)}, u32[]{:S(2)}) copy-start(bf16[4,512,1024]{2,1,0:T(8,128)(2,1)} %refs_6_.1) | copy-start | bytes 12582916
  30.0 2.0 %collective-permute-start.5 = (bf16[256,1024]{1,0:T(8,128)(2,1)S(1)}, bf16[256,1024]{1,0:T(8,128)(2,1)S(1)}, u32[]{:S(2)}, u32[]{:S(2)}) collective-permute-start(bf16[256,1024]{1,0:T(8,128)(2,1)S(1)} %get-tuple-element.31), channel_id=1, source_target_pairs={{0,4},{4,0},{8,12},{12,8},{1,5},{5,1},{9,13},{13,9},{2,6},{6,2},{1... | collective-permute-start | bytes 1572872 | tf_op jit(solution)/shard_map/ppermute | solution.py:203
  30.1 2.6 %collective-permute-start.4 = (bf16[256,1024]{1,0:T(8,128)(2,1)S(1)}, bf16[256,1024]{1,0:T(8,128)(2,1)S(1)}, u32[]{:S(2)}, u32[]{:S(2)}) collective-permute-start(bf16[256,1024]{1,0:T(8,128)(2,1)S(1)} %get-tuple-element.32), channel_id=1, source_target_pairs={{0,4},{4,0},{8,12},{12,8},{1,5},{5,1},{9,13},{13,9},{2,6},{6,2},{1... | collective-permute-start | bytes 1572872 | tf_op jit(solution)/shard_map/ppermute | solution.py:203
  32.0 19.8 %collective-permute-start.12 = (bf16[512,1024]{1,0:T(8,128)(2,1)S(1)}, bf16[512,1024]{1,0:T(8,128)(2,1)S(1)}, u32[]{:S(2)}, u32[]{:S(2)}) collective-permute-start(bf16[512,1024]{1,0:T(8,128)(2,1)S(1)} %slice_bitcast_fusion.refs_1_), channel_id=1, source_target_pairs={{0,4},{4,0},{8,12},{12,8},{1,5},{5,1},{9,13},{13,9},{2,6},{6,2},{1... | collective-permute-start | bytes 3145736 | tf_op jit(solution)/shard_map/ppermute | solution.py:203
  44.2 42.7 %collective-permute-start.11 = (bf16[512,1536]{1,0:T(8,128)(2,1)S(1)}, bf16[512,1536]{1,0:T(8,128)(2,1)S(1)}, u32[]{:S(2)}, u32[]{:S(2)}) collective-permute-start(bf16[512,1536]{1,0:T(8,128)(2,1)S(1)} %space.6.refs_1_), channel_id=1, source_target_pairs={{0,8},{4,12},{8,0},{12,4},{1,9},{5,13},{9,1},{13,5},{2,10},{6,14},... | collective-permute-start | bytes 4718600 | tf_op jit(solution)/shard_map/ppermute | solution.py:206
  51.0 2.0 %collective-permute-start.15 = (bf16[256,1024]{1,0:T(8,128)(2,1)S(1)}, bf16[256,1024]{1,0:T(8,128)(2,1)S(1)}, u32[]{:S(2)}, u32[]{:S(2)}) collective-permute-start(bf16[256,1024]{1,0:T(8,128)(2,1)S(1)} %get-tuple-element.27), channel_id=1, source_target_pairs={{0,4},{4,0},{8,12},{12,8},{1,5},{5,1},{9,13},{13,9},{2,6},{6,2},{1... | collective-permute-start | bytes 1572872 | tf_op jit(solution)/shard_map/ppermute | solution.py:203
  51.1 6.7 %collective-permute-start.14 = (bf16[256,1024]{1,0:T(8,128)(2,1)S(1)}, bf16[256,1024]{1,0:T(8,128)(2,1)S(1)}, u32[]{:S(2)}, u32[]{:S(2)}) collective-permute-start(bf16[256,1024]{1,0:T(8,128)(2,1)S(1)} %get-tuple-element.28), channel_id=1, source_target_pairs={{0,4},{4,0},{8,12},{12,8},{1,5},{5,1},{9,13},{13,9},{2,6},{6,2},{1... | collective-permute-start | bytes 1572872 | tf_op jit(solution)/shard_map/ppermute | solution.py:203
  51.6 36.1 %collective-permute-start.10 = (bf16[512,1536]{1,0:T(8,128)(2,1)S(1)}, bf16[512,1536]{1,0:T(8,128)(2,1)S(1)}, u32[]{:S(2)}, u32[]{:S(2)}) collective-permute-start(bf16[512,1536]{1,0:T(8,128)(2,1)S(1)} %space.6.refs_1_), channel_id=1, source_target_pairs={{0,4},{4,0},{8,12},{12,8},{1,5},{5,1},{9,13},{13,9},{2,6},{6,2},{1... | collective-permute-start | bytes 4718600 | tf_op jit(solution)/shard_map/ppermute | solution.py:203
  51.8 16.8 %collective-permute-start.7 = (bf16[1,512,512]{2,1,0:T(8,128)(2,1)S(1)}, bf16[1,512,512]{2,1,0:T(8,128)(2,1)S(1)}, u32[]{:S(2)}, u32[]{:S(2)}) collective-permute-start(bf16[1,512,512]{2,1,0:T(8,128)(2,1)S(1)} %get-tuple-element.29), channel_id=1, source_target_pairs={{1,0},{2,1},{3,2},{5,4},{6,5},{7,6},{9,8},{10,9},{11,10},{13,12},{... | collective-permute-start | bytes 1572872 | tf_op jit(solution)/shard_map/ppermute | solution.py:211
  53.1 19.4 %copy-start.2 = (f32[1024]{0:T(1024)S(1)}, f32[1024]{0:T(1024)}, u32[]{:S(2)}) copy-start(f32[1024]{0:T(1024)} %param.9) | copy-start | bytes 12292
  53.1 19.3 %collective-permute-start.6 = (bf16[1,512,512]{2,1,0:T(8,128)(2,1)S(1)}, bf16[1,512,512]{2,1,0:T(8,128)(2,1)S(1)}, u32[]{:S(2)}, u32[]{:S(2)}) collective-permute-start(bf16[1,512,512]{2,1,0:T(8,128)(2,1)S(1)} %get-tuple-element.30), channel_id=1, source_target_pairs={{0,1},{1,2},{2,3},{4,5},{5,6},{6,7},{8,9},{9,10},{10,11},{12,13},{... | collective-permute-start | bytes 1572872 | tf_op jit(solution)/shard_map/ppermute | solution.py:210
  60.8 20.1 %collective-permute-start.17 = (bf16[1,512,512]{2,1,0:T(8,128)(2,1)S(1)}, bf16[1,512,512]{2,1,0:T(8,128)(2,1)S(1)}, u32[]{:S(2)}, u32[]{:S(2)}) collective-permute-start(bf16[1,512,512]{2,1,0:T(8,128)(2,1)S(1)} %get-tuple-element.25), channel_id=1, source_target_pairs={{1,0},{2,1},{3,2},{5,4},{6,5},{7,6},{9,8},{10,9},{11,10},{13,12},{... | collective-permute-start | bytes 1572872 | tf_op jit(solution)/shard_map/ppermute | solution.py:211
  68.5 14.4 %collective-permute-start.16 = (bf16[1,512,512]{2,1,0:T(8,128)(2,1)S(1)}, bf16[1,512,512]{2,1,0:T(8,128)(2,1)S(1)}, u32[]{:S(2)}, u32[]{:S(2)}) collective-permute-start(bf16[1,512,512]{2,1,0:T(8,128)(2,1)S(1)} %get-tuple-element.26), channel_id=1, source_target_pairs={{0,1},{1,2},{2,3},{4,5},{5,6},{6,7},{8,9},{9,10},{10,11},{12,13},{... | collective-permute-start | bytes 1572872 | tf_op jit(solution)/shard_map/ppermute | solution.py:210
  79.2 16.5 %collective-permute-start.9 = (bf16[512,512]{1,0:T(8,128)(2,1)S(1)}, bf16[512,512]{1,0:T(8,128)(2,1)S(1)}, u32[]{:S(2)}, u32[]{:S(2)}) collective-permute-start(bf16[512,512]{1,0:T(8,128)(2,1)S(1)} %space.5.refs_1_), channel_id=1, source_target_pairs={{0,8},{4,12},{8,0},{12,4},{1,9},{5,13},{9,1},{13,5},{2,10},{6,14},... | collective-permute-start | bytes 1572872 | tf_op jit(solution)/shard_map/ppermute | solution.py:206
  87.0 1.8 %collective-permute-start.21 = (bf16[128,1536]{1,0:T(8,128)(2,1)S(1)}, bf16[128,1536]{1,0:T(8,128)(2,1)S(1)}, u32[]{:S(2)}, u32[]{:S(2)}) collective-permute-start(bf16[128,1536]{1,0:T(8,128)(2,1)S(1)} %get-tuple-element.21), channel_id=1, source_target_pairs={{0,4},{4,0},{8,12},{12,8},{1,5},{5,1},{9,13},{13,9},{2,6},{6,2},{1... | collective-permute-start | bytes 1179656 | tf_op jit(solution)/shard_map/ppermute | solution.py:203
  87.1 2.3 %collective-permute-start.20 = (bf16[128,1536]{1,0:T(8,128)(2,1)S(1)}, bf16[128,1536]{1,0:T(8,128)(2,1)S(1)}, u32[]{:S(2)}, u32[]{:S(2)}) collective-permute-start(bf16[128,1536]{1,0:T(8,128)(2,1)S(1)} %get-tuple-element.22), channel_id=1, source_target_pairs={{0,4},{4,0},{8,12},{12,8},{1,5},{5,1},{9,13},{13,9},{2,6},{6,2},{1... | collective-permute-start | bytes 1179656 | tf_op jit(solution)/shard_map/ppermute | solution.py:203
  87.6 2.3 %collective-permute-start.19 = (bf16[128,1536]{1,0:T(8,128)(2,1)S(1)}, bf16[128,1536]{1,0:T(8,128)(2,1)S(1)}, u32[]{:S(2)}, u32[]{:S(2)}) collective-permute-start(bf16[128,1536]{1,0:T(8,128)(2,1)S(1)} %get-tuple-element.23), channel_id=1, source_target_pairs={{0,4},{4,0},{8,12},{12,8},{1,5},{5,1},{9,13},{13,9},{2,6},{6,2},{1... | collective-permute-start | bytes 1179656 | tf_op jit(solution)/shard_map/ppermute | solution.py:203
  87.7 2.8 %collective-permute-start.18 = (bf16[128,1536]{1,0:T(8,128)(2,1)S(1)}, bf16[128,1536]{1,0:T(8,128)(2,1)S(1)}, u32[]{:S(2)}, u32[]{:S(2)}) collective-permute-start(bf16[128,1536]{1,0:T(8,128)(2,1)S(1)} %get-tuple-element.24), channel_id=1, source_target_pairs={{0,4},{4,0},{8,12},{12,8},{1,5},{5,1},{9,13},{13,9},{2,6},{6,2},{1... | collective-permute-start | bytes 1179656 | tf_op jit(solution)/shard_map/ppermute | solution.py:203
  88.8 7.1 %collective-permute-start.8 = (bf16[512,512]{1,0:T(8,128)(2,1)S(1)}, bf16[512,512]{1,0:T(8,128)(2,1)S(1)}, u32[]{:S(2)}, u32[]{:S(2)}) collective-permute-start(bf16[512,512]{1,0:T(8,128)(2,1)S(1)} %space.5.refs_1_), channel_id=1, source_target_pairs={{0,4},{4,0},{8,12},{12,8},{1,5},{5,1},{9,13},{13,9},{2,6},{6,2},{1... | collective-permute-start | bytes 1572872 | tf_op jit(solution)/shard_map/ppermute | solution.py:203
  95.7 1.9 %collective-permute-start.22 = (bf16[512,512]{1,0:T(8,128)(2,1)S(1)}, bf16[512,512]{1,0:T(8,128)(2,1)S(1)}, u32[]{:S(2)}, u32[]{:S(2)}) collective-permute-start(bf16[512,512]{1,0:T(8,128)(2,1)S(1)} %collective-permute-done.9.refs_3_), channel_id=1, source_target_pairs={{0,4},{4,0},{8,12},{12,8},{1,5},{5,1},{9,13},{13,9},{2,6},{6,2},{1... | collective-permute-start | bytes 1572872 | tf_op jit(solution)/shard_map/ppermute | solution.py:203

commit v3 on v2

--- a/solution.py
+++ b/solution.py
@@ -199,8 +199,8 @@
     up = [(i, i + 1) for i in range(sites - 1)]
     down = [(i + 1, i) for i in range(sites - 1)]
 
-    def to_core(block):
-        return lax.ppermute(block, "slot", swap)
+    def to_core(block, pieces=1):
+        return [lax.ppermute(part, "slot", swap) for part in jnp.split(block, pieces, axis=0)]
 
     def to_chips(block):
         return [lax.ppermute(block, "slot", [(i, (i + s) % count) for i in range(count)]) for s in shifts]
@@ -216,11 +216,11 @@
         order[0].extend([(-s) % count, (1 - s) % count])
         order[1].extend([(-s) % count, (-1 - s) % count])
 
-    def gathered(own, far, pieces, *others):
-        blocks = [[own], [to_core(own)]]
+    def gathered(own, near, far, pieces, *others):
+        blocks = [[own], near]
         for got in far:
             got = after(got, *others)
-            blocks += [[got], [to_core(part) for part in jnp.split(got, pieces, axis=0)]]
+            blocks += [[got], to_core(got, pieces)]
         return blocks
 
     firsts = probes // 2
@@ -238,22 +238,28 @@
     mask = (col[None, :] >= offsets[:, None]) & (col[None, :] < offsets[:, None] + width)
     band = jnp.where(mask, sp_weight, jnp.zeros_like(sp_weight))
 
+    near = [to_core(block) for block in own]
     columns = (probes - firsts) * width
-    mixed = [mix(table, gathered(own[0], far[0], 2, table, band))]
+    mixed = [mix(table, gathered(own[0], near[0], far[0], 2, table, band))]
     long = space(low, field, high, after(band, mixed[0]), firsts, 0, columns - half)
-    sent = [(0, long, to_chips(long), 4)]
+    far_long = to_chips(long)
     for p in range(1, firsts):
-        mixed.append(mix(table, gathered(own[p], far[p], 2, mixed[-1], long)))
+        mixed.append(mix(table, gathered(own[p], near[p], far[p], 2, mixed[-1], long)))
 
     image = None
     for p in range(firsts):
         got_low, got_high = halo(mixed[p])
         image = space(got_low, mixed[p], got_high, band, 0, 0, width, image=(noise, field, p, image))
         if p == 0:
+            near_long = to_core(after(long, image), 4)
             short = space(low, field, high, after(band, image), firsts, columns - half, half)
-            sent.append((columns - half, short, to_chips(short), 1))
-    for start, block, got, pieces in sent:
-        image = mix(table, gathered(block, got, pieces, image), image=(noise, field, firsts, start, image))
+            near_short, far_short = to_core(short), to_chips(short)
+    for start, block, beside, got, pieces in (
+        (0, long, near_long, far_long, 4),
+        (columns - half, short, near_short, far_short, 1),
+    ):
+        blocks = gathered(block, beside, got, pieces, image)
+        image = mix(table, blocks, image=(noise, field, firsts, start, image))
     return image
 
 

time: 100 us -> 99.4 us (level)
  waiting for transfers between devices: 24.7 us -> 22.3 us
  starting transfers between devices: 27.2 us -> 28.7 us
    ppermute x3, waiting for transfers between devices: 6.62 us -> 2.13 us  [halo(): lax.ppermute(block[:, :, :half], 'site', down)]
    ppermute x4, waiting for transfers between devices: 8.7 us -> 10.2 us  [to_chips(): lax.ppermute(block, 'slot', [(i, (i + s) % count) for i in range(count)])]
    ppermute x13 -> x16, waiting for transfers between devices: 6.04 us -> 6.42 us  [to_core(): lax.ppermute(part, 'slot', swap)]
    ppermute x13 -> x16, starting transfers between devices: 2.7 us -> 3.04 us  [to_core(): lax.ppermute(part, 'slot', swap)]
  transfers between devices with their start and end apart: 23 -> 26, of which waited for: 13 -> 18; matrix products, arithmetic and copies ran while one was open for 11% -> 12% of each run, Pallas kernels for 33% -> 33%
where the time goes in v3:
time: 99.4 us; the launch traced here: 99 us
  Pallas kernels  34.7 us (35%)
  starting transfers between devices  28.7 us (29%)
  waiting for transfers between devices  22.3 us (22%)
  local copies, waits for them, and re-layouts  8.42 us (8%)
  other arithmetic  4.72 us (5%)
    pallas_call x4, Pallas kernels, space(): pl.pallas_call(functools.partial(space_kernel, half, image is not None),...  17 us
    ppermute x3, starting transfers between devices, halo(): lax.ppermute(block[:, :, width - half:], 'site', up)  14.8 us
    pallas_call x4, Pallas kernels, mix(): pl.pallas_call(functools.partial(mix_kernel, [len(block) for block in blo...  14 us
    ppermute x4, waiting for transfers between devices, to_chips(): lax.ppermute(block, 'slot', [(i, (i + s) % count) for i in range(count)])  10.2 us
    ppermute x4, starting transfers between devices, to_chips(): lax.ppermute(block, 'slot', [(i, (i + s) % count) for i in range(count)])  6.99 us
    ppermute x16, waiting for transfers between devices, to_core(): lax.ppermute(part, 'slot', swap)  6.42 us
    select_n x1, other arithmetic, on_device(): band = jnp.where(mask, sp_weight, jnp.zeros_like(sp_weight))  4.01 us
    ppermute x3, starting transfers between devices, halo(): lax.ppermute(block[:, :, :half], 'site', down)  3.86 us
  transfers between devices with their start and end apart: 26, of which 18 were waited for; matrix products, arithmetic and copies ran while one was open for 12% of the time, Pallas kernels for 33%

profile of v3, /device:TPU:0, one launch (start us, length us, event | category | flops | bytes accessed | tf_op | source)
XLA Modules:
  0.0 99.0 jit_solution(9013736562690845001)
XLA Ops:
  0.0 1.4 %slice_bitcast_fusion.1.refs_1_ = bf16[512,1024]{1,0:T(8,128)(2,1)S(1)} fusion(bf16[4,512,1024]{2,1,0:T(8,128)(2,1)} %refs_6_.1), kind=kLoop, calls=%fused_computation.5 | loop fusion | bytes 2097152 | tf_op jit(solution)/shard_map/squeeze | solution.py:230
  1.5 3.0 %collective-permute-start.3 = (bf16[512,1024]{1,0:T(8,128)(2,1)S(1)}, bf16[512,1024]{1,0:T(8,128)(2,1)}, u32[]{:S(2)}, u32[]{:S(2)}) collective-permute-start(bf16[512,1024]{1,0:T(8,128)(2,1)S(1)} %slice_bitcast_fusion.1.refs_1_), channel_id=1, source_target_pairs={{0,8},{4,12},{8,0},{12,4},{1,9},{5,13},{9,1},{13,5},{2,10},{6,14},... | collective-permute-start | bytes 3145736 | tf_op jit(solution)/shard_map/ppermute | solution.py:206
  4.5 1.3 %slice_bitcast_fusion.refs_1_ = bf16[512,1024]{1,0:T(8,128)(2,1)S(1)} fusion(bf16[4,512,1024]{2,1,0:T(8,128)(2,1)} %refs_6_.1), kind=kLoop, calls=%fused_computation.4 | loop fusion | bytes 2097152 | tf_op jit(solution)/shard_map/squeeze | solution.py:230
  5.8 0.2 collective-permute-start.16
  5.9 3.0 %fusion.2 = (bf16[2,512,512]{2,1,0:T(8,128)(2,1)}, bf16[2,512,512]{2,1,0:T(8,128)(2,1)}) fusion(bf16[4,512,1024]{2,1,0:T(8,128)(2,1)} %refs_6_.1), kind=kLoop, calls=%fused_computation.8 | loop fusion | bytes 4194304 | tf_op jit(solution)/shard_map/slice | solution.py:211
  9.0 1.3 %collective-permute-start.1 = (bf16[2,512,512]{2,1,0:T(8,128)(2,1)}, bf16[2,512,512]{2,1,0:T(8,128)(2,1)}, u32[]{:S(2)}, u32[]{:S(2)}) collective-permute-start(bf16[2,512,512]{2,1,0:T(8,128)(2,1)} %get-tuple-element.21), channel_id=1, source_target_pairs={{1,0},{2,1},{3,2},{5,4},{6,5},{7,6},{9,8},{10,9},{11,10},{13,12},{... | collective-permute-start | bytes 3145736 | tf_op jit(solution)/shard_map/ppermute | solution.py:211
  10.3 5.5 %collective-permute-start = (bf16[2,512,512]{2,1,0:T(8,128)(2,1)}, bf16[2,512,512]{2,1,0:T(8,128)(2,1)}, u32[]{:S(2)}, u32[]{:S(2)}) collective-permute-start(bf16[2,512,512]{2,1,0:T(8,128)(2,1)} %get-tuple-element.22), channel_id=1, source_target_pairs={{0,1},{1,2},{2,3},{4,5},{5,6},{6,7},{8,9},{9,10},{10,11},{12,13},{... | collective-permute-start | bytes 3145736 | tf_op jit(solution)/shard_map/ppermute | solution.py:210
  15.8 4.0 %fusion.1.refs_3_ = bf16[1024,2048]{1,0:T(8,128)(2,1)} fusion(bf16[1024,2048]{1,0:T(8,128)(2,1)S(1)} %copy-done.3, s32[1024]{0:T(1024)S(1)} %broadcast_add_fusion, s32[1024]{0:T(1024)S(1)} %copy-done.4), kind=kLoop, calls=%fused_computation.3 | loop fusion | flops 8388608 | bytes 8396800 | tf_op jit(solution)/shard_map/jit(_where)/select_n | solution.py:239
  19.8 0.5 slice.33
  20.4 0.1 slice.34
  20.5 0.1 reverse
  20.5 0.1 slice.49
  20.6 0.7 maximum_convert_fusion.row_ref
  21.3 3.6 %time_table.1.refs_0_ = bf16[512,2048]{1,0:T(8,128)(2,1)S(1)} custom-call(s32[1]{0:T(128)} %bitcast.core_ref, f32[1,2048]{1,0:T(1,128)S(1)} %maximum_convert_fusion.row_ref), custom_call_target="tpu_custom_call" | custom-call | tf_op jit(solution)/shard_map/time_table/pallas_call | solution.py:51
  24.9 3.6 %collective-permute-done.3.refs_3_ = bf16[512,1024]{1,0:T(8,128)(2,1)} collective-permute-done((bf16[512,1024]{1,0:T(8,128)(2,1)S(1)}, bf16[512,1024]{1,0:T(8,128)(2,1)}, u32[]{:S(2)}, u32[]{:S(2)}) %collective-permute-start.3) | collective-permute-done | bytes 1048608 | tf_op jit(solution)/shard_map/ppermute | solution.py:206
  28.6 1.4 %fusion.8 = (bf16[256,1024]{1,0:T(8,128)(2,1)S(1)}, bf16[256,1024]{1,0:T(8,128)(2,1)S(1)}) fusion(bf16[512,1024]{1,0:T(8,128)(2,1)} %collective-permute-done.3.refs_3_), kind=kLoop, calls=%fused_computation.14 | loop fusion | bytes 2097152 | tf_op jit(solution)/shard_map/split | solution.py:203
  30.0 0.1 collective-permute-start.5
  30.1 0.5 collective-permute-start.4
  30.6 1.4 %collective-permute-done.5.refs_5_ = bf16[256,1024]{1,0:T(8,128)(2,1)S(1)} collective-permute-done((bf16[256,1024]{1,0:T(8,128)(2,1)S(1)}, bf16[256,1024]{1,0:T(8,128)(2,1)S(1)}, u32[]{:S(2)}, u32[]{:S(2)}) %collective-permute-start.5) | collective-permute-done | bytes 524320 | tf_op jit(solution)/shard_map/ppermute | solution.py:203
  32.0 0.1 collective-permute-start.15
  32.1 0.6 collective-permute-done.4.refs_4_
  32.7 3.8 %mix.4.refs_1_ = bf16[1,512,1024]{2,1,0:T(8,128)(2,1)S(1)} custom-call(bf16[512,2048]{1,0:T(8,128)(2,1)S(1)} %time_table.1.refs_0_, bf16[512,1024]{1,0:T(8,128)(2,1)S(1)} %slice_bitcast_fusion.1.refs_1_, bf16[512,1024]{1,0:T(8,128)(2,1)} %collective-permute-done.2.refs_2_, bf16[512,1024]{1,0:T(8,128)(2,1)} %collective-permute-done.3.refs_3_, ...), custom_call_target="tpu_custom_call" | custom-call | tf_op jit(solution)/shard_map/mix/pallas_call | solution.py:172
  36.6 0.2 collective-permute-done.1.refs_2_
  36.7 1.2 %collective-permute-done.refs_0_ = bf16[2,512,512]{2,1,0:T(8,128)(2,1)} collective-permute-done((bf16[2,512,512]{2,1,0:T(8,128)(2,1)}, bf16[2,512,512]{2,1,0:T(8,128)(2,1)}, u32[]{:S(2)}, u32[]{:S(2)}) %collective-permute-start) | collective-permute-done | bytes 1048608 | tf_op jit(solution)/shard_map/ppermute | solution.py:210
  37.9 6.3 %space.6.refs_1_ = bf16[512,1536]{1,0:T(8,128)(2,1)S(1)} custom-call(bf16[2,512,512]{2,1,0:T(8,128)(2,1)} %collective-permute-done.refs_0_, bf16[4,512,1024]{2,1,0:T(8,128)(2,1)S(1)} %copy-done, bf16[2,512,512]{2,1,0:T(8,128)(2,1)} %collective-permute-done.1.refs_2_, bf16[1024,2048]{1,0:T(8,128)(2,1)S(1)} %copy-done.1), custom_call_target="tpu_custom_call" | custom-call | tf_op jit(solution)/shard_map/space/pallas_call | solution.py:116
  44.2 1.7 %collective-permute-start.14 = (bf16[512,1536]{1,0:T(8,128)(2,1)S(1)}, bf16[512,1536]{1,0:T(8,128)(2,1)S(1)}, u32[]{:S(2)}, u32[]{:S(2)}) collective-permute-start(bf16[512,1536]{1,0:T(8,128)(2,1)S(1)} %space.6.refs_1_), channel_id=1, source_target_pairs={{0,8},{4,12},{8,0},{12,4},{1,9},{5,13},{9,1},{13,5},{2,10},{6,14},... | collective-permute-start | bytes 4718600 | tf_op jit(solution)/shard_map/ppermute | solution.py:206
  46.0 5.0 %collective-permute-done.16.refs_3_ = bf16[512,1024]{1,0:T(8,128)(2,1)S(1)} collective-permute-done((bf16[512,1024]{1,0:T(8,128)(2,1)S(1)}, bf16[512,1024]{1,0:T(8,128)(2,1)S(1)}, u32[]{:S(2)}, u32[]{:S(2)}) %collective-permute-start.16) | collective-permute-done | bytes 1048608 | tf_op jit(solution)/shard_map/ppermute | solution.py:206
  51.0 0.1 collective-permute-start.18
  51.1 0.5 collective-permute-start.17
  51.6 0.1 fusion.7
  51.7 1.3 %collective-permute-start.7 = (bf16[1,512,512]{2,1,0:T(8,128)(2,1)S(1)}, bf16[1,512,512]{2,1,0:T(8,128)(2,1)S(1)}, u32[]{:S(2)}, u32[]{:S(2)}) collective-permute-start(bf16[1,512,512]{2,1,0:T(8,128)(2,1)S(1)} %get-tuple-element.35), channel_id=1, source_target_pairs={{1,0},{2,1},{3,2},{5,4},{6,5},{7,6},{9,8},{10,9},{11,10},{13,12},{... | collective-permute-start | bytes 1572872 | tf_op jit(solution)/shard_map/ppermute | solution.py:211
  53.0 4.7 %collective-permute-start.6 = (bf16[1,512,512]{2,1,0:T(8,128)(2,1)S(1)}, bf16[1,512,512]{2,1,0:T(8,128)(2,1)S(1)}, u32[]{:S(2)}, u32[]{:S(2)}) collective-permute-start(bf16[1,512,512]{2,1,0:T(8,128)(2,1)S(1)} %get-tuple-element.36), channel_id=1, source_target_pairs={{0,1},{1,2},{2,3},{4,5},{5,6},{6,7},{8,9},{9,10},{10,11},{12,13},{... | collective-permute-start | bytes 1572872 | tf_op jit(solution)/shard_map/ppermute | solution.py:210
  57.7 2.9 %mix.5.refs_1_ = bf16[1,512,1024]{2,1,0:T(8,128)(2,1)S(1)} custom-call(bf16[512,2048]{1,0:T(8,128)(2,1)S(1)} %time_table.1.refs_0_, bf16[512,1024]{1,0:T(8,128)(2,1)S(1)} %slice_bitcast_fusion.refs_1_, bf16[512,1024]{1,0:T(8,128)(2,1)S(1)} %collective-permute-done.15.refs_2_, bf16[512,1024]{1,0:T(8,128)(2,1)S(1)} %collective-permute-done.16.refs_3_, ...), custom_call_target="tpu_custom_call" | custom-call | tf_op jit(solution)/shard_map/mix/pallas_call | solution.py:172
  60.6 0.1 fusion.5
  60.7 1.3 %collective-permute-start.20 = (bf16[1,512,512]{2,1,0:T(8,128)(2,1)S(1)}, bf16[1,512,512]{2,1,0:T(8,128)(2,1)S(1)}, u32[]{:S(2)}, u32[]{:S(2)}) collective-permute-start(bf16[1,512,512]{2,1,0:T(8,128)(2,1)S(1)} %get-tuple-element.31), channel_id=1, source_target_pairs={{1,0},{2,1},{3,2},{5,4},{6,5},{7,6},{9,8},{10,9},{11,10},{13,12},{... | collective-permute-start | bytes 1572872 | tf_op jit(solution)/shard_map/ppermute | solution.py:211
  62.0 4.6 %collective-permute-start.19 = (bf16[1,512,512]{2,1,0:T(8,128)(2,1)S(1)}, bf16[1,512,512]{2,1,0:T(8,128)(2,1)S(1)}, u32[]{:S(2)}, u32[]{:S(2)}) collective-permute-start(bf16[1,512,512]{2,1,0:T(8,128)(2,1)S(1)} %get-tuple-element.32), channel_id=1, source_target_pairs={{0,1},{1,2},{2,3},{4,5},{5,6},{6,7},{8,9},{9,10},{10,11},{12,13},{... | collective-permute-start | bytes 1572872 | tf_op jit(solution)/shard_map/ppermute | solution.py:210
  66.6 1.8 %collective-permute-done.7.refs_2_ = bf16[1,512,512]{2,1,0:T(8,128)(2,1)S(1)} collective-permute-done((bf16[1,512,512]{2,1,0:T(8,128)(2,1)S(1)}, bf16[1,512,512]{2,1,0:T(8,128)(2,1)S(1)}, u32[]{:S(2)}, u32[]{:S(2)}) %collective-permute-start.7) | collective-permute-done | bytes 524320 | tf_op jit(solution)/shard_map/ppermute | solution.py:211
  68.4 1.5 %collective-permute-done.6.refs_0_ = bf16[1,512,512]{2,1,0:T(8,128)(2,1)S(1)} collective-permute-done((bf16[1,512,512]{2,1,0:T(8,128)(2,1)S(1)}, bf16[1,512,512]{2,1,0:T(8,128)(2,1)S(1)}, u32[]{:S(2)}, u32[]{:S(2)}) %collective-permute-start.6) | collective-permute-done | bytes 524320 | tf_op jit(solution)/shard_map/ppermute | solution.py:210
  69.9 4.0 %space.4.refs_6_ = bf16[4,512,1024]{2,1,0:T(8,128)(2,1)} custom-call(bf16[1,512,512]{2,1,0:T(8,128)(2,1)S(1)} %collective-permute-done.6.refs_0_, bf16[1,512,1024]{2,1,0:T(8,128)(2,1)S(1)} %mix.4.refs_1_, bf16[1,512,512]{2,1,0:T(8,128)(2,1)S(1)} %collective-permute-done.7.refs_2_, bf16[1024,2048]{1,0:T(8,128)(2,1)S(1)} %copy-done.1, f32[1,1024]{1,0:T(1,128)S(1)} %bitcast.8, ...), custom_call_target="tpu_custom_call" | custom-call | tf_op jit(solution)/shard_map/space/pallas_call | solution.py:116
  73.9 2.8 %space.5.refs_1_ = bf16[512,512]{1,0:T(8,128)(2,1)S(1)} custom-call(bf16[2,512,512]{2,1,0:T(8,128)(2,1)} %collective-permute-done.refs_0_, bf16[4,512,1024]{2,1,0:T(8,128)(2,1)S(1)} %copy-done, bf16[2,512,512]{2,1,0:T(8,128)(2,1)} %collective-permute-done.1.refs_2_, bf16[1024,2048]{1,0:T(8,128)(2,1)S(1)} %copy-done.1), custom_call_target="tpu_custom_call" | custom-call | tf_op jit(solution)/shard_map/space/pallas_call | solution.py:116
  76.7 2.1 %collective-permute-start.9 = (bf16[512,512]{1,0:T(8,128)(2,1)S(1)}, bf16[512,512]{1,0:T(8,128)(2,1)S(1)}, u32[]{:S(2)}, u32[]{:S(2)}) collective-permute-start(bf16[512,512]{1,0:T(8,128)(2,1)S(1)} %space.5.refs_1_), channel_id=1, source_target_pairs={{0,8},{4,12},{8,0},{12,4},{1,9},{5,13},{9,1},{13,5},{2,10},{6,14},... | collective-permute-start | bytes 1572872 | tf_op jit(solution)/shard_map/ppermute | solution.py:206
  78.7 0.1 fusion.4
  78.9 0.1 collective-permute-start.13
  78.9 0.2 collective-permute-done.20.refs_2_
  79.1 0.3 collective-permute-start.12
  79.4 0.9 collective-permute-done.19.refs_0_
  80.3 4.0 %space.7.refs_13_ = bf16[4,512,1024]{2,1,0:T(8,128)(2,1)} custom-call(bf16[1,512,512]{2,1,0:T(8,128)(2,1)S(1)} %collective-permute-done.19.refs_0_, bf16[1,512,1024]{2,1,0:T(8,128)(2,1)S(1)} %mix.5.refs_1_, bf16[1,512,512]{2,1,0:T(8,128)(2,1)S(1)} %collective-permute-done.20.refs_2_, ...), custom_call_target="tpu_custom_call", output_to_operand_aliasing={{}: (6, {})} | custom-call | tf_op jit(solution)/shard_map/space/pallas_call | solution.py:116
  84.3 0.4 collective-permute-done.14.refs_6_
  84.6 0.1 collective-permute-start.10
  84.8 0.1 fusion.3
  84.9 0.4 collective-permute-start.24
  85.3 0.1 collective-permute-start.23
  85.5 0.4 collective-permute-start.22
  85.9 0.5 collective-permute-done.10.refs_2_
  86.4 0.1 collective-permute-start.21
  86.5 0.4 collective-permute-done.24.refs_10_
  86.9 0.1 collective-permute-start.8
  87.1 0.4 collective-permute-done.23.refs_9_
  87.5 0.6 collective-permute-done.22.refs_8_
  88.1 0.6 collective-permute-done.21.refs_7_
  88.6 5.3 %mix.6.refs_7_ = bf16[4,512,1024]{2,1,0:T(8,128)(2,1)} custom-call(bf16[512,2048]{1,0:T(8,128)(2,1)S(1)} %time_table.1.refs_0_, bf16[512,1536]{1,0:T(8,128)(2,1)S(1)} %space.6.refs_1_, bf16[128,1536]{1,0:T(8,128)(2,1)S(1)} %collective-permute-done.10.refs_2_, bf16[128,1536]{1,0:T(8,128)(2,1)S(1)} %collective-permute-done.11.refs_3_, ...), custom_call_target="tpu_custom_call", output_to_operand_aliasing={{}: (13, {})} | custom-call | tf_op jit(solution)/shard_map/mix/pallas_call | solution.py:172
  93.9 1.2 %collective-permute-done.9.refs_3_ = bf16[512,512]{1,0:T(8,128)(2,1)S(1)} collective-permute-done((bf16[512,512]{1,0:T(8,128)(2,1)S(1)}, bf16[512,512]{1,0:T(8,128)(2,1)S(1)}, u32[]{:S(2)}, u32[]{:S(2)}) %collective-permute-start.9) | collective-permute-done | bytes 524320 | tf_op jit(solution)/shard_map/ppermute | solution.py:206
  95.1 1.9 %collective-permute-done.25.refs_4_ = bf16[512,512]{1,0:T(8,128)(2,1)S(1)} collective-permute-done((bf16[512,512]{1,0:T(8,128)(2,1)S(1)}, bf16[512,512]{1,0:T(8,128)(2,1)S(1)}, u32[]{:S(2)}, u32[]{:S(2)}) %collective-permute-start.25) | collective-permute-done | bytes 524320 | tf_op jit(solution)/shard_map/ppermute | solution.py:203
  97.0 2.0 %mix.7 = bf16[4,512,1024]{2,1,0:T(8,128)(2,1)} custom-call(bf16[512,2048]{1,0:T(8,128)(2,1)S(1)} %time_table.1.refs_0_, bf16[512,512]{1,0:T(8,128)(2,1)S(1)} %space.5.refs_1_, bf16[512,512]{1,0:T(8,128)(2,1)S(1)} %collective-permute-done.8.refs_2_, bf16[512,512]{1,0:T(8,128)(2,1)S(1)} %collective-permute-done.9.refs_3_, ...), custom_call_target="tpu_custom_call", output_to_operand_aliasing={{}: (7, {})} | custom-call | tf_op jit(solution)/shard_map/mix/pallas_call | solution.py:172
  (26 shorter events, 0.1 us)
Async XLA Ops:
  0.0 15.8 %copy-start.4 = (s32[1024]{0:T(1024)S(1)}, s32[1024]{0:T(1024)}, u32[]{:S(2)}) copy-start(s32[1024]{0:T(1024)} %param.8) | copy-start | bytes 12292
  0.0 15.8 %copy-start.3 = (bf16[1024,2048]{1,0:T(8,128)(2,1)S(1)}, bf16[1024,2048]{1,0:T(8,128)(2,1)}, u32[]{:S(2)}) copy-start(bf16[1024,2048]{1,0:T(8,128)(2,1)} %param.7) | copy-start | bytes 12582916
  1.5 27.1 %collective-permute-start.3 = (bf16[512,1024]{1,0:T(8,128)(2,1)S(1)}, bf16[512,1024]{1,0:T(8,128)(2,1)}, u32[]{:S(2)}, u32[]{:S(2)}) collective-permute-start(bf16[512,1024]{1,0:T(8,128)(2,1)S(1)} %slice_bitcast_fusion.1.refs_1_), channel_id=1, source_target_pairs={{0,8},{4,12},{8,0},{12,4},{1,9},{5,13},{9,1},{13,5},{2,10},{6,14},... | collective-permute-start | bytes 3145736 | tf_op jit(solution)/shard_map/ppermute | solution.py:206
  4.5 25.6 %collective-permute-start.2 = (bf16[512,1024]{1,0:T(8,128)(2,1)S(1)}, bf16[512,1024]{1,0:T(8,128)(2,1)}, u32[]{:S(2)}, u32[]{:S(2)}) collective-permute-start(bf16[512,1024]{1,0:T(8,128)(2,1)S(1)} %slice_bitcast_fusion.1.refs_1_), channel_id=1, source_target_pairs={{0,4},{4,0},{8,12},{12,8},{1,5},{5,1},{9,13},{13,9},{2,6},{6,2},{1... | collective-permute-start | bytes 3145736 | tf_op jit(solution)/shard_map/ppermute | solution.py:203
  5.8 45.2 %collective-permute-start.16 = (bf16[512,1024]{1,0:T(8,128)(2,1)S(1)}, bf16[512,1024]{1,0:T(8,128)(2,1)S(1)}, u32[]{:S(2)}, u32[]{:S(2)}) collective-permute-start(bf16[512,1024]{1,0:T(8,128)(2,1)S(1)} %slice_bitcast_fusion.refs_1_), channel_id=1, source_target_pairs={{0,8},{4,12},{8,0},{12,4},{1,9},{5,13},{9,1},{13,5},{2,10},{6,14},... | collective-permute-start | bytes 3145736 | tf_op jit(solution)/shard_map/ppermute | solution.py:206
  9.0 27.7 %collective-permute-start.1 = (bf16[2,512,512]{2,1,0:T(8,128)(2,1)}, bf16[2,512,512]{2,1,0:T(8,128)(2,1)}, u32[]{:S(2)}, u32[]{:S(2)}) collective-permute-start(bf16[2,512,512]{2,1,0:T(8,128)(2,1)} %get-tuple-element.21), channel_id=1, source_target_pairs={{1,0},{2,1},{3,2},{5,4},{6,5},{7,6},{9,8},{10,9},{11,10},{13,12},{... | collective-permute-start | bytes 3145736 | tf_op jit(solution)/shard_map/ppermute | solution.py:211
  10.3 27.6 %collective-permute-start = (bf16[2,512,512]{2,1,0:T(8,128)(2,1)}, bf16[2,512,512]{2,1,0:T(8,128)(2,1)}, u32[]{:S(2)}, u32[]{:S(2)}) collective-permute-start(bf16[2,512,512]{2,1,0:T(8,128)(2,1)} %get-tuple-element.22), channel_id=1, source_target_pairs={{0,1},{1,2},{2,3},{4,5},{5,6},{6,7},{8,9},{9,10},{10,11},{12,13},{... | collective-permute-start | bytes 3145736 | tf_op jit(solution)/shard_map/ppermute | solution.py:210
  15.8 4.0 %copy-start.5 = (bf16[2048]{0:T(1024)(128)(2,1)S(1)}, bf16[2048]{0:T(1024)(128)(2,1)}, u32[]{:S(2)}) copy-start(bf16[2048]{0:T(1024)(128)(2,1)} %param.6) | copy-start | bytes 12292
  28.6 9.3 %copy-start.1 = (bf16[1024,2048]{1,0:T(8,128)(2,1)S(1)}, bf16[1024,2048]{1,0:T(8,128)(2,1)}, u32[]{:S(2)}) copy-start(bf16[1024,2048]{1,0:T(8,128)(2,1)} %fusion.1.refs_3_) | copy-start | bytes 12582916
  30.0 7.9 %copy-start = (bf16[4,512,1024]{2,1,0:T(8,128)(2,1)S(1)}, bf16[4,512,1024]{2,1,0:T(8,128)(2,1)}, u32[]{:S(2)}) copy-start(bf16[4,512,1024]{2,1,0:T(8,128)(2,1)} %refs_6_.1) | copy-start | bytes 12582916
  30.0 2.0 %collective-permute-start.5 = (bf16[256,1024]{1,0:T(8,128)(2,1)S(1)}, bf16[256,1024]{1,0:T(8,128)(2,1)S(1)}, u32[]{:S(2)}, u32[]{:S(2)}) collective-permute-start(bf16[256,1024]{1,0:T(8,128)(2,1)S(1)} %get-tuple-element.37), channel_id=1, source_target_pairs={{0,4},{4,0},{8,12},{12,8},{1,5},{5,1},{9,13},{13,9},{2,6},{6,2},{1... | collective-permute-start | bytes 1572872 | tf_op jit(solution)/shard_map/ppermute | solution.py:203
  30.1 2.6 %collective-permute-start.4 = (bf16[256,1024]{1,0:T(8,128)(2,1)S(1)}, bf16[256,1024]{1,0:T(8,128)(2,1)S(1)}, u32[]{:S(2)}, u32[]{:S(2)}) collective-permute-start(bf16[256,1024]{1,0:T(8,128)(2,1)S(1)} %get-tuple-element.38), channel_id=1, source_target_pairs={{0,4},{4,0},{8,12},{12,8},{1,5},{5,1},{9,13},{13,9},{2,6},{6,2},{1... | collective-permute-start | bytes 1572872 | tf_op jit(solution)/shard_map/ppermute | solution.py:203
  32.0 21.0 %collective-permute-start.15 = (bf16[512,1024]{1,0:T(8,128)(2,1)S(1)}, bf16[512,1024]{1,0:T(8,128)(2,1)S(1)}, u32[]{:S(2)}, u32[]{:S(2)}) collective-permute-start(bf16[512,1024]{1,0:T(8,128)(2,1)S(1)} %slice_bitcast_fusion.refs_1_), channel_id=1, source_target_pairs={{0,4},{4,0},{8,12},{12,8},{1,5},{5,1},{9,13},{13,9},{2,6},{6,2},{1... | collective-permute-start | bytes 3145736 | tf_op jit(solution)/shard_map/ppermute | solution.py:203
  44.2 40.4 %collective-permute-start.14 = (bf16[512,1536]{1,0:T(8,128)(2,1)S(1)}, bf16[512,1536]{1,0:T(8,128)(2,1)S(1)}, u32[]{:S(2)}, u32[]{:S(2)}) collective-permute-start(bf16[512,1536]{1,0:T(8,128)(2,1)S(1)} %space.6.refs_1_), channel_id=1, source_target_pairs={{0,8},{4,12},{8,0},{12,4},{1,9},{5,13},{9,1},{13,5},{2,10},{6,14},... | collective-permute-start | bytes 4718600 | tf_op jit(solution)/shard_map/ppermute | solution.py:206
  51.0 6.7 %collective-permute-start.18 = (bf16[256,1024]{1,0:T(8,128)(2,1)S(1)}, bf16[256,1024]{1,0:T(8,128)(2,1)S(1)}, u32[]{:S(2)}, u32[]{:S(2)}) collective-permute-start(bf16[256,1024]{1,0:T(8,128)(2,1)S(1)} %get-tuple-element.33), channel_id=1, source_target_pairs={{0,4},{4,0},{8,12},{12,8},{1,5},{5,1},{9,13},{13,9},{2,6},{6,2},{1... | collective-permute-start | bytes 1572872 | tf_op jit(solution)/shard_map/ppermute | solution.py:203
  51.1 6.6 %collective-permute-start.17 = (bf16[256,1024]{1,0:T(8,128)(2,1)S(1)}, bf16[256,1024]{1,0:T(8,128)(2,1)S(1)}, u32[]{:S(2)}, u32[]{:S(2)}) collective-permute-start(bf16[256,1024]{1,0:T(8,128)(2,1)S(1)} %get-tuple-element.34), channel_id=1, source_target_pairs={{0,4},{4,0},{8,12},{12,8},{1,5},{5,1},{9,13},{13,9},{2,6},{6,2},{1... | collective-permute-start | bytes 1572872 | tf_op jit(solution)/shard_map/ppermute | solution.py:203
  51.7 16.7 %collective-permute-start.7 = (bf16[1,512,512]{2,1,0:T(8,128)(2,1)S(1)}, bf16[1,512,512]{2,1,0:T(8,128)(2,1)S(1)}, u32[]{:S(2)}, u32[]{:S(2)}) collective-permute-start(bf16[1,512,512]{2,1,0:T(8,128)(2,1)S(1)} %get-tuple-element.35), channel_id=1, source_target_pairs={{1,0},{2,1},{3,2},{5,4},{6,5},{7,6},{9,8},{10,9},{11,10},{13,12},{... | collective-permute-start | bytes 1572872 | tf_op jit(solution)/shard_map/ppermute | solution.py:211
  53.0 16.9 %copy-start.2 = (f32[1024]{0:T(1024)S(1)}, f32[1024]{0:T(1024)}, u32[]{:S(2)}) copy-start(f32[1024]{0:T(1024)} %param.9) | copy-start | bytes 12292
  53.0 16.9 %collective-permute-start.6 = (bf16[1,512,512]{2,1,0:T(8,128)(2,1)S(1)}, bf16[1,512,512]{2,1,0:T(8,128)(2,1)S(1)}, u32[]{:S(2)}, u32[]{:S(2)}) collective-permute-start(bf16[1,512,512]{2,1,0:T(8,128)(2,1)S(1)} %get-tuple-element.36), channel_id=1, source_target_pairs={{0,1},{1,2},{2,3},{4,5},{5,6},{6,7},{8,9},{9,10},{10,11},{12,13},{... | collective-permute-start | bytes 1572872 | tf_op jit(solution)/shard_map/ppermute | solution.py:210
  60.7 18.4 %collective-permute-start.20 = (bf16[1,512,512]{2,1,0:T(8,128)(2,1)S(1)}, bf16[1,512,512]{2,1,0:T(8,128)(2,1)S(1)}, u32[]{:S(2)}, u32[]{:S(2)}) collective-permute-start(bf16[1,512,512]{2,1,0:T(8,128)(2,1)S(1)} %get-tuple-element.31), channel_id=1, source_target_pairs={{1,0},{2,1},{3,2},{5,4},{6,5},{7,6},{9,8},{10,9},{11,10},{13,12},{... | collective-permute-start | bytes 1572872 | tf_op jit(solution)/shard_map/ppermute | solution.py:211
  62.0 18.3 %collective-permute-start.19 = (bf16[1,512,512]{2,1,0:T(8,128)(2,1)S(1)}, bf16[1,512,512]{2,1,0:T(8,128)(2,1)S(1)}, u32[]{:S(2)}, u32[]{:S(2)}) collective-permute-start(bf16[1,512,512]{2,1,0:T(8,128)(2,1)S(1)} %get-tuple-element.32), channel_id=1, source_target_pairs={{0,1},{1,2},{2,3},{4,5},{5,6},{6,7},{8,9},{9,10},{10,11},{12,13},{... | collective-permute-start | bytes 1572872 | tf_op jit(solution)/shard_map/ppermute | solution.py:210
  76.7 18.4 %collective-permute-start.9 = (bf16[512,512]{1,0:T(8,128)(2,1)S(1)}, bf16[512,512]{1,0:T(8,128)(2,1)S(1)}, u32[]{:S(2)}, u32[]{:S(2)}) collective-permute-start(bf16[512,512]{1,0:T(8,128)(2,1)S(1)} %space.5.refs_1_), channel_id=1, source_target_pairs={{0,8},{4,12},{8,0},{12,4},{1,9},{5,13},{9,1},{13,5},{2,10},{6,14},... | collective-permute-start | bytes 1572872 | tf_op jit(solution)/shard_map/ppermute | solution.py:206
  78.9 6.0 %collective-permute-start.13 = (bf16[128,1536]{1,0:T(8,128)(2,1)S(1)}, bf16[128,1536]{1,0:T(8,128)(2,1)S(1)}, u32[]{:S(2)}, u32[]{:S(2)}) collective-permute-start(bf16[128,1536]{1,0:T(8,128)(2,1)S(1)} %get-tuple-element.27), channel_id=1, source_target_pairs={{0,4},{4,0},{8,12},{12,8},{1,5},{5,1},{9,13},{13,9},{2,6},{6,2},{1... | collective-permute-start | bytes 1179656 | tf_op jit(solution)/shard_map/ppermute | solution.py:203
  79.1 6.3 %collective-permute-start.12 = (bf16[128,1536]{1,0:T(8,128)(2,1)S(1)}, bf16[128,1536]{1,0:T(8,128)(2,1)S(1)}, u32[]{:S(2)}, u32[]{:S(2)}) collective-permute-start(bf16[128,1536]{1,0:T(8,128)(2,1)S(1)} %get-tuple-element.28), channel_id=1, source_target_pairs={{0,4},{4,0},{8,12},{12,8},{1,5},{5,1},{9,13},{13,9},{2,6},{6,2},{1... | collective-permute-start | bytes 1179656 | tf_op jit(solution)/shard_map/ppermute | solution.py:203
  80.3 5.2 %collective-permute-start.11 = (bf16[128,1536]{1,0:T(8,128)(2,1)S(1)}, bf16[128,1536]{1,0:T(8,128)(2,1)S(1)}, u32[]{:S(2)}, u32[]{:S(2)}) collective-permute-start(bf16[128,1536]{1,0:T(8,128)(2,1)S(1)} %get-tuple-element.29), channel_id=1, source_target_pairs={{0,4},{4,0},{8,12},{12,8},{1,5},{5,1},{9,13},{13,9},{2,6},{6,2},{1... | collective-permute-start | bytes 1179656 | tf_op jit(solution)/shard_map/ppermute | solution.py:203
  84.6 1.7 %collective-permute-start.10 = (bf16[128,1536]{1,0:T(8,128)(2,1)S(1)}, bf16[128,1536]{1,0:T(8,128)(2,1)S(1)}, u32[]{:S(2)}, u32[]{:S(2)}) collective-permute-start(bf16[128,1536]{1,0:T(8,128)(2,1)S(1)} %get-tuple-element.30), channel_id=1, source_target_pairs={{0,4},{4,0},{8,12},{12,8},{1,5},{5,1},{9,13},{13,9},{2,6},{6,2},{1... | collective-permute-start | bytes 1179656 | tf_op jit(solution)/shard_map/ppermute | solution.py:203
  84.9 2.0 %collective-permute-start.24 = (bf16[128,1536]{1,0:T(8,128)(2,1)S(1)}, bf16[128,1536]{1,0:T(8,128)(2,1)S(1)}, u32[]{:S(2)}, u32[]{:S(2)}) collective-permute-start(bf16[128,1536]{1,0:T(8,128)(2,1)S(1)} %get-tuple-element.23), channel_id=1, source_target_pairs={{0,4},{4,0},{8,12},{12,8},{1,5},{5,1},{9,13},{13,9},{2,6},{6,2},{1... | collective-permute-start | bytes 1179656 | tf_op jit(solution)/shard_map/ppermute | solution.py:203
  85.3 2.2 %collective-permute-start.23 = (bf16[128,1536]{1,0:T(8,128)(2,1)S(1)}, bf16[128,1536]{1,0:T(8,128)(2,1)S(1)}, u32[]{:S(2)}, u32[]{:S(2)}) collective-permute-start(bf16[128,1536]{1,0:T(8,128)(2,1)S(1)} %get-tuple-element.24), channel_id=1, source_target_pairs={{0,4},{4,0},{8,12},{12,8},{1,5},{5,1},{9,13},{13,9},{2,6},{6,2},{1... | collective-permute-start | bytes 1179656 | tf_op jit(solution)/shard_map/ppermute | solution.py:203
  85.5 2.6 %collective-permute-start.22 = (bf16[128,1536]{1,0:T(8,128)(2,1)S(1)}, bf16[128,1536]{1,0:T(8,128)(2,1)S(1)}, u32[]{:S(2)}, u32[]{:S(2)}) collective-permute-start(bf16[128,1536]{1,0:T(8,128)(2,1)S(1)} %get-tuple-element.25), channel_id=1, source_target_pairs={{0,4},{4,0},{8,12},{12,8},{1,5},{5,1},{9,13},{13,9},{2,6},{6,2},{1... | collective-permute-start | bytes 1179656 | tf_op jit(solution)/shard_map/ppermute | solution.py:203
  86.4 2.2 %collective-permute-start.21 = (bf16[128,1536]{1,0:T(8,128)(2,1)S(1)}, bf16[128,1536]{1,0:T(8,128)(2,1)S(1)}, u32[]{:S(2)}, u32[]{:S(2)}) collective-permute-start(bf16[128,1536]{1,0:T(8,128)(2,1)S(1)} %get-tuple-element.26), channel_id=1, source_target_pairs={{0,4},{4,0},{8,12},{12,8},{1,5},{5,1},{9,13},{13,9},{2,6},{6,2},{1... | collective-permute-start | bytes 1179656 | tf_op jit(solution)/shard_map/ppermute | solution.py:203
  86.9 8.1 %collective-permute-start.8 = (bf16[512,512]{1,0:T(8,128)(2,1)S(1)}, bf16[512,512]{1,0:T(8,128)(2,1)S(1)}, u32[]{:S(2)}, u32[]{:S(2)}) collective-permute-start(bf16[512,512]{1,0:T(8,128)(2,1)S(1)} %space.5.refs_1_), channel_id=1, source_target_pairs={{0,4},{4,0},{8,12},{12,8},{1,5},{5,1},{9,13},{13,9},{2,6},{6,2},{1... | collective-permute-start | bytes 1572872 | tf_op jit(solution)/shard_map/ppermute | solution.py:203
  95.1 1.9 %collective-permute-start.25 = (bf16[512,512]{1,0:T(8,128)(2,1)S(1)}, bf16[512,512]{1,0:T(8,128)(2,1)S(1)}, u32[]{:S(2)}, u32[]{:S(2)}) collective-permute-start(bf16[512,512]{1,0:T(8,128)(2,1)S(1)} %collective-permute-done.9.refs_3_), channel_id=1, source_target_pairs={{0,4},{4,0},{8,12},{12,8},{1,5},{5,1},{9,13},{13,9},{2,6},{6,2},{1... | collective-permute-start | bytes 1572872 | tf_op jit(solution)/shard_map/ppermute | solution.py:203

commit v4 on v3

v4 whole, which is shorter than its diff:
```python
import functools

import jax
import jax.numpy as jnp
from jax import lax
from jax.experimental import pallas as pl
from jax.experimental.pallas import tpu as pltpu
from jax.sharding import PartitionSpec as P

F32 = jnp.float32
BF16 = jnp.bfloat16
VMEM_BYTES = 24 * 1024 * 1024


def dot(a, b):
    return lax.dot_general(a, b, (((1,), (0,)), ((), ())), preferred_element_type=F32)


def dot_t(a, b):
    return lax.dot_general(a, b, (((1,), (1,)), ((), ())), preferred_element_type=F32)


def params():
    return pltpu.CompilerParams(vmem_limit_bytes=VMEM_BYTES)


BRIEF = pl.CostEstimate(flops=0, bytes_accessed=0, transcendentals=0)


def table_kernel(order, rows, core_ref, row_ref, out_ref):
    first = core_ref[0] == 0
    length = row_ref.shape[1]
    lags = pltpu.roll(jnp.broadcast_to(row_ref[...], (16, length)), 0, 1, stride=1, stride_axis=0)

    def group(g, carry):
        base = g * 16
        whole = pltpu.roll(lags, base, 1)
        for m, (a, b) in enumerate(zip(*order)):
            left = whole[:, a * rows : (a + 1) * rows]
            right = whole[:, b * rows : (b + 1) * rows]
            picked = left if a == b else jnp.where(first, left, right)
            out_ref[pl.ds(pl.multiple_of(base, 16), 16), m * rows : (m + 1) * rows] = picked.astype(BF16)
        return carry

    lax.fori_loop(0, rows // 16, group, 0)


def time_table(time_row, core, order, rows):
    reversed_row = jnp.concatenate([time_row[:1], time_row[1:][::-1]]).astype(F32)[None, :]
    length = time_row.shape[0]
    return pl.pallas_call(
        functools.partial(table_kernel, order, rows),
        out_shape=jax.ShapeDtypeStruct((rows, length), BF16),
        in_specs=[
            pl.BlockSpec(memory_space=pltpu.SMEM),
            pl.BlockSpec(memory_space=pltpu.VMEM),
        ],
        out_specs=pl.BlockSpec(memory_space=pltpu.VMEM),
        compiler_params=params(),
        cost_estimate=BRIEF,
        name="time_table",
    )(core, reversed_row)


ANY = pl.BlockSpec(memory_space=pl.ANY)


def by_columns(name, body, args, rows, start, size, step, width, probe, terms=None, image=None, dtype=BF16):
    vmem = pl.BlockSpec(memory_space=pltpu.VMEM)
    args = list(args) + list(terms or ())
    specs = [vmem] * len(args)
    used = len(args)
    aliases, scratch = {}, []
    if image is None:
        out_shape = jax.ShapeDtypeStruct((rows, size), dtype)
        out_spec = vmem
    else:
        if not isinstance(image, jax.ShapeDtypeStruct):
            aliases = {used: 0}
            args.append(image)
            specs.append(ANY)
        out_shape = jax.ShapeDtypeStruct(image.shape, image.dtype)
        out_spec = ANY
        scratch = [
            pltpu.VMEM((size // step, rows, step), image.dtype),
            pltpu.SemaphoreType.DMA((size // step,)),
        ]

    def kernel(*refs):
        inputs, out = refs[:used], refs[len(args)]
        copies = []
        for index in range(size // step):
            column = start + index * step
            place, site = probe + column // width, column % width
            total = body(inputs, index * step, column // width, site)
            if terms is not None:
                noise, field = inputs[used - 2 :]
                total += noise[:, site : site + step] * field[place, :, site : site + step].astype(F32)
            if image is None:
                out[:, index * step : (index + 1) * step] = total.astype(dtype)
            else:
                buffer, sems = refs[len(args) + 1 :]
                buffer[index] = total.astype(image.dtype)
                copy = pltpu.make_async_copy(
                    buffer.at[index], out.at[place, :, pl.ds(site, step)], sems.at[index]
                )
                copy.start()
                copies.append(copy)
        for copy in copies:
            copy.wait()

    return pl.pallas_call(
        kernel,
        out_shape=out_shape,
        in_specs=specs,
        out_specs=out_spec,
        scratch_shapes=scratch,
        input_output_aliases=aliases,
        compiler_params=params(),
        cost_estimate=BRIEF,
        name=name,
    )(*args)


def space(low, mid, high, band, base, start, size, width, **where):
    half, step = width // 2, min(256, size)

    def body(refs, offset, probe, site):
        low, mid, high, band = refs[:4]
        weights = band.at[site : site + step]
        total = dot_t(mid[base + probe], weights[:, half : half + width])
        total += dot_t(low[probe], weights[:, :half])
        total += dot_t(high[probe], weights[:, half + width :])
        return total

    where = dict(dict(probe=0), **where)
    return by_columns("space", body, [low, mid, high, band], mid.shape[1], start, size, step, width, **where)


def mix(table, blocks, width, start=0, begun=None, step=512, **where):
    rows = table.shape[0]
    flat = [piece for block in blocks.values() for piece in block]
    size = flat[0].shape[1]
    step = min(step, size)

    def body(refs, offset, probe, site):
        columns = slice(offset, offset + step)
        taken = 1
        total = None
        for m, block in blocks.items():
            parts = [ref[:, columns] for ref in refs[taken : taken + len(block)]]
            taken += len(block)
            term = dot(refs[0][:, m * rows : (m + 1) * rows], jnp.concatenate(parts, axis=0))
            total = term if total is None else total + term
        return total if begun is None else total + refs[taken][:, columns]

    args = [table] + flat + ([] if begun is None else [begun])
    where = dict(dict(probe=0), **where)
    return by_columns("mix", body, args, rows, start, size, step, width, **where)


def after(value, *others):
    return lax.optimization_barrier((value,) + others)[0]


def on_device(field, time_row, sp_weight, offsets, noise):
    probes, rows, width = field.shape
    half = width // 2
    count = lax.axis_size("slot")
    sites = lax.axis_size("site")
    core = (lax.axis_index("slot") % 2).astype(jnp.int32).reshape(1)
    noise = noise[None, :]

    swap = [(i, i ^ 1) for i in range(count)]
    shifts = range(2, count, 2)
    up = [(i, i + 1) for i in range(sites - 1)]
    down = [(i + 1, i) for i in range(sites - 1)]

    def to_core(block, pieces=1):
        return [lax.ppermute(part, "slot", swap) for part in jnp.split(block, pieces, axis=0)]

    def to_chips(block):
        return [lax.ppermute(block, "slot", [(i, (i + s) % count) for i in range(count)]) for s in shifts]

    def halo(block):
        return (
            lax.ppermute(block[:, :, width - half :], "site", up),
            lax.ppermute(block[:, :, :half], "site", down),
        )

    order = ([0, 1], [0, count - 1])
    for s in shifts:
        order[0].extend([(-s) % count, (1 - s) % count])
        order[1].extend([(-s) % count, (-1 - s) % count])

    def arrived(far, pieces, *others):
        blocks = {}
        for k, got in enumerate(far):
            got = after(got, *others)
            blocks[2 + 2 * k] = [got]
            blocks[3 + 2 * k] = to_core(got, pieces)
        return blocks

    def here(own, near):
        return {0: [own], 1: near}

    firsts = probes // 2
    own, far = [], []
    rest = field
    for p in range(firsts):
        own.append(rest[p])
        far.append(to_chips(own[p]))
        rest = after(field, own[p])
        if p == 0:
            low, high = halo(rest[firsts:])

    table = time_table(time_row, core, order, rows)
    col = jnp.arange(sp_weight.shape[1], dtype=jnp.int32)
    mask = (col[None, :] >= offsets[:, None]) & (col[None, :] < offsets[:, None] + width)
    band = jnp.where(mask, sp_weight, jnp.zeros_like(sp_weight))

    near = [to_core(block) for block in own]
    columns = (probes - firsts) * width
    cut = columns - half
    terms = (noise, field)
    image = jax.ShapeDtypeStruct(field.shape, field.dtype)

    blocks = here(own[0], near[0]) | arrived(far[0], 2, table, band)
    mixed = [mix(table, blocks, width)]
    long = space(low, field, high, after(band, mixed[0]), firsts, 0, cut, width)
    far_long = to_chips(long)
    for p in range(1, firsts):
        blocks = here(own[p], near[p]) | arrived(far[p], 2, mixed[-1], long)
        mixed.append(mix(table, blocks, width))

    for p in range(firsts):
        middle = mixed[p][None]
        got_low, got_high = halo(middle)
        image = space(got_low, middle, got_high, band, 0, 0, width, width, probe=p, terms=terms, image=image)
        if p == 0:
            near_long = to_core(after(long, image), 4)
            short = space(low, field, high, after(band, image), firsts, cut, half, width)
            near_short, far_short = to_core(short), to_chips(short)

    at = dict(start=cut, probe=firsts)
    begun = mix(table, here(short, after(near_short, image)), width, terms=terms, dtype=F32, **at)
    blocks = here(long, near_long) | arrived(far_long, 4, begun)
    image = mix(table, blocks, width, probe=firsts, terms=terms, image=image)
    blocks = arrived(far_short, 1, image)
    straight = {m: block for m, block in blocks.items() if m % 2 == 0}
    crossed = {m: block for m, block in blocks.items() if m % 2 == 1}
    begun = mix(table, straight, width, begun=begun, dtype=F32, **at)
    return mix(table, crossed, width, begun=begun, image=image, step=256, **at)


def solution(mesh):
    in_specs = (P("grp", "slot", "site"), P(), P("site", None), P("site"), P("site"))
    out_specs = P("grp", "slot", "site")
    return jax.shard_map(
        on_device, mesh=mesh, in_specs=in_specs, out_specs=out_specs, check_vma=False
    )
```

time: 99.4 us -> 98.8 us (level)
  Pallas kernels: 34.7 us -> 30.9 us
  waiting for transfers between devices: 22.3 us -> 24.9 us
    pallas_call x8 -> x10, Pallas kernels: 31.1 us -> 27.2 us  [by_columns(): pl.pallas_call(kernel, out_shape=out_shape, in_specs=specs, out_specs=out...]
    ppermute x4, waiting for transfers between devices: 10.2 us -> 11.8 us  [to_chips(): lax.ppermute(block, 'slot', [(i, (i + s) % count) for i in range(count)])]
  transfers between devices with their start and end apart: 26 -> 26, of which waited for: 18 -> 17; matrix products, arithmetic and copies ran while one was open for 12% -> 12% of each run, Pallas kernels for 33% -> 30%
where the time goes in v4:
time: 98.8 us; the launch traced here: 98.4 us
  Pallas kernels  30.9 us (31%)
  starting transfers between devices  29 us (29%)
  waiting for transfers between devices  24.9 us (25%)
  local copies, waits for them, and re-layouts  8.41 us (9%)
  other arithmetic  4.72 us (5%)
    pallas_call x10, Pallas kernels, by_columns(): pl.pallas_call(kernel, out_shape=out_shape, in_specs=specs, out_specs=out...  27.2 us
    ppermute x3, starting transfers between devices, halo(): lax.ppermute(block[:, :, width - half:], 'site', up)  15 us
    ppermute x4, waiting for transfers between devices, to_chips(): lax.ppermute(block, 'slot', [(i, (i + s) % count) for i in range(count)])  11.8 us
    ppermute x4, starting transfers between devices, to_chips(): lax.ppermute(block, 'slot', [(i, (i + s) % count) for i in range(count)])  6.99 us
    ppermute x16, waiting for transfers between devices, to_core(): lax.ppermute(part, 'slot', swap)  6.12 us
    select_n x1, other arithmetic, on_device(): band = jnp.where(mask, sp_weight, jnp.zeros_like(sp_weight))  4.01 us
    ppermute x3, waiting for transfers between devices, halo(): lax.ppermute(block[:, :, width - half:], 'site', up)  3.9 us
    ppermute x3, starting transfers between devices, halo(): lax.ppermute(block[:, :, :half], 'site', down)  3.86 us
  transfers between devices with their start and end apart: 26, of which 17 were waited for; matrix products, arithmetic and copies ran while one was open for 12% of the time, Pallas kernels for 30%

profile of v4, /device:TPU:0, one launch (start us, length us, event | category | flops | bytes accessed | tf_op | source)
XLA Modules:
  0.0 98.4 jit_solution(2734608907785325742)
XLA Ops:
  0.0 1.4 %slice_bitcast_fusion.1.refs_1_ = bf16[512,1024]{1,0:T(8,128)(2,1)S(1)} fusion(bf16[4,512,1024]{2,1,0:T(8,128)(2,1)} %refs_12_.1), kind=kLoop, calls=%fused_computation.5 | loop fusion | bytes 2097152 | tf_op jit(solution)/shard_map/squeeze | solution.py:211
  1.5 3.0 %collective-permute-start.3 = (bf16[512,1024]{1,0:T(8,128)(2,1)S(1)}, bf16[512,1024]{1,0:T(8,128)(2,1)}, u32[]{:S(2)}, u32[]{:S(2)}) collective-permute-start(bf16[512,1024]{1,0:T(8,128)(2,1)S(1)} %slice_bitcast_fusion.1.refs_1_), channel_id=1, source_target_pairs={{0,8},{4,12},{8,0},{12,4},{1,9},{5,13},{9,1},{13,5},{2,10},{6,14},... | collective-permute-start | bytes 3145736 | tf_op jit(solution)/shard_map/ppermute | solution.py:183
  4.5 1.3 %slice_bitcast_fusion.refs_1_ = bf16[512,1024]{1,0:T(8,128)(2,1)S(1)} fusion(bf16[4,512,1024]{2,1,0:T(8,128)(2,1)} %refs_12_.1), kind=kLoop, calls=%fused_computation.4 | loop fusion | bytes 2097152 | tf_op jit(solution)/shard_map/squeeze | solution.py:211
  5.8 0.2 collective-permute-start.16
  5.9 3.0 %fusion.2 = (bf16[2,512,512]{2,1,0:T(8,128)(2,1)}, bf16[2,512,512]{2,1,0:T(8,128)(2,1)}) fusion(bf16[4,512,1024]{2,1,0:T(8,128)(2,1)} %refs_12_.1), kind=kLoop, calls=%fused_computation.8 | loop fusion | bytes 4194304 | tf_op jit(solution)/shard_map/slice | solution.py:188
  9.0 1.3 %collective-permute-start.1 = (bf16[2,512,512]{2,1,0:T(8,128)(2,1)}, bf16[2,512,512]{2,1,0:T(8,128)(2,1)}, u32[]{:S(2)}, u32[]{:S(2)}) collective-permute-start(bf16[2,512,512]{2,1,0:T(8,128)(2,1)} %get-tuple-element.23), channel_id=1, source_target_pairs={{1,0},{2,1},{3,2},{5,4},{6,5},{7,6},{9,8},{10,9},{11,10},{13,12},{... | collective-permute-start | bytes 3145736 | tf_op jit(solution)/shard_map/ppermute | solution.py:188
  10.3 5.5 %collective-permute-start = (bf16[2,512,512]{2,1,0:T(8,128)(2,1)}, bf16[2,512,512]{2,1,0:T(8,128)(2,1)}, u32[]{:S(2)}, u32[]{:S(2)}) collective-permute-start(bf16[2,512,512]{2,1,0:T(8,128)(2,1)} %get-tuple-element.24), channel_id=1, source_target_pairs={{0,1},{1,2},{2,3},{4,5},{5,6},{6,7},{8,9},{9,10},{10,11},{12,13},{... | collective-permute-start | bytes 3145736 | tf_op jit(solution)/shard_map/ppermute | solution.py:187
  15.8 4.0 %fusion.1.refs_3_ = bf16[1024,2048]{1,0:T(8,128)(2,1)} fusion(bf16[1024,2048]{1,0:T(8,128)(2,1)S(1)} %copy-done.3, s32[1024]{0:T(1024)S(1)} %broadcast_add_fusion, s32[1024]{0:T(1024)S(1)} %copy-done.4), kind=kLoop, calls=%fused_computation.3 | loop fusion | flops 8388608 | bytes 8396800 | tf_op jit(solution)/shard_map/jit(_where)/select_n | solution.py:220
  19.8 0.5 slice.33
  20.4 0.1 slice.34
  20.5 0.1 reverse
  20.5 0.1 slice.49
  20.6 0.7 maximum_convert_fusion.row_ref
  21.3 3.6 %time_table.1.refs_0_ = bf16[512,2048]{1,0:T(8,128)(2,1)S(1)} custom-call(s32[1]{0:T(128)} %bitcast.core_ref, f32[1,2048]{1,0:T(1,128)S(1)} %maximum_convert_fusion.row_ref), custom_call_target="tpu_custom_call" | custom-call | tf_op jit(solution)/shard_map/time_table/pallas_call | solution.py:51
  24.9 3.6 %collective-permute-done.3.refs_3_ = bf16[512,1024]{1,0:T(8,128)(2,1)} collective-permute-done((bf16[512,1024]{1,0:T(8,128)(2,1)S(1)}, bf16[512,1024]{1,0:T(8,128)(2,1)}, u32[]{:S(2)}, u32[]{:S(2)}) %collective-permute-start.3) | collective-permute-done | bytes 1048608 | tf_op jit(solution)/shard_map/ppermute | solution.py:183
  28.6 1.4 %fusion.8 = (bf16[256,1024]{1,0:T(8,128)(2,1)S(1)}, bf16[256,1024]{1,0:T(8,128)(2,1)S(1)}) fusion(bf16[512,1024]{1,0:T(8,128)(2,1)} %collective-permute-done.3.refs_3_), kind=kLoop, calls=%fused_computation.14 | loop fusion | bytes 2097152 | tf_op jit(solution)/shard_map/split | solution.py:180
  30.0 0.1 collective-permute-start.5
  30.1 0.5 collective-permute-start.4
  30.6 1.4 %collective-permute-done.5.refs_5_ = bf16[256,1024]{1,0:T(8,128)(2,1)S(1)} collective-permute-done((bf16[256,1024]{1,0:T(8,128)(2,1)S(1)}, bf16[256,1024]{1,0:T(8,128)(2,1)S(1)}, u32[]{:S(2)}, u32[]{:S(2)}) %collective-permute-start.5) | collective-permute-done | bytes 524320 | tf_op jit(solution)/shard_map/ppermute | solution.py:180
  32.0 0.1 collective-permute-start.15
  32.1 0.6 collective-permute-done.4.refs_4_
  32.7 3.9 %mix.6 = bf16[512,1024]{1,0:T(8,128)(2,1)S(1)} custom-call(bf16[512,2048]{1,0:T(8,128)(2,1)S(1)} %time_table.1.refs_0_, bf16[512,1024]{1,0:T(8,128)(2,1)S(1)} %slice_bitcast_fusion.1.refs_1_, bf16[512,1024]{1,0:T(8,128)(2,1)} %collective-permute-done.2.refs_2_, bf16[512,1024]{1,0:T(8,128)(2,1)} %collective-permute-done.3.refs_3_, ...), custom_call_target="tpu_custom_call" | custom-call | tf_op jit(solution)/shard_map/mix/pallas_call | solution.py:112
  36.6 0.1 collective-permute-done.1.refs_2_
  36.7 1.2 %collective-permute-done.refs_0_ = bf16[2,512,512]{2,1,0:T(8,128)(2,1)} collective-permute-done((bf16[2,512,512]{2,1,0:T(8,128)(2,1)}, bf16[2,512,512]{2,1,0:T(8,128)(2,1)}, u32[]{:S(2)}, u32[]{:S(2)}) %collective-permute-start) | collective-permute-done | bytes 1048608 | tf_op jit(solution)/shard_map/ppermute | solution.py:187
  37.9 5.0 %space.6.refs_1_ = bf16[512,1536]{1,0:T(8,128)(2,1)S(1)} custom-call(bf16[2,512,512]{2,1,0:T(8,128)(2,1)} %collective-permute-done.refs_0_, bf16[4,512,1024]{2,1,0:T(8,128)(2,1)S(1)} %copy-done, bf16[2,512,512]{2,1,0:T(8,128)(2,1)} %collective-permute-done.1.refs_2_, bf16[1024,2048]{1,0:T(8,128)(2,1)S(1)} %copy-done.1), custom_call_target="tpu_custom_call" | custom-call | tf_op jit(solution)/shard_map/space/pallas_call | solution.py:112
  43.0 1.7 %collective-permute-start.13 = (bf16[512,1536]{1,0:T(8,128)(2,1)S(1)}, bf16[512,1536]{1,0:T(8,128)(2,1)S(1)}, u32[]{:S(2)}, u32[]{:S(2)}) collective-permute-start(bf16[512,1536]{1,0:T(8,128)(2,1)S(1)} %space.6.refs_1_), channel_id=1, source_target_pairs={{0,8},{4,12},{8,0},{12,4},{1,9},{5,13},{9,1},{13,5},{2,10},{6,14},... | collective-permute-start | bytes 4718600 | tf_op jit(solution)/shard_map/ppermute | solution.py:183
  44.7 6.2 %collective-permute-done.16.refs_3_ = bf16[512,1024]{1,0:T(8,128)(2,1)S(1)} collective-permute-done((bf16[512,1024]{1,0:T(8,128)(2,1)S(1)}, bf16[512,1024]{1,0:T(8,128)(2,1)S(1)}, u32[]{:S(2)}, u32[]{:S(2)}) %collective-permute-start.16) | collective-permute-done | bytes 1048608 | tf_op jit(solution)/shard_map/ppermute | solution.py:183
  50.9 0.1 fusion.6
  51.0 0.1 collective-permute-start.18
  51.1 0.5 collective-permute-start.17
  51.7 1.3 %collective-permute-start.7 = (bf16[1,512,512]{2,1,0:T(8,128)(2,1)S(1)}, bf16[1,512,512]{2,1,0:T(8,128)(2,1)S(1)}, u32[]{:S(2)}, u32[]{:S(2)}) collective-permute-start(bf16[1,512,512]{2,1,0:T(8,128)(2,1)S(1)} %get-tuple-element.37), channel_id=1, source_target_pairs={{1,0},{2,1},{3,2},{5,4},{6,5},{7,6},{9,8},{10,9},{11,10},{13,12},{... | collective-permute-start | bytes 1572872 | tf_op jit(solution)/shard_map/ppermute | solution.py:188
  53.0 4.7 %collective-permute-start.6 = (bf16[1,512,512]{2,1,0:T(8,128)(2,1)S(1)}, bf16[1,512,512]{2,1,0:T(8,128)(2,1)S(1)}, u32[]{:S(2)}, u32[]{:S(2)}) collective-permute-start(bf16[1,512,512]{2,1,0:T(8,128)(2,1)S(1)} %get-tuple-element.38), channel_id=1, source_target_pairs={{0,1},{1,2},{2,3},{4,5},{5,6},{6,7},{8,9},{9,10},{10,11},{12,13},{... | collective-permute-start | bytes 1572872 | tf_op jit(solution)/shard_map/ppermute | solution.py:187
  57.7 2.4 %mix.7 = bf16[512,1024]{1,0:T(8,128)(2,1)S(1)} custom-call(bf16[512,2048]{1,0:T(8,128)(2,1)S(1)} %time_table.1.refs_0_, bf16[512,1024]{1,0:T(8,128)(2,1)S(1)} %slice_bitcast_fusion.refs_1_, bf16[512,1024]{1,0:T(8,128)(2,1)S(1)} %collective-permute-done.15.refs_2_, bf16[512,1024]{1,0:T(8,128)(2,1)S(1)} %collective-permute-done.16.refs_3_, ...), custom_call_target="tpu_custom_call" | custom-call | tf_op jit(solution)/shard_map/mix/pallas_call | solution.py:112
  60.1 0.1 fusion.5
  60.1 1.3 %collective-permute-start.20 = (bf16[1,512,512]{2,1,0:T(8,128)(2,1)S(1)}, bf16[1,512,512]{2,1,0:T(8,128)(2,1)S(1)}, u32[]{:S(2)}, u32[]{:S(2)}) collective-permute-start(bf16[1,512,512]{2,1,0:T(8,128)(2,1)S(1)} %get-tuple-element.33), channel_id=1, source_target_pairs={{1,0},{2,1},{3,2},{5,4},{6,5},{7,6},{9,8},{10,9},{11,10},{13,12},{... | collective-permute-start | bytes 1572872 | tf_op jit(solution)/shard_map/ppermute | solution.py:188
  61.4 4.8 %collective-permute-start.19 = (bf16[1,512,512]{2,1,0:T(8,128)(2,1)S(1)}, bf16[1,512,512]{2,1,0:T(8,128)(2,1)S(1)}, u32[]{:S(2)}, u32[]{:S(2)}) collective-permute-start(bf16[1,512,512]{2,1,0:T(8,128)(2,1)S(1)} %get-tuple-element.34), channel_id=1, source_target_pairs={{0,1},{1,2},{2,3},{4,5},{5,6},{6,7},{8,9},{9,10},{10,11},{12,13},{... | collective-permute-start | bytes 1572872 | tf_op jit(solution)/shard_map/ppermute | solution.py:187
  66.2 2.2 %collective-permute-done.7.refs_2_ = bf16[1,512,512]{2,1,0:T(8,128)(2,1)S(1)} collective-permute-done((bf16[1,512,512]{2,1,0:T(8,128)(2,1)S(1)}, bf16[1,512,512]{2,1,0:T(8,128)(2,1)S(1)}, u32[]{:S(2)}, u32[]{:S(2)}) %collective-permute-start.7) | collective-permute-done | bytes 524320 | tf_op jit(solution)/shard_map/ppermute | solution.py:188
  68.4 1.5 %collective-permute-done.6.refs_0_ = bf16[1,512,512]{2,1,0:T(8,128)(2,1)S(1)} collective-permute-done((bf16[1,512,512]{2,1,0:T(8,128)(2,1)S(1)}, bf16[1,512,512]{2,1,0:T(8,128)(2,1)S(1)}, u32[]{:S(2)}, u32[]{:S(2)}) %collective-permute-start.6) | collective-permute-done | bytes 524320 | tf_op jit(solution)/shard_map/ppermute | solution.py:187
  69.9 3.3 %space.4.refs_6_ = bf16[4,512,1024]{2,1,0:T(8,128)(2,1)} custom-call(bf16[1,512,512]{2,1,0:T(8,128)(2,1)S(1)} %collective-permute-done.6.refs_0_, bf16[1,512,1024]{2,1,0:T(8,128)(2,1)S(1)} %bitcast.13, bf16[1,512,512]{2,1,0:T(8,128)(2,1)S(1)} %collective-permute-done.7.refs_2_, bf16[1024,2048]{1,0:T(8,128)(2,1)S(1)} %copy-done.1, f32[1,1024]{1,0:T(1,128)S(1)} %bitcast.14, ...), custom_call_target="tpu_custom_call" | custom-call | tf_op jit(solution)/shard_map/space/pallas_call | solution.py:112
  73.2 2.8 %space.5.refs_1_ = bf16[512,512]{1,0:T(8,128)(2,1)S(1)} custom-call(bf16[2,512,512]{2,1,0:T(8,128)(2,1)} %collective-permute-done.refs_0_, bf16[4,512,1024]{2,1,0:T(8,128)(2,1)S(1)} %copy-done, bf16[2,512,512]{2,1,0:T(8,128)(2,1)} %collective-permute-done.1.refs_2_, bf16[1024,2048]{1,0:T(8,128)(2,1)S(1)} %copy-done.1), custom_call_target="tpu_custom_call" | custom-call | tf_op jit(solution)/shard_map/space/pallas_call | solution.py:112
  76.0 0.1 collective-permute-start.14
  76.1 2.1 %collective-permute-start.8 = (bf16[512,512]{1,0:T(8,128)(2,1)S(1)}, bf16[512,512]{1,0:T(8,128)(2,1)S(1)}, u32[]{:S(2)}, u32[]{:S(2)}) collective-permute-start(bf16[512,512]{1,0:T(8,128)(2,1)S(1)} %space.5.refs_1_), channel_id=1, source_target_pairs={{0,8},{4,12},{8,0},{12,4},{1,9},{5,13},{9,1},{13,5},{2,10},{6,14},... | collective-permute-start | bytes 1572872 | tf_op jit(solution)/shard_map/ppermute | solution.py:183
  78.2 0.1 fusion.4
  78.3 0.8 collective-permute-done.20.refs_2_
  79.1 1.2 %collective-permute-done.19.refs_0_ = bf16[1,512,512]{2,1,0:T(8,128)(2,1)S(1)} collective-permute-done((bf16[1,512,512]{2,1,0:T(8,128)(2,1)S(1)}, bf16[1,512,512]{2,1,0:T(8,128)(2,1)S(1)}, u32[]{:S(2)}, u32[]{:S(2)}) %collective-permute-start.19) | collective-permute-done | bytes 524320 | tf_op jit(solution)/shard_map/ppermute | solution.py:187
  80.3 3.2 %space.7.refs_13_ = bf16[4,512,1024]{2,1,0:T(8,128)(2,1)} custom-call(bf16[1,512,512]{2,1,0:T(8,128)(2,1)S(1)} %collective-permute-done.19.refs_0_, bf16[1,512,1024]{2,1,0:T(8,128)(2,1)S(1)} %bitcast.11, bf16[1,512,512]{2,1,0:T(8,128)(2,1)S(1)} %collective-permute-done.20.refs_2_, bf16[1024,2048]{1,0:T(8,128)(2,1)S(1)} %copy-done.1, ...), custom_call_target="tpu_custom_call", output_to_operand_aliasing={{}: (6, {})} | custom-call | tf_op jit(solution)/shard_map/space/pallas_call | solution.py:112
  83.5 0.6 collective-permute-start.10
  84.1 0.7 mix.8.refs_2_
  84.8 0.1 collective-permute-start.9
  84.9 0.1 fusion.3
  85.0 0.6 collective-permute-start.24
  85.6 0.1 collective-permute-start.23
  85.7 0.4 collective-permute-start.22
  86.1 0.5 collective-permute-done.9.refs_2_
  86.6 0.1 collective-permute-start.21
  86.8 0.4 collective-permute-done.24.refs_10_
  87.2 0.6 collective-permute-done.23.refs_9_
  87.8 0.6 collective-permute-done.22.refs_8_
  88.3 0.6 collective-permute-done.21.refs_7_
  88.9 4.2 %mix.9.refs_3_ = bf16[4,512,1024]{2,1,0:T(8,128)(2,1)} custom-call(bf16[512,2048]{1,0:T(8,128)(2,1)S(1)} %time_table.1.refs_0_, bf16[512,1536]{1,0:T(8,128)(2,1)S(1)} %space.6.refs_1_, bf16[128,1536]{1,0:T(8,128)(2,1)S(1)} %collective-permute-done.9.refs_2_, bf16[128,1536]{1,0:T(8,128)(2,1)S(1)} %collective-permute-done.10.refs_3_, ...), custom_call_target="tpu_custom_call", output_to_operand_aliasing={{}: (13, {})} | custom-call | tf_op jit(solution)/shard_map/mix/pallas_call | solution.py:112
  93.1 1.9 %collective-permute-done.8.refs_1_ = bf16[512,512]{1,0:T(8,128)(2,1)S(1)} collective-permute-done((bf16[512,512]{1,0:T(8,128)(2,1)S(1)}, bf16[512,512]{1,0:T(8,128)(2,1)S(1)}, u32[]{:S(2)}, u32[]{:S(2)}) %collective-permute-start.8) | collective-permute-done | bytes 524320 | tf_op jit(solution)/shard_map/ppermute | solution.py:183
  95.1 0.4 mix.10.refs_2_
  95.5 1.5 %collective-permute-done.25.refs_1_ = bf16[512,512]{1,0:T(8,128)(2,1)S(1)} collective-permute-done((bf16[512,512]{1,0:T(8,128)(2,1)S(1)}, bf16[512,512]{1,0:T(8,128)(2,1)S(1)}, u32[]{:S(2)}, u32[]{:S(2)}) %collective-permute-start.25) | collective-permute-done | bytes 524320 | tf_op jit(solution)/shard_map/ppermute | solution.py:180
  97.0 1.2 %mix.11 = bf16[4,512,1024]{2,1,0:T(8,128)(2,1)} custom-call(bf16[512,2048]{1,0:T(8,128)(2,1)S(1)} %time_table.1.refs_0_, bf16[512,512]{1,0:T(8,128)(2,1)S(1)} %collective-permute-done.25.refs_1_, f32[512,512]{1,0:T(8,128)S(1)} %mix.10.refs_2_, bf16[4,512,1024]{2,1,0:T(8,128)(2,1)} %mix.9.refs_3_), custom_call_target="tpu_custom_call", output_to_operand_aliasing={{}: (3, {})} | custom-call | tf_op jit(solution)/shard_map/mix/pallas_call | solution.py:112
  (28 shorter events, 0.1 us)
Async XLA Ops:
  0.0 15.8 %copy-start.4 = (s32[1024]{0:T(1024)S(1)}, s32[1024]{0:T(1024)}, u32[]{:S(2)}) copy-start(s32[1024]{0:T(1024)} %param.8) | copy-start | bytes 12292
  0.0 15.8 %copy-start.3 = (bf16[1024,2048]{1,0:T(8,128)(2,1)S(1)}, bf16[1024,2048]{1,0:T(8,128)(2,1)}, u32[]{:S(2)}) copy-start(bf16[1024,2048]{1,0:T(8,128)(2,1)} %param.7) | copy-start | bytes 12582916
  1.5 27.1 %collective-permute-start.3 = (bf16[512,1024]{1,0:T(8,128)(2,1)S(1)}, bf16[512,1024]{1,0:T(8,128)(2,1)}, u32[]{:S(2)}, u32[]{:S(2)}) collective-permute-start(bf16[512,1024]{1,0:T(8,128)(2,1)S(1)} %slice_bitcast_fusion.1.refs_1_), channel_id=1, source_target_pairs={{0,8},{4,12},{8,0},{12,4},{1,9},{5,13},{9,1},{13,5},{2,10},{6,14},... | collective-permute-start | bytes 3145736 | tf_op jit(solution)/shard_map/ppermute | solution.py:183
  4.5 25.6 %collective-permute-start.2 = (bf16[512,1024]{1,0:T(8,128)(2,1)S(1)}, bf16[512,1024]{1,0:T(8,128)(2,1)}, u32[]{:S(2)}, u32[]{:S(2)}) collective-permute-start(bf16[512,1024]{1,0:T(8,128)(2,1)S(1)} %slice_bitcast_fusion.1.refs_1_), channel_id=1, source_target_pairs={{0,4},{4,0},{8,12},{12,8},{1,5},{5,1},{9,13},{13,9},{2,6},{6,2},{1... | collective-permute-start | bytes 3145736 | tf_op jit(solution)/shard_map/ppermute | solution.py:180
  5.8 45.2 %collective-permute-start.16 = (bf16[512,1024]{1,0:T(8,128)(2,1)S(1)}, bf16[512,1024]{1,0:T(8,128)(2,1)S(1)}, u32[]{:S(2)}, u32[]{:S(2)}) collective-permute-start(bf16[512,1024]{1,0:T(8,128)(2,1)S(1)} %slice_bitcast_fusion.refs_1_), channel_id=1, source_target_pairs={{0,8},{4,12},{8,0},{12,4},{1,9},{5,13},{9,1},{13,5},{2,10},{6,14},... | collective-permute-start | bytes 3145736 | tf_op jit(solution)/shard_map/ppermute | solution.py:183
  9.0 27.7 %collective-permute-start.1 = (bf16[2,512,512]{2,1,0:T(8,128)(2,1)}, bf16[2,512,512]{2,1,0:T(8,128)(2,1)}, u32[]{:S(2)}, u32[]{:S(2)}) collective-permute-start(bf16[2,512,512]{2,1,0:T(8,128)(2,1)} %get-tuple-element.23), channel_id=1, source_target_pairs={{1,0},{2,1},{3,2},{5,4},{6,5},{7,6},{9,8},{10,9},{11,10},{13,12},{... | collective-permute-start | bytes 3145736 | tf_op jit(solution)/shard_map/ppermute | solution.py:188
  10.3 27.6 %collective-permute-start = (bf16[2,512,512]{2,1,0:T(8,128)(2,1)}, bf16[2,512,512]{2,1,0:T(8,128)(2,1)}, u32[]{:S(2)}, u32[]{:S(2)}) collective-permute-start(bf16[2,512,512]{2,1,0:T(8,128)(2,1)} %get-tuple-element.24), channel_id=1, source_target_pairs={{0,1},{1,2},{2,3},{4,5},{5,6},{6,7},{8,9},{9,10},{10,11},{12,13},{... | collective-permute-start | bytes 3145736 | tf_op jit(solution)/shard_map/ppermute | solution.py:187
  15.8 4.0 %copy-start.5 = (bf16[2048]{0:T(1024)(128)(2,1)S(1)}, bf16[2048]{0:T(1024)(128)(2,1)}, u32[]{:S(2)}) copy-start(bf16[2048]{0:T(1024)(128)(2,1)} %param.6) | copy-start | bytes 12292
  28.6 9.3 %copy-start.1 = (bf16[1024,2048]{1,0:T(8,128)(2,1)S(1)}, bf16[1024,2048]{1,0:T(8,128)(2,1)}, u32[]{:S(2)}) copy-start(bf16[1024,2048]{1,0:T(8,128)(2,1)} %fusion.1.refs_3_) | copy-start | bytes 12582916
  30.0 7.9 %copy-start = (bf16[4,512,1024]{2,1,0:T(8,128)(2,1)S(1)}, bf16[4,512,1024]{2,1,0:T(8,128)(2,1)}, u32[]{:S(2)}) copy-start(bf16[4,512,1024]{2,1,0:T(8,128)(2,1)} %refs_12_.1) | copy-start | bytes 12582916
  30.0 2.0 %collective-permute-start.5 = (bf16[256,1024]{1,0:T(8,128)(2,1)S(1)}, bf16[256,1024]{1,0:T(8,128)(2,1)S(1)}, u32[]{:S(2)}, u32[]{:S(2)}) collective-permute-start(bf16[256,1024]{1,0:T(8,128)(2,1)S(1)} %get-tuple-element.39), channel_id=1, source_target_pairs={{0,4},{4,0},{8,12},{12,8},{1,5},{5,1},{9,13},{13,9},{2,6},{6,2},{1... | collective-permute-start | bytes 1572872 | tf_op jit(solution)/shard_map/ppermute | solution.py:180
  30.1 2.6 %collective-permute-start.4 = (bf16[256,1024]{1,0:T(8,128)(2,1)S(1)}, bf16[256,1024]{1,0:T(8,128)(2,1)S(1)}, u32[]{:S(2)}, u32[]{:S(2)}) collective-permute-start(bf16[256,1024]{1,0:T(8,128)(2,1)S(1)} %get-tuple-element.40), channel_id=1, source_target_pairs={{0,4},{4,0},{8,12},{12,8},{1,5},{5,1},{9,13},{13,9},{2,6},{6,2},{1... | collective-permute-start | bytes 1572872 | tf_op jit(solution)/shard_map/ppermute | solution.py:180
  32.0 21.0 %collective-permute-start.15 = (bf16[512,1024]{1,0:T(8,128)(2,1)S(1)}, bf16[512,1024]{1,0:T(8,128)(2,1)S(1)}, u32[]{:S(2)}, u32[]{:S(2)}) collective-permute-start(bf16[512,1024]{1,0:T(8,128)(2,1)S(1)} %slice_bitcast_fusion.refs_1_), channel_id=1, source_target_pairs={{0,4},{4,0},{8,12},{12,8},{1,5},{5,1},{9,13},{13,9},{2,6},{6,2},{1... | collective-permute-start | bytes 3145736 | tf_op jit(solution)/shard_map/ppermute | solution.py:180
  43.0 41.9 %collective-permute-start.13 = (bf16[512,1536]{1,0:T(8,128)(2,1)S(1)}, bf16[512,1536]{1,0:T(8,128)(2,1)S(1)}, u32[]{:S(2)}, u32[]{:S(2)}) collective-permute-start(bf16[512,1536]{1,0:T(8,128)(2,1)S(1)} %space.6.refs_1_), channel_id=1, source_target_pairs={{0,8},{4,12},{8,0},{12,4},{1,9},{5,13},{9,1},{13,5},{2,10},{6,14},... | collective-permute-start | bytes 4718600 | tf_op jit(solution)/shard_map/ppermute | solution.py:183
  51.0 6.7 %collective-permute-start.18 = (bf16[256,1024]{1,0:T(8,128)(2,1)S(1)}, bf16[256,1024]{1,0:T(8,128)(2,1)S(1)}, u32[]{:S(2)}, u32[]{:S(2)}) collective-permute-start(bf16[256,1024]{1,0:T(8,128)(2,1)S(1)} %get-tuple-element.35), channel_id=1, source_target_pairs={{0,4},{4,0},{8,12},{12,8},{1,5},{5,1},{9,13},{13,9},{2,6},{6,2},{1... | collective-permute-start | bytes 1572872 | tf_op jit(solution)/shard_map/ppermute | solution.py:180
  51.1 6.6 %collective-permute-start.17 = (bf16[256,1024]{1,0:T(8,128)(2,1)S(1)}, bf16[256,1024]{1,0:T(8,128)(2,1)S(1)}, u32[]{:S(2)}, u32[]{:S(2)}) collective-permute-start(bf16[256,1024]{1,0:T(8,128)(2,1)S(1)} %get-tuple-element.36), channel_id=1, source_target_pairs={{0,4},{4,0},{8,12},{12,8},{1,5},{5,1},{9,13},{13,9},{2,6},{6,2},{1... | collective-permute-start | bytes 1572872 | tf_op jit(solution)/shard_map/ppermute | solution.py:180
  51.7 16.7 %collective-permute-start.7 = (bf16[1,512,512]{2,1,0:T(8,128)(2,1)S(1)}, bf16[1,512,512]{2,1,0:T(8,128)(2,1)S(1)}, u32[]{:S(2)}, u32[]{:S(2)}) collective-permute-start(bf16[1,512,512]{2,1,0:T(8,128)(2,1)S(1)} %get-tuple-element.37), channel_id=1, source_target_pairs={{1,0},{2,1},{3,2},{5,4},{6,5},{7,6},{9,8},{10,9},{11,10},{13,12},{... | collective-permute-start | bytes 1572872 | tf_op jit(solution)/shard_map/ppermute | solution.py:188
  53.0 16.9 %copy-start.2 = (f32[1024]{0:T(1024)S(1)}, f32[1024]{0:T(1024)}, u32[]{:S(2)}) copy-start(f32[1024]{0:T(1024)} %param.9) | copy-start | bytes 12292
  53.0 16.9 %collective-permute-start.6 = (bf16[1,512,512]{2,1,0:T(8,128)(2,1)S(1)}, bf16[1,512,512]{2,1,0:T(8,128)(2,1)S(1)}, u32[]{:S(2)}, u32[]{:S(2)}) collective-permute-start(bf16[1,512,512]{2,1,0:T(8,128)(2,1)S(1)} %get-tuple-element.38), channel_id=1, source_target_pairs={{0,1},{1,2},{2,3},{4,5},{5,6},{6,7},{8,9},{9,10},{10,11},{12,13},{... | collective-permute-start | bytes 1572872 | tf_op jit(solution)/shard_map/ppermute | solution.py:187
  60.1 18.9 %collective-permute-start.20 = (bf16[1,512,512]{2,1,0:T(8,128)(2,1)S(1)}, bf16[1,512,512]{2,1,0:T(8,128)(2,1)S(1)}, u32[]{:S(2)}, u32[]{:S(2)}) collective-permute-start(bf16[1,512,512]{2,1,0:T(8,128)(2,1)S(1)} %get-tuple-element.33), channel_id=1, source_target_pairs={{1,0},{2,1},{3,2},{5,4},{6,5},{7,6},{9,8},{10,9},{11,10},{13,12},{... | collective-permute-start | bytes 1572872 | tf_op jit(solution)/shard_map/ppermute | solution.py:188
  61.4 18.8 %collective-permute-start.19 = (bf16[1,512,512]{2,1,0:T(8,128)(2,1)S(1)}, bf16[1,512,512]{2,1,0:T(8,128)(2,1)S(1)}, u32[]{:S(2)}, u32[]{:S(2)}) collective-permute-start(bf16[1,512,512]{2,1,0:T(8,128)(2,1)S(1)} %get-tuple-element.34), channel_id=1, source_target_pairs={{0,1},{1,2},{2,3},{4,5},{5,6},{6,7},{8,9},{9,10},{10,11},{12,13},{... | collective-permute-start | bytes 1572872 | tf_op jit(solution)/shard_map/ppermute | solution.py:187
  76.0 7.5 %collective-permute-start.14 = (bf16[512,512]{1,0:T(8,128)(2,1)S(1)}, bf16[512,512]{1,0:T(8,128)(2,1)S(1)}, u32[]{:S(2)}, u32[]{:S(2)}) collective-permute-start(bf16[512,512]{1,0:T(8,128)(2,1)S(1)} %space.5.refs_1_), channel_id=1, source_target_pairs={{0,4},{4,0},{8,12},{12,8},{1,5},{5,1},{9,13},{13,9},{2,6},{6,2},{1... | collective-permute-start | bytes 1572872 | tf_op jit(solution)/shard_map/ppermute | solution.py:180
  76.1 18.9 %collective-permute-start.8 = (bf16[512,512]{1,0:T(8,128)(2,1)S(1)}, bf16[512,512]{1,0:T(8,128)(2,1)S(1)}, u32[]{:S(2)}, u32[]{:S(2)}) collective-permute-start(bf16[512,512]{1,0:T(8,128)(2,1)S(1)} %space.5.refs_1_), channel_id=1, source_target_pairs={{0,8},{4,12},{8,0},{12,4},{1,9},{5,13},{9,1},{13,5},{2,10},{6,14},... | collective-permute-start | bytes 1572872 | tf_op jit(solution)/shard_map/ppermute | solution.py:183
  79.1 6.0 %collective-permute-start.12 = (bf16[128,1536]{1,0:T(8,128)(2,1)S(1)}, bf16[128,1536]{1,0:T(8,128)(2,1)S(1)}, u32[]{:S(2)}, u32[]{:S(2)}) collective-permute-start(bf16[128,1536]{1,0:T(8,128)(2,1)S(1)} %get-tuple-element.29), channel_id=1, source_target_pairs={{0,4},{4,0},{8,12},{12,8},{1,5},{5,1},{9,13},{13,9},{2,6},{6,2},{1... | collective-permute-start | bytes 1179656 | tf_op jit(solution)/shard_map/ppermute | solution.py:180
  80.3 5.3 %collective-permute-start.11 = (bf16[128,1536]{1,0:T(8,128)(2,1)S(1)}, bf16[128,1536]{1,0:T(8,128)(2,1)S(1)}, u32[]{:S(2)}, u32[]{:S(2)}) collective-permute-start(bf16[128,1536]{1,0:T(8,128)(2,1)S(1)} %get-tuple-element.30), channel_id=1, source_target_pairs={{0,4},{4,0},{8,12},{12,8},{1,5},{5,1},{9,13},{13,9},{2,6},{6,2},{1... | collective-permute-start | bytes 1179656 | tf_op jit(solution)/shard_map/ppermute | solution.py:180
  83.5 2.1 %collective-permute-start.10 = (bf16[128,1536]{1,0:T(8,128)(2,1)S(1)}, bf16[128,1536]{1,0:T(8,128)(2,1)S(1)}, u32[]{:S(2)}, u32[]{:S(2)}) collective-permute-start(bf16[128,1536]{1,0:T(8,128)(2,1)S(1)} %get-tuple-element.31), channel_id=1, source_target_pairs={{0,4},{4,0},{8,12},{12,8},{1,5},{5,1},{9,13},{13,9},{2,6},{6,2},{1... | collective-permute-start | bytes 1179656 | tf_op jit(solution)/shard_map/ppermute | solution.py:180
  84.8 1.8 %collective-permute-start.9 = (bf16[128,1536]{1,0:T(8,128)(2,1)S(1)}, bf16[128,1536]{1,0:T(8,128)(2,1)S(1)}, u32[]{:S(2)}, u32[]{:S(2)}) collective-permute-start(bf16[128,1536]{1,0:T(8,128)(2,1)S(1)} %get-tuple-element.32), channel_id=1, source_target_pairs={{0,4},{4,0},{8,12},{12,8},{1,5},{5,1},{9,13},{13,9},{2,6},{6,2},{1... | collective-permute-start | bytes 1179656 | tf_op jit(solution)/shard_map/ppermute | solution.py:180
  85.0 2.1 %collective-permute-start.24 = (bf16[128,1536]{1,0:T(8,128)(2,1)S(1)}, bf16[128,1536]{1,0:T(8,128)(2,1)S(1)}, u32[]{:S(2)}, u32[]{:S(2)}) collective-permute-start(bf16[128,1536]{1,0:T(8,128)(2,1)S(1)} %get-tuple-element.25), channel_id=1, source_target_pairs={{0,4},{4,0},{8,12},{12,8},{1,5},{5,1},{9,13},{13,9},{2,6},{6,2},{1... | collective-permute-start | bytes 1179656 | tf_op jit(solution)/shard_map/ppermute | solution.py:180
  85.6 2.2 %collective-permute-start.23 = (bf16[128,1536]{1,0:T(8,128)(2,1)S(1)}, bf16[128,1536]{1,0:T(8,128)(2,1)S(1)}, u32[]{:S(2)}, u32[]{:S(2)}) collective-permute-start(bf16[128,1536]{1,0:T(8,128)(2,1)S(1)} %get-tuple-element.26), channel_id=1, source_target_pairs={{0,4},{4,0},{8,12},{12,8},{1,5},{5,1},{9,13},{13,9},{2,6},{6,2},{1... | collective-permute-start | bytes 1179656 | tf_op jit(solution)/shard_map/ppermute | solution.py:180
  85.7 2.6 %collective-permute-start.22 = (bf16[128,1536]{1,0:T(8,128)(2,1)S(1)}, bf16[128,1536]{1,0:T(8,128)(2,1)S(1)}, u32[]{:S(2)}, u32[]{:S(2)}) collective-permute-start(bf16[128,1536]{1,0:T(8,128)(2,1)S(1)} %get-tuple-element.27), channel_id=1, source_target_pairs={{0,4},{4,0},{8,12},{12,8},{1,5},{5,1},{9,13},{13,9},{2,6},{6,2},{1... | collective-permute-start | bytes 1179656 | tf_op jit(solution)/shard_map/ppermute | solution.py:180
  86.6 2.2 %collective-permute-start.21 = (bf16[128,1536]{1,0:T(8,128)(2,1)S(1)}, bf16[128,1536]{1,0:T(8,128)(2,1)S(1)}, u32[]{:S(2)}, u32[]{:S(2)}) collective-permute-start(bf16[128,1536]{1,0:T(8,128)(2,1)S(1)} %get-tuple-element.28), channel_id=1, source_target_pairs={{0,4},{4,0},{8,12},{12,8},{1,5},{5,1},{9,13},{13,9},{2,6},{6,2},{1... | collective-permute-start | bytes 1179656 | tf_op jit(solution)/shard_map/ppermute | solution.py:180
  95.1 1.9 %collective-permute-start.25 = (bf16[512,512]{1,0:T(8,128)(2,1)S(1)}, bf16[512,512]{1,0:T(8,128)(2,1)S(1)}, u32[]{:S(2)}, u32[]{:S(2)}) collective-permute-start(bf16[512,512]{1,0:T(8,128)(2,1)S(1)} %collective-permute-done.8.refs_1_), channel_id=1, source_target_pairs={{0,4},{4,0},{8,12},{12,8},{1,5},{5,1},{9,13},{13,9},{2,6},{6,2},{1... | collective-permute-start | bytes 1572872 | tf_op jit(solution)/shard_map/ppermute | solution.py:180

commit v5 on v4

--- a/solution.py
+++ b/solution.py
@@ -65,11 +65,16 @@
 ANY = pl.BlockSpec(memory_space=pl.ANY)
 
 
-def by_columns(name, body, args, rows, start, size, step, width, probe, terms=None, image=None, dtype=BF16):
+def by_columns(name, body, args, rows, start, size, step, width, probe=0, terms=None, image=None, dtype=BF16):
     vmem = pl.BlockSpec(memory_space=pltpu.VMEM)
     args = list(args) + list(terms or ())
     specs = [vmem] * len(args)
     used = len(args)
+    blocks, column = [], start
+    while column < start + size:
+        length = min(step, width - column % width, start + size - column)
+        blocks.append((slice(column - start, column - start + length), *divmod(column, width), length))
+        column += length
     aliases, scratch = {}, []
     if image is None:
         out_shape = jax.ShapeDtypeStruct((rows, size), dtype)
@@ -81,28 +86,24 @@
             specs.append(ANY)
         out_shape = jax.ShapeDtypeStruct(image.shape, image.dtype)
         out_spec = ANY
-        scratch = [
-            pltpu.VMEM((size // step, rows, step), image.dtype),
-            pltpu.SemaphoreType.DMA((size // step,)),
-        ]
+        scratch = [pltpu.VMEM((rows, size), image.dtype), pltpu.SemaphoreType.DMA((len(blocks),))]
 
     def kernel(*refs):
         inputs, out = refs[:used], refs[len(args)]
         copies = []
-        for index in range(size // step):
-            column = start + index * step
-            place, site = probe + column // width, column % width
-            total = body(inputs, index * step, column // width, site)
+        for index, (columns, offset, site, length) in enumerate(blocks):
+            sites = slice(site, site + length)
+            total = body(inputs, columns, offset, sites)
             if terms is not None:
                 noise, field = inputs[used - 2 :]
-                total += noise[:, site : site + step] * field[place, :, site : site + step].astype(F32)
+                total += noise[:, sites] * field[probe + offset, :, sites].astype(F32)
             if image is None:
-                out[:, index * step : (index + 1) * step] = total.astype(dtype)
+                out[:, columns] = total.astype(dtype)
             else:
                 buffer, sems = refs[len(args) + 1 :]
-                buffer[index] = total.astype(image.dtype)
+                buffer[:, columns] = total.astype(image.dtype)
                 copy = pltpu.make_async_copy(
-                    buffer.at[index], out.at[place, :, pl.ds(site, step)], sems.at[index]
+                    buffer.at[:, columns], out.at[probe + offset, :, sites], sems.at[index]
                 )
                 copy.start()
                 copies.append(copy)
@@ -123,28 +124,23 @@
 
 
 def space(low, mid, high, band, base, start, size, width, **where):
-    half, step = width // 2, min(256, size)
-
-    def body(refs, offset, probe, site):
+    half = width // 2
+
+    def body(refs, columns, probe, sites):
         low, mid, high, band = refs[:4]
-        weights = band.at[site : site + step]
-        total = dot_t(mid[base + probe], weights[:, half : half + width])
-        total += dot_t(low[probe], weights[:, :half])
-        total += dot_t(high[probe], weights[:, half + width :])
+        total = dot_t(mid[base + probe], band[sites, half : half + width])
+        total += dot_t(low[probe], band[sites, :half])
+        total += dot_t(high[probe], band[sites, half + width :])
         return total
 
-    where = dict(dict(probe=0), **where)
-    return by_columns("space", body, [low, mid, high, band], mid.shape[1], start, size, step, width, **where)
+    return by_columns("space", body, [low, mid, high, band], mid.shape[1], start, size, 256, width, **where)
 
 
 def mix(table, blocks, width, start=0, begun=None, step=512, **where):
     rows = table.shape[0]
     flat = [piece for block in blocks.values() for piece in block]
-    size = flat[0].shape[1]
-    step = min(step, size)
-
-    def body(refs, offset, probe, site):
-        columns = slice(offset, offset + step)
+
+    def body(refs, columns, probe, sites):
         taken = 1
         total = None
         for m, block in blocks.items():
@@ -155,8 +151,7 @@
         return total if begun is None else total + refs[taken][:, columns]
 
     args = [table] + flat + ([] if begun is None else [begun])
-    where = dict(dict(probe=0), **where)
-    return by_columns("mix", body, args, rows, start, size, step, width, **where)
+    return by_columns("mix", body, args, rows, start, flat[0].shape[1], step, width, **where)
 
 
 def after(value, *others):
@@ -194,12 +189,12 @@
         order[1].extend([(-s) % count, (-1 - s) % count])
 
     def arrived(far, pieces, *others):
-        blocks = {}
+        straight, crossed = {}, {}
         for k, got in enumerate(far):
             got = after(got, *others)
-            blocks[2 + 2 * k] = [got]
-            blocks[3 + 2 * k] = to_core(got, pieces)
-        return blocks
+            straight[2 + 2 * k] = [got]
+            crossed[3 + 2 * k] = to_core(got, pieces)
+        return straight, crossed
 
     def here(own, near):
         return {0: [own], 1: near}
@@ -221,16 +216,19 @@
 
     near = [to_core(block) for block in own]
     columns = (probes - firsts) * width
-    cut = columns - half
+    last = half
+    cut = columns - last
     terms = (noise, field)
     image = jax.ShapeDtypeStruct(field.shape, field.dtype)
 
-    blocks = here(own[0], near[0]) | arrived(far[0], 2, table, band)
+    straight, crossed = arrived(far[0], 2, table, band)
+    blocks = here(own[0], near[0]) | straight | crossed
     mixed = [mix(table, blocks, width)]
     long = space(low, field, high, after(band, mixed[0]), firsts, 0, cut, width)
     far_long = to_chips(long)
     for p in range(1, firsts):
-        blocks = here(own[p], near[p]) | arrived(far[p], 2, mixed[-1], long)
+        straight, crossed = arrived(far[p], 2, mixed[-1], long)
+        blocks = here(own[p], near[p]) | straight | crossed
         mixed.append(mix(table, blocks, width))
 
     for p in range(firsts):
@@ -239,16 +237,16 @@
         image = space(got_low, middle, got_high, band, 0, 0, width, width, probe=p, terms=terms, image=image)
         if p == 0:
             near_long = to_core(after(long, image), 4)
-            short = space(low, field, high, after(band, image), firsts, cut, half, width)
+            short = space(low, field, high, after(band, image), firsts, cut, last, width)
             near_short, far_short = to_core(short), to_chips(short)
 
     at = dict(start=cut, probe=firsts)
     begun = mix(table, here(short, after(near_short, image)), width, terms=terms, dtype=F32, **at)
-    blocks = here(long, near_long) | arrived(far_long, 4, begun)
-    image = mix(table, blocks, width, probe=firsts, terms=terms, image=image)
-    blocks = arrived(far_short, 1, image)
-    straight = {m: block for m, block in blocks.items() if m % 2 == 0}
-    crossed = {m: block for m, block in blocks.items() if m % 2 == 1}
+    straight, crossed = arrived(far_long, 4, begun)
+    straight = here(long, near_long) | straight
+    sums = mix(table, straight, width, probe=firsts, terms=terms, dtype=F32)
+    image = mix(table, crossed, width, probe=firsts, begun=sums, image=image)
+    straight, crossed = arrived(far_short, 1, image)
     begun = mix(table, straight, width, begun=begun, dtype=F32, **at)
     return mix(table, crossed, width, begun=begun, image=image, step=256, **at)
 

time: 98.8 us -> 98.8 us (level)
    ppermute x16, waiting for transfers between devices: 6.12 us -> 4.02 us  [to_core(): lax.ppermute(part, 'slot', swap)]
    ppermute x4, waiting for transfers between devices: 11.8 us -> 13.6 us  [to_chips(): lax.ppermute(block, 'slot', [(i, (i + s) % count) for i in range(count)])]
    pallas_call x10 -> x11, Pallas kernels: 27.2 us -> 27.5 us  [by_columns(): pl.pallas_call(kernel, out_shape=out_shape, in_specs=specs, out_specs=out...]
  transfers between devices with their start and end apart: 26 -> 26, of which waited for: 17 -> 13; matrix products, arithmetic and copies ran while one was open for 12% -> 12% of each run, Pallas kernels for 30% -> 30%
where the time goes in v5:
time: 98.8 us; the launch traced here: 98.4 us
  Pallas kernels  31.1 us (31%)
  starting transfers between devices  29 us (29%)
  waiting for transfers between devices  24.6 us (25%)
  local copies, waits for them, and re-layouts  8.42 us (9%)
  other arithmetic  4.72 us (5%)
    pallas_call x11, Pallas kernels, by_columns(): pl.pallas_call(kernel, out_shape=out_shape, in_specs=specs, out_specs=out...  27.5 us
    ppermute x3, starting transfers between devices, halo(): lax.ppermute(block[:, :, width - half:], 'site', up)  15 us
    ppermute x4, waiting for transfers between devices, to_chips(): lax.ppermute(block, 'slot', [(i, (i + s) % count) for i in range(count)])  13.6 us
    ppermute x4, starting transfers between devices, to_chips(): lax.ppermute(block, 'slot', [(i, (i + s) % count) for i in range(count)])  6.99 us
    ppermute x16, waiting for transfers between devices, to_core(): lax.ppermute(part, 'slot', swap)  4.02 us
    select_n x1, other arithmetic, on_device(): band = jnp.where(mask, sp_weight, jnp.zeros_like(sp_weight))  4.01 us
    ppermute x3, waiting for transfers between devices, halo(): lax.ppermute(block[:, :, width - half:], 'site', up)  3.9 us
    ppermute x3, starting transfers between devices, halo(): lax.ppermute(block[:, :, :half], 'site', down)  3.86 us
  transfers between devices with their start and end apart: 26, of which 13 were waited for; matrix products, arithmetic and copies ran while one was open for 12% of the time, Pallas kernels for 30%

profile of v5, /device:TPU:0, one launch (start us, length us, event | category | flops | bytes accessed | tf_op | source)
XLA Modules:
  0.0 98.4 jit_solution(17027109001337801574)
XLA Ops:
  0.0 1.4 %slice_bitcast_fusion.1.refs_1_ = bf16[512,1024]{1,0:T(8,128)(2,1)S(1)} fusion(bf16[4,512,1024]{2,1,0:T(8,128)(2,1)} %refs_8_.1), kind=kLoop, calls=%fused_computation.5 | loop fusion | bytes 2097152 | tf_op jit(solution)/shard_map/squeeze | solution.py:206
  1.5 3.0 %collective-permute-start.3 = (bf16[512,1024]{1,0:T(8,128)(2,1)S(1)}, bf16[512,1024]{1,0:T(8,128)(2,1)}, u32[]{:S(2)}, u32[]{:S(2)}) collective-permute-start(bf16[512,1024]{1,0:T(8,128)(2,1)S(1)} %slice_bitcast_fusion.1.refs_1_), channel_id=1, source_target_pairs={{0,8},{4,12},{8,0},{12,4},{1,9},{5,13},{9,1},{13,5},{2,10},{6,14},... | collective-permute-start | bytes 3145736 | tf_op jit(solution)/shard_map/ppermute | solution.py:178
  4.5 1.3 %slice_bitcast_fusion.refs_1_ = bf16[512,1024]{1,0:T(8,128)(2,1)S(1)} fusion(bf16[4,512,1024]{2,1,0:T(8,128)(2,1)} %refs_8_.1), kind=kLoop, calls=%fused_computation.4 | loop fusion | bytes 2097152 | tf_op jit(solution)/shard_map/squeeze | solution.py:206
  5.8 0.2 collective-permute-start.12
  5.9 3.0 %fusion.2 = (bf16[2,512,512]{2,1,0:T(8,128)(2,1)}, bf16[2,512,512]{2,1,0:T(8,128)(2,1)}) fusion(bf16[4,512,1024]{2,1,0:T(8,128)(2,1)} %refs_8_.1), kind=kLoop, calls=%fused_computation.8 | loop fusion | bytes 4194304 | tf_op jit(solution)/shard_map/slice | solution.py:183
  9.0 1.3 %collective-permute-start.1 = (bf16[2,512,512]{2,1,0:T(8,128)(2,1)}, bf16[2,512,512]{2,1,0:T(8,128)(2,1)}, u32[]{:S(2)}, u32[]{:S(2)}) collective-permute-start(bf16[2,512,512]{2,1,0:T(8,128)(2,1)} %get-tuple-element.23), channel_id=1, source_target_pairs={{1,0},{2,1},{3,2},{5,4},{6,5},{7,6},{9,8},{10,9},{11,10},{13,12},{... | collective-permute-start | bytes 3145736 | tf_op jit(solution)/shard_map/ppermute | solution.py:183
  10.3 5.5 %collective-permute-start = (bf16[2,512,512]{2,1,0:T(8,128)(2,1)}, bf16[2,512,512]{2,1,0:T(8,128)(2,1)}, u32[]{:S(2)}, u32[]{:S(2)}) collective-permute-start(bf16[2,512,512]{2,1,0:T(8,128)(2,1)} %get-tuple-element.24), channel_id=1, source_target_pairs={{0,1},{1,2},{2,3},{4,5},{5,6},{6,7},{8,9},{9,10},{10,11},{12,13},{... | collective-permute-start | bytes 3145736 | tf_op jit(solution)/shard_map/ppermute | solution.py:182
  15.8 4.0 %fusion.1.refs_3_ = bf16[1024,2048]{1,0:T(8,128)(2,1)} fusion(bf16[1024,2048]{1,0:T(8,128)(2,1)S(1)} %copy-done.3, s32[1024]{0:T(1024)S(1)} %broadcast_add_fusion, s32[1024]{0:T(1024)S(1)} %copy-done.4), kind=kLoop, calls=%fused_computation.3 | loop fusion | flops 8388608 | bytes 8396800 | tf_op jit(solution)/shard_map/jit(_where)/select_n | solution.py:215
  19.8 0.5 slice.33
  20.4 0.1 slice.34
  20.5 0.1 reverse
  20.5 0.1 slice.49
  20.6 0.7 maximum_convert_fusion.row_ref
  21.3 3.6 %time_table.1.refs_0_ = bf16[512,2048]{1,0:T(8,128)(2,1)S(1)} custom-call(s32[1]{0:T(128)} %bitcast.core_ref, f32[1,2048]{1,0:T(1,128)S(1)} %maximum_convert_fusion.row_ref), custom_call_target="tpu_custom_call" | custom-call | tf_op jit(solution)/shard_map/time_table/pallas_call | solution.py:51
  24.9 3.6 %collective-permute-done.3.refs_3_ = bf16[512,1024]{1,0:T(8,128)(2,1)} collective-permute-done((bf16[512,1024]{1,0:T(8,128)(2,1)S(1)}, bf16[512,1024]{1,0:T(8,128)(2,1)}, u32[]{:S(2)}, u32[]{:S(2)}) %collective-permute-start.3) | collective-permute-done | bytes 1048608 | tf_op jit(solution)/shard_map/ppermute | solution.py:178
  28.6 1.4 %fusion.8 = (bf16[256,1024]{1,0:T(8,128)(2,1)S(1)}, bf16[256,1024]{1,0:T(8,128)(2,1)S(1)}) fusion(bf16[512,1024]{1,0:T(8,128)(2,1)} %collective-permute-done.3.refs_3_), kind=kLoop, calls=%fused_computation.14 | loop fusion | bytes 2097152 | tf_op jit(solution)/shard_map/split | solution.py:175
  30.0 0.0 copy-start
  30.0 0.1 collective-permute-start.5
  30.1 0.5 collective-permute-start.4
  30.6 1.4 %collective-permute-done.5.refs_5_ = bf16[256,1024]{1,0:T(8,128)(2,1)S(1)} collective-permute-done((bf16[256,1024]{1,0:T(8,128)(2,1)S(1)}, bf16[256,1024]{1,0:T(8,128)(2,1)S(1)}, u32[]{:S(2)}, u32[]{:S(2)}) %collective-permute-start.5) | collective-permute-done | bytes 524320 | tf_op jit(solution)/shard_map/ppermute | solution.py:175
  32.0 0.1 collective-permute-start.11
  32.1 0.6 collective-permute-done.4.refs_4_
  32.7 3.9 %mix.7 = bf16[512,1024]{1,0:T(8,128)(2,1)S(1)} custom-call(bf16[512,2048]{1,0:T(8,128)(2,1)S(1)} %time_table.1.refs_0_, bf16[512,1024]{1,0:T(8,128)(2,1)S(1)} %slice_bitcast_fusion.1.refs_1_, bf16[512,1024]{1,0:T(8,128)(2,1)} %collective-permute-done.2.refs_2_, bf16[512,1024]{1,0:T(8,128)(2,1)} %collective-permute-done.3.refs_3_, ...), custom_call_target="tpu_custom_call" | custom-call | tf_op jit(solution)/shard_map/mix/pallas_call | solution.py:113
  36.6 0.1 collective-permute-done.1.refs_2_
  36.7 1.2 %collective-permute-done.refs_0_ = bf16[2,512,512]{2,1,0:T(8,128)(2,1)} collective-permute-done((bf16[2,512,512]{2,1,0:T(8,128)(2,1)}, bf16[2,512,512]{2,1,0:T(8,128)(2,1)}, u32[]{:S(2)}, u32[]{:S(2)}) %collective-permute-start) | collective-permute-done | bytes 1048608 | tf_op jit(solution)/shard_map/ppermute | solution.py:182
  37.9 5.0 %space.6.refs_1_ = bf16[512,1536]{1,0:T(8,128)(2,1)S(1)} custom-call(bf16[2,512,512]{2,1,0:T(8,128)(2,1)} %collective-permute-done.refs_0_, bf16[4,512,1024]{2,1,0:T(8,128)(2,1)S(1)} %copy-done, bf16[2,512,512]{2,1,0:T(8,128)(2,1)} %collective-permute-done.1.refs_2_, bf16[1024,2048]{1,0:T(8,128)(2,1)S(1)} %copy-done.1), custom_call_target="tpu_custom_call" | custom-call | tf_op jit(solution)/shard_map/space/pallas_call | solution.py:113
  43.0 1.7 %collective-permute-start.9 = (bf16[512,1536]{1,0:T(8,128)(2,1)S(1)}, bf16[512,1536]{1,0:T(8,128)(2,1)S(1)}, u32[]{:S(2)}, u32[]{:S(2)}) collective-permute-start(bf16[512,1536]{1,0:T(8,128)(2,1)S(1)} %space.6.refs_1_), channel_id=1, source_target_pairs={{0,8},{4,12},{8,0},{12,4},{1,9},{5,13},{9,1},{13,5},{2,10},{6,14},... | collective-permute-start | bytes 4718600 | tf_op jit(solution)/shard_map/ppermute | solution.py:178
  44.7 6.2 %collective-permute-done.12.refs_3_ = bf16[512,1024]{1,0:T(8,128)(2,1)S(1)} collective-permute-done((bf16[512,1024]{1,0:T(8,128)(2,1)S(1)}, bf16[512,1024]{1,0:T(8,128)(2,1)S(1)}, u32[]{:S(2)}, u32[]{:S(2)}) %collective-permute-start.12) | collective-permute-done | bytes 1048608 | tf_op jit(solution)/shard_map/ppermute | solution.py:178
  50.9 0.1 fusion.6
  51.0 0.1 collective-permute-start.14
  51.1 0.5 collective-permute-start.13
  51.6 0.1 fusion.7
  51.7 1.3 %collective-permute-start.7 = (bf16[1,512,512]{2,1,0:T(8,128)(2,1)S(1)}, bf16[1,512,512]{2,1,0:T(8,128)(2,1)S(1)}, u32[]{:S(2)}, u32[]{:S(2)}) collective-permute-start(bf16[1,512,512]{2,1,0:T(8,128)(2,1)S(1)} %get-tuple-element.37), channel_id=1, source_target_pairs={{1,0},{2,1},{3,2},{5,4},{6,5},{7,6},{9,8},{10,9},{11,10},{13,12},{... | collective-permute-start | bytes 1572872 | tf_op jit(solution)/shard_map/ppermute | solution.py:183
  53.0 0.0 copy-start.2
  53.0 4.7 %collective-permute-start.6 = (bf16[1,512,512]{2,1,0:T(8,128)(2,1)S(1)}, bf16[1,512,512]{2,1,0:T(8,128)(2,1)S(1)}, u32[]{:S(2)}, u32[]{:S(2)}) collective-permute-start(bf16[1,512,512]{2,1,0:T(8,128)(2,1)S(1)} %get-tuple-element.38), channel_id=1, source_target_pairs={{0,1},{1,2},{2,3},{4,5},{5,6},{6,7},{8,9},{9,10},{10,11},{12,13},{... | collective-permute-start | bytes 1572872 | tf_op jit(solution)/shard_map/ppermute | solution.py:182
  57.7 2.4 %mix.8 = bf16[512,1024]{1,0:T(8,128)(2,1)S(1)} custom-call(bf16[512,2048]{1,0:T(8,128)(2,1)S(1)} %time_table.1.refs_0_, bf16[512,1024]{1,0:T(8,128)(2,1)S(1)} %slice_bitcast_fusion.refs_1_, bf16[512,1024]{1,0:T(8,128)(2,1)S(1)} %collective-permute-done.11.refs_2_, bf16[512,1024]{1,0:T(8,128)(2,1)S(1)} %collective-permute-done.12.refs_3_, ...), custom_call_target="tpu_custom_call" | custom-call | tf_op jit(solution)/shard_map/mix/pallas_call | solution.py:113
  60.1 0.1 fusion.5
  60.1 1.3 %collective-permute-start.16 = (bf16[1,512,512]{2,1,0:T(8,128)(2,1)S(1)}, bf16[1,512,512]{2,1,0:T(8,128)(2,1)S(1)}, u32[]{:S(2)}, u32[]{:S(2)}) collective-permute-start(bf16[1,512,512]{2,1,0:T(8,128)(2,1)S(1)} %get-tuple-element.33), channel_id=1, source_target_pairs={{1,0},{2,1},{3,2},{5,4},{6,5},{7,6},{9,8},{10,9},{11,10},{13,12},{... | collective-permute-start | bytes 1572872 | tf_op jit(solution)/shard_map/ppermute | solution.py:183
  61.4 4.8 %collective-permute-start.15 = (bf16[1,512,512]{2,1,0:T(8,128)(2,1)S(1)}, bf16[1,512,512]{2,1,0:T(8,128)(2,1)S(1)}, u32[]{:S(2)}, u32[]{:S(2)}) collective-permute-start(bf16[1,512,512]{2,1,0:T(8,128)(2,1)S(1)} %get-tuple-element.34), channel_id=1, source_target_pairs={{0,1},{1,2},{2,3},{4,5},{5,6},{6,7},{8,9},{9,10},{10,11},{12,13},{... | collective-permute-start | bytes 1572872 | tf_op jit(solution)/shard_map/ppermute | solution.py:182
  66.2 2.2 %collective-permute-done.7.refs_2_ = bf16[1,512,512]{2,1,0:T(8,128)(2,1)S(1)} collective-permute-done((bf16[1,512,512]{2,1,0:T(8,128)(2,1)S(1)}, bf16[1,512,512]{2,1,0:T(8,128)(2,1)S(1)}, u32[]{:S(2)}, u32[]{:S(2)}) %collective-permute-start.7) | collective-permute-done | bytes 524320 | tf_op jit(solution)/shard_map/ppermute | solution.py:183
  68.4 1.5 %collective-permute-done.6.refs_0_ = bf16[1,512,512]{2,1,0:T(8,128)(2,1)S(1)} collective-permute-done((bf16[1,512,512]{2,1,0:T(8,128)(2,1)S(1)}, bf16[1,512,512]{2,1,0:T(8,128)(2,1)S(1)}, u32[]{:S(2)}, u32[]{:S(2)}) %collective-permute-start.6) | collective-permute-done | bytes 524320 | tf_op jit(solution)/shard_map/ppermute | solution.py:182
  69.9 3.3 %space.4.refs_6_ = bf16[4,512,1024]{2,1,0:T(8,128)(2,1)} custom-call(bf16[1,512,512]{2,1,0:T(8,128)(2,1)S(1)} %collective-permute-done.6.refs_0_, bf16[1,512,1024]{2,1,0:T(8,128)(2,1)S(1)} %bitcast.13, bf16[1,512,512]{2,1,0:T(8,128)(2,1)S(1)} %collective-permute-done.7.refs_2_, bf16[1024,2048]{1,0:T(8,128)(2,1)S(1)} %copy-done.1, f32[1,1024]{1,0:T(1,128)S(1)} %bitcast.14, ...), custom_call_target="tpu_custom_call" | custom-call | tf_op jit(solution)/shard_map/space/pallas_call | solution.py:113
  73.2 2.8 %space.5.refs_1_ = bf16[512,512]{1,0:T(8,128)(2,1)S(1)} custom-call(bf16[2,512,512]{2,1,0:T(8,128)(2,1)} %collective-permute-done.refs_0_, bf16[4,512,1024]{2,1,0:T(8,128)(2,1)S(1)} %copy-done, bf16[2,512,512]{2,1,0:T(8,128)(2,1)} %collective-permute-done.1.refs_2_, bf16[1024,2048]{1,0:T(8,128)(2,1)S(1)} %copy-done.1), custom_call_target="tpu_custom_call" | custom-call | tf_op jit(solution)/shard_map/space/pallas_call | solution.py:113
  76.1 0.1 collective-permute-start.10
  76.1 2.1 %collective-permute-start.8 = (bf16[512,512]{1,0:T(8,128)(2,1)S(1)}, bf16[512,512]{1,0:T(8,128)(2,1)S(1)}, u32[]{:S(2)}, u32[]{:S(2)}) collective-permute-start(bf16[512,512]{1,0:T(8,128)(2,1)S(1)} %space.5.refs_1_), channel_id=1, source_target_pairs={{0,8},{4,12},{8,0},{12,4},{1,9},{5,13},{9,1},{13,5},{2,10},{6,14},... | collective-permute-start | bytes 1572872 | tf_op jit(solution)/shard_map/ppermute | solution.py:178
  78.2 0.1 fusion.3
  78.3 0.8 collective-permute-done.16.refs_2_
  79.1 1.2 %collective-permute-done.15.refs_0_ = bf16[1,512,512]{2,1,0:T(8,128)(2,1)S(1)} collective-permute-done((bf16[1,512,512]{2,1,0:T(8,128)(2,1)S(1)}, bf16[1,512,512]{2,1,0:T(8,128)(2,1)S(1)}, u32[]{:S(2)}, u32[]{:S(2)}) %collective-permute-start.15) | collective-permute-done | bytes 524320 | tf_op jit(solution)/shard_map/ppermute | solution.py:182
  80.3 3.3 %space.7.refs_6_ = bf16[4,512,1024]{2,1,0:T(8,128)(2,1)} custom-call(bf16[1,512,512]{2,1,0:T(8,128)(2,1)S(1)} %collective-permute-done.15.refs_0_, bf16[1,512,1024]{2,1,0:T(8,128)(2,1)S(1)} %bitcast.11, bf16[1,512,512]{2,1,0:T(8,128)(2,1)S(1)} %collective-permute-done.16.refs_2_, bf16[1024,2048]{1,0:T(8,128)(2,1)S(1)} %copy-done.1, ...), custom_call_target="tpu_custom_call", output_to_operand_aliasing={{}: (6, {})} | custom-call | tf_op jit(solution)/shard_map/space/pallas_call | solution.py:113
  83.6 0.6 collective-permute-start.22
  84.1 0.7 mix.9.refs_2_
  84.9 0.1 collective-permute-start.21
  84.9 0.1 fusion.4
  85.1 0.6 collective-permute-start.20
  85.6 0.1 collective-permute-start.19
  85.7 0.4 collective-permute-start.18
  86.1 0.5 collective-permute-done.21.refs_2_
  86.6 0.1 collective-permute-start.17
  86.8 2.6 %mix.10.refs_5_ = f32[512,1536]{1,0:T(8,128)S(1)} custom-call(bf16[512,2048]{1,0:T(8,128)(2,1)S(1)} %time_table.1.refs_0_, bf16[512,1536]{1,0:T(8,128)(2,1)S(1)} %space.6.refs_1_, bf16[128,1536]{1,0:T(8,128)(2,1)S(1)} %collective-permute-done.21.refs_2_, bf16[128,1536]{1,0:T(8,128)(2,1)S(1)} %collective-permute-done.22.refs_3_, ...), custom_call_target="tpu_custom_call" | custom-call | tf_op jit(solution)/shard_map/mix/pallas_call | solution.py:113
  89.4 1.9 %mix.11.refs_3_ = bf16[4,512,1024]{2,1,0:T(8,128)(2,1)} custom-call(bf16[512,2048]{1,0:T(8,128)(2,1)S(1)} %time_table.1.refs_0_, bf16[128,1536]{1,0:T(8,128)(2,1)S(1)} %collective-permute-done.17.refs_1_, bf16[128,1536]{1,0:T(8,128)(2,1)S(1)} %collective-permute-done.18.refs_2_, ...), custom_call_target="tpu_custom_call", output_to_operand_aliasing={{}: (6, {})} | custom-call | tf_op jit(solution)/shard_map/mix/pallas_call | solution.py:113
  91.3 3.8 %collective-permute-done.8.refs_1_ = bf16[512,512]{1,0:T(8,128)(2,1)S(1)} collective-permute-done((bf16[512,512]{1,0:T(8,128)(2,1)S(1)}, bf16[512,512]{1,0:T(8,128)(2,1)S(1)}, u32[]{:S(2)}, u32[]{:S(2)}) %collective-permute-start.8) | collective-permute-done | bytes 524320 | tf_op jit(solution)/shard_map/ppermute | solution.py:178
  95.1 0.4 mix.12.refs_2_
  95.5 1.5 %collective-permute-done.25.refs_1_ = bf16[512,512]{1,0:T(8,128)(2,1)S(1)} collective-permute-done((bf16[512,512]{1,0:T(8,128)(2,1)S(1)}, bf16[512,512]{1,0:T(8,128)(2,1)S(1)}, u32[]{:S(2)}, u32[]{:S(2)}) %collective-permute-start.25) | collective-permute-done | bytes 524320 | tf_op jit(solution)/shard_map/ppermute | solution.py:175
  97.0 1.2 %mix.13 = bf16[4,512,1024]{2,1,0:T(8,128)(2,1)} custom-call(bf16[512,2048]{1,0:T(8,128)(2,1)S(1)} %time_table.1.refs_0_, bf16[512,512]{1,0:T(8,128)(2,1)S(1)} %collective-permute-done.25.refs_1_, f32[512,512]{1,0:T(8,128)S(1)} %mix.12.refs_2_, bf16[4,512,1024]{2,1,0:T(8,128)(2,1)} %mix.11.refs_3_), custom_call_target="tpu_custom_call", output_to_operand_aliasing={{}: (3, {})} | custom-call | tf_op jit(solution)/shard_map/mix/pallas_call | solution.py:113
  (29 shorter events, 0.1 us)
Async XLA Ops:
  0.0 15.8 %copy-start.4 = (s32[1024]{0:T(1024)S(1)}, s32[1024]{0:T(1024)}, u32[]{:S(2)}) copy-start(s32[1024]{0:T(1024)} %param.8) | copy-start | bytes 12292
  0.0 15.8 %copy-start.3 = (bf16[1024,2048]{1,0:T(8,128)(2,1)S(1)}, bf16[1024,2048]{1,0:T(8,128)(2,1)}, u32[]{:S(2)}) copy-start(bf16[1024,2048]{1,0:T(8,128)(2,1)} %param.7) | copy-start | bytes 12582916
  1.5 27.1 %collective-permute-start.3 = (bf16[512,1024]{1,0:T(8,128)(2,1)S(1)}, bf16[512,1024]{1,0:T(8,128)(2,1)}, u32[]{:S(2)}, u32[]{:S(2)}) collective-permute-start(bf16[512,1024]{1,0:T(8,128)(2,1)S(1)} %slice_bitcast_fusion.1.refs_1_), channel_id=1, source_target_pairs={{0,8},{4,12},{8,0},{12,4},{1,9},{5,13},{9,1},{13,5},{2,10},{6,14},... | collective-permute-start | bytes 3145736 | tf_op jit(solution)/shard_map/ppermute | solution.py:178
  4.5 25.6 %collective-permute-start.2 = (bf16[512,1024]{1,0:T(8,128)(2,1)S(1)}, bf16[512,1024]{1,0:T(8,128)(2,1)}, u32[]{:S(2)}, u32[]{:S(2)}) collective-permute-start(bf16[512,1024]{1,0:T(8,128)(2,1)S(1)} %slice_bitcast_fusion.1.refs_1_), channel_id=1, source_target_pairs={{0,4},{4,0},{8,12},{12,8},{1,5},{5,1},{9,13},{13,9},{2,6},{6,2},{1... | collective-permute-start | bytes 3145736 | tf_op jit(solution)/shard_map/ppermute | solution.py:175
  5.8 45.2 %collective-permute-start.12 = (bf16[512,1024]{1,0:T(8,128)(2,1)S(1)}, bf16[512,1024]{1,0:T(8,128)(2,1)S(1)}, u32[]{:S(2)}, u32[]{:S(2)}) collective-permute-start(bf16[512,1024]{1,0:T(8,128)(2,1)S(1)} %slice_bitcast_fusion.refs_1_), channel_id=1, source_target_pairs={{0,8},{4,12},{8,0},{12,4},{1,9},{5,13},{9,1},{13,5},{2,10},{6,14},... | collective-permute-start | bytes 3145736 | tf_op jit(solution)/shard_map/ppermute | solution.py:178
  9.0 27.7 %collective-permute-start.1 = (bf16[2,512,512]{2,1,0:T(8,128)(2,1)}, bf16[2,512,512]{2,1,0:T(8,128)(2,1)}, u32[]{:S(2)}, u32[]{:S(2)}) collective-permute-start(bf16[2,512,512]{2,1,0:T(8,128)(2,1)} %get-tuple-element.23), channel_id=1, source_target_pairs={{1,0},{2,1},{3,2},{5,4},{6,5},{7,6},{9,8},{10,9},{11,10},{13,12},{... | collective-permute-start | bytes 3145736 | tf_op jit(solution)/shard_map/ppermute | solution.py:183
  10.3 27.6 %collective-permute-start = (bf16[2,512,512]{2,1,0:T(8,128)(2,1)}, bf16[2,512,512]{2,1,0:T(8,128)(2,1)}, u32[]{:S(2)}, u32[]{:S(2)}) collective-permute-start(bf16[2,512,512]{2,1,0:T(8,128)(2,1)} %get-tuple-element.24), channel_id=1, source_target_pairs={{0,1},{1,2},{2,3},{4,5},{5,6},{6,7},{8,9},{9,10},{10,11},{12,13},{... | collective-permute-start | bytes 3145736 | tf_op jit(solution)/shard_map/ppermute | solution.py:182
  15.8 4.0 %copy-start.5 = (bf16[2048]{0:T(1024)(128)(2,1)S(1)}, bf16[2048]{0:T(1024)(128)(2,1)}, u32[]{:S(2)}) copy-start(bf16[2048]{0:T(1024)(128)(2,1)} %param.6) | copy-start | bytes 12292
  28.6 9.3 %copy-start.1 = (bf16[1024,2048]{1,0:T(8,128)(2,1)S(1)}, bf16[1024,2048]{1,0:T(8,128)(2,1)}, u32[]{:S(2)}) copy-start(bf16[1024,2048]{1,0:T(8,128)(2,1)} %fusion.1.refs_3_) | copy-start | bytes 12582916
  30.0 7.9 %copy-start = (bf16[4,512,1024]{2,1,0:T(8,128)(2,1)S(1)}, bf16[4,512,1024]{2,1,0:T(8,128)(2,1)}, u32[]{:S(2)}) copy-start(bf16[4,512,1024]{2,1,0:T(8,128)(2,1)} %refs_8_.1) | copy-start | bytes 12582916
  30.0 2.0 %collective-permute-start.5 = (bf16[256,1024]{1,0:T(8,128)(2,1)S(1)}, bf16[256,1024]{1,0:T(8,128)(2,1)S(1)}, u32[]{:S(2)}, u32[]{:S(2)}) collective-permute-start(bf16[256,1024]{1,0:T(8,128)(2,1)S(1)} %get-tuple-element.39), channel_id=1, source_target_pairs={{0,4},{4,0},{8,12},{12,8},{1,5},{5,1},{9,13},{13,9},{2,6},{6,2},{1... | collective-permute-start | bytes 1572872 | tf_op jit(solution)/shard_map/ppermute | solution.py:175
  30.1 2.6 %collective-permute-start.4 = (bf16[256,1024]{1,0:T(8,128)(2,1)S(1)}, bf16[256,1024]{1,0:T(8,128)(2,1)S(1)}, u32[]{:S(2)}, u32[]{:S(2)}) collective-permute-start(bf16[256,1024]{1,0:T(8,128)(2,1)S(1)} %get-tuple-element.40), channel_id=1, source_target_pairs={{0,4},{4,0},{8,12},{12,8},{1,5},{5,1},{9,13},{13,9},{2,6},{6,2},{1... | collective-permute-start | bytes 1572872 | tf_op jit(solution)/shard_map/ppermute | solution.py:175
  32.0 21.0 %collective-permute-start.11 = (bf16[512,1024]{1,0:T(8,128)(2,1)S(1)}, bf16[512,1024]{1,0:T(8,128)(2,1)S(1)}, u32[]{:S(2)}, u32[]{:S(2)}) collective-permute-start(bf16[512,1024]{1,0:T(8,128)(2,1)S(1)} %slice_bitcast_fusion.refs_1_), channel_id=1, source_target_pairs={{0,4},{4,0},{8,12},{12,8},{1,5},{5,1},{9,13},{13,9},{2,6},{6,2},{1... | collective-permute-start | bytes 3145736 | tf_op jit(solution)/shard_map/ppermute | solution.py:175
  43.0 41.9 %collective-permute-start.9 = (bf16[512,1536]{1,0:T(8,128)(2,1)S(1)}, bf16[512,1536]{1,0:T(8,128)(2,1)S(1)}, u32[]{:S(2)}, u32[]{:S(2)}) collective-permute-start(bf16[512,1536]{1,0:T(8,128)(2,1)S(1)} %space.6.refs_1_), channel_id=1, source_target_pairs={{0,8},{4,12},{8,0},{12,4},{1,9},{5,13},{9,1},{13,5},{2,10},{6,14},... | collective-permute-start | bytes 4718600 | tf_op jit(solution)/shard_map/ppermute | solution.py:178
  51.0 6.7 %collective-permute-start.14 = (bf16[256,1024]{1,0:T(8,128)(2,1)S(1)}, bf16[256,1024]{1,0:T(8,128)(2,1)S(1)}, u32[]{:S(2)}, u32[]{:S(2)}) collective-permute-start(bf16[256,1024]{1,0:T(8,128)(2,1)S(1)} %get-tuple-element.35), channel_id=1, source_target_pairs={{0,4},{4,0},{8,12},{12,8},{1,5},{5,1},{9,13},{13,9},{2,6},{6,2},{1... | collective-permute-start | bytes 1572872 | tf_op jit(solution)/shard_map/ppermute | solution.py:175
  51.1 6.6 %collective-permute-start.13 = (bf16[256,1024]{1,0:T(8,128)(2,1)S(1)}, bf16[256,1024]{1,0:T(8,128)(2,1)S(1)}, u32[]{:S(2)}, u32[]{:S(2)}) collective-permute-start(bf16[256,1024]{1,0:T(8,128)(2,1)S(1)} %get-tuple-element.36), channel_id=1, source_target_pairs={{0,4},{4,0},{8,12},{12,8},{1,5},{5,1},{9,13},{13,9},{2,6},{6,2},{1... | collective-permute-start | bytes 1572872 | tf_op jit(solution)/shard_map/ppermute | solution.py:175
  51.7 16.7 %collective-permute-start.7 = (bf16[1,512,512]{2,1,0:T(8,128)(2,1)S(1)}, bf16[1,512,512]{2,1,0:T(8,128)(2,1)S(1)}, u32[]{:S(2)}, u32[]{:S(2)}) collective-permute-start(bf16[1,512,512]{2,1,0:T(8,128)(2,1)S(1)} %get-tuple-element.37), channel_id=1, source_target_pairs={{1,0},{2,1},{3,2},{5,4},{6,5},{7,6},{9,8},{10,9},{11,10},{13,12},{... | collective-permute-start | bytes 1572872 | tf_op jit(solution)/shard_map/ppermute | solution.py:183
  53.0 16.9 %copy-start.2 = (f32[1024]{0:T(1024)S(1)}, f32[1024]{0:T(1024)}, u32[]{:S(2)}) copy-start(f32[1024]{0:T(1024)} %param.9) | copy-start | bytes 12292
  53.0 16.9 %collective-permute-start.6 = (bf16[1,512,512]{2,1,0:T(8,128)(2,1)S(1)}, bf16[1,512,512]{2,1,0:T(8,128)(2,1)S(1)}, u32[]{:S(2)}, u32[]{:S(2)}) collective-permute-start(bf16[1,512,512]{2,1,0:T(8,128)(2,1)S(1)} %get-tuple-element.38), channel_id=1, source_target_pairs={{0,1},{1,2},{2,3},{4,5},{5,6},{6,7},{8,9},{9,10},{10,11},{12,13},{... | collective-permute-start | bytes 1572872 | tf_op jit(solution)/shard_map/ppermute | solution.py:182
  60.1 18.9 %collective-permute-start.16 = (bf16[1,512,512]{2,1,0:T(8,128)(2,1)S(1)}, bf16[1,512,512]{2,1,0:T(8,128)(2,1)S(1)}, u32[]{:S(2)}, u32[]{:S(2)}) collective-permute-start(bf16[1,512,512]{2,1,0:T(8,128)(2,1)S(1)} %get-tuple-element.33), channel_id=1, source_target_pairs={{1,0},{2,1},{3,2},{5,4},{6,5},{7,6},{9,8},{10,9},{11,10},{13,12},{... | collective-permute-start | bytes 1572872 | tf_op jit(solution)/shard_map/ppermute | solution.py:183
  61.4 18.8 %collective-permute-start.15 = (bf16[1,512,512]{2,1,0:T(8,128)(2,1)S(1)}, bf16[1,512,512]{2,1,0:T(8,128)(2,1)S(1)}, u32[]{:S(2)}, u32[]{:S(2)}) collective-permute-start(bf16[1,512,512]{2,1,0:T(8,128)(2,1)S(1)} %get-tuple-element.34), channel_id=1, source_target_pairs={{0,1},{1,2},{2,3},{4,5},{5,6},{6,7},{8,9},{9,10},{10,11},{12,13},{... | collective-permute-start | bytes 1572872 | tf_op jit(solution)/shard_map/ppermute | solution.py:182
  76.1 7.5 %collective-permute-start.10 = (bf16[512,512]{1,0:T(8,128)(2,1)S(1)}, bf16[512,512]{1,0:T(8,128)(2,1)S(1)}, u32[]{:S(2)}, u32[]{:S(2)}) collective-permute-start(bf16[512,512]{1,0:T(8,128)(2,1)S(1)} %space.5.refs_1_), channel_id=1, source_target_pairs={{0,4},{4,0},{8,12},{12,8},{1,5},{5,1},{9,13},{13,9},{2,6},{6,2},{1... | collective-permute-start | bytes 1572872 | tf_op jit(solution)/shard_map/ppermute | solution.py:175
  76.1 18.9 %collective-permute-start.8 = (bf16[512,512]{1,0:T(8,128)(2,1)S(1)}, bf16[512,512]{1,0:T(8,128)(2,1)S(1)}, u32[]{:S(2)}, u32[]{:S(2)}) collective-permute-start(bf16[512,512]{1,0:T(8,128)(2,1)S(1)} %space.5.refs_1_), channel_id=1, source_target_pairs={{0,8},{4,12},{8,0},{12,4},{1,9},{5,13},{9,1},{13,5},{2,10},{6,14},... | collective-permute-start | bytes 1572872 | tf_op jit(solution)/shard_map/ppermute | solution.py:178
  79.1 6.0 %collective-permute-start.24 = (bf16[128,1536]{1,0:T(8,128)(2,1)S(1)}, bf16[128,1536]{1,0:T(8,128)(2,1)S(1)}, u32[]{:S(2)}, u32[]{:S(2)}) collective-permute-start(bf16[128,1536]{1,0:T(8,128)(2,1)S(1)} %get-tuple-element.25), channel_id=1, source_target_pairs={{0,4},{4,0},{8,12},{12,8},{1,5},{5,1},{9,13},{13,9},{2,6},{6,2},{1... | collective-permute-start | bytes 1179656 | tf_op jit(solution)/shard_map/ppermute | solution.py:175
  80.3 5.3 %collective-permute-start.23 = (bf16[128,1536]{1,0:T(8,128)(2,1)S(1)}, bf16[128,1536]{1,0:T(8,128)(2,1)S(1)}, u32[]{:S(2)}, u32[]{:S(2)}) collective-permute-start(bf16[128,1536]{1,0:T(8,128)(2,1)S(1)} %get-tuple-element.26), channel_id=1, source_target_pairs={{0,4},{4,0},{8,12},{12,8},{1,5},{5,1},{9,13},{13,9},{2,6},{6,2},{1... | collective-permute-start | bytes 1179656 | tf_op jit(solution)/shard_map/ppermute | solution.py:175
  83.6 2.1 %collective-permute-start.22 = (bf16[128,1536]{1,0:T(8,128)(2,1)S(1)}, bf16[128,1536]{1,0:T(8,128)(2,1)S(1)}, u32[]{:S(2)}, u32[]{:S(2)}) collective-permute-start(bf16[128,1536]{1,0:T(8,128)(2,1)S(1)} %get-tuple-element.27), channel_id=1, source_target_pairs={{0,4},{4,0},{8,12},{12,8},{1,5},{5,1},{9,13},{13,9},{2,6},{6,2},{1... | collective-permute-start | bytes 1179656 | tf_op jit(solution)/shard_map/ppermute | solution.py:175
  84.9 1.8 %collective-permute-start.21 = (bf16[128,1536]{1,0:T(8,128)(2,1)S(1)}, bf16[128,1536]{1,0:T(8,128)(2,1)S(1)}, u32[]{:S(2)}, u32[]{:S(2)}) collective-permute-start(bf16[128,1536]{1,0:T(8,128)(2,1)S(1)} %get-tuple-element.28), channel_id=1, source_target_pairs={{0,4},{4,0},{8,12},{12,8},{1,5},{5,1},{9,13},{13,9},{2,6},{6,2},{1... | collective-permute-start | bytes 1179656 | tf_op jit(solution)/shard_map/ppermute | solution.py:175
  85.1 4.3 %collective-permute-start.20 = (bf16[128,1536]{1,0:T(8,128)(2,1)S(1)}, bf16[128,1536]{1,0:T(8,128)(2,1)S(1)}, u32[]{:S(2)}, u32[]{:S(2)}) collective-permute-start(bf16[128,1536]{1,0:T(8,128)(2,1)S(1)} %get-tuple-element.29), channel_id=1, source_target_pairs={{0,4},{4,0},{8,12},{12,8},{1,5},{5,1},{9,13},{13,9},{2,6},{6,2},{1... | collective-permute-start | bytes 1179656 | tf_op jit(solution)/shard_map/ppermute | solution.py:175
  85.6 3.8 %collective-permute-start.19 = (bf16[128,1536]{1,0:T(8,128)(2,1)S(1)}, bf16[128,1536]{1,0:T(8,128)(2,1)S(1)}, u32[]{:S(2)}, u32[]{:S(2)}) collective-permute-start(bf16[128,1536]{1,0:T(8,128)(2,1)S(1)} %get-tuple-element.30), channel_id=1, source_target_pairs={{0,4},{4,0},{8,12},{12,8},{1,5},{5,1},{9,13},{13,9},{2,6},{6,2},{1... | collective-permute-start | bytes 1179656 | tf_op jit(solution)/shard_map/ppermute | solution.py:175
  85.7 3.7 %collective-permute-start.18 = (bf16[128,1536]{1,0:T(8,128)(2,1)S(1)}, bf16[128,1536]{1,0:T(8,128)(2,1)S(1)}, u32[]{:S(2)}, u32[]{:S(2)}) collective-permute-start(bf16[128,1536]{1,0:T(8,128)(2,1)S(1)} %get-tuple-element.31), channel_id=1, source_target_pairs={{0,4},{4,0},{8,12},{12,8},{1,5},{5,1},{9,13},{13,9},{2,6},{6,2},{1... | collective-permute-start | bytes 1179656 | tf_op jit(solution)/shard_map/ppermute | solution.py:175
  86.6 2.8 %collective-permute-start.17 = (bf16[128,1536]{1,0:T(8,128)(2,1)S(1)}, bf16[128,1536]{1,0:T(8,128)(2,1)S(1)}, u32[]{:S(2)}, u32[]{:S(2)}) collective-permute-start(bf16[128,1536]{1,0:T(8,128)(2,1)S(1)} %get-tuple-element.32), channel_id=1, source_target_pairs={{0,4},{4,0},{8,12},{12,8},{1,5},{5,1},{9,13},{13,9},{2,6},{6,2},{1... | collective-permute-start | bytes 1179656 | tf_op jit(solution)/shard_map/ppermute | solution.py:175
  95.1 1.9 %collective-permute-start.25 = (bf16[512,512]{1,0:T(8,128)(2,1)S(1)}, bf16[512,512]{1,0:T(8,128)(2,1)S(1)}, u32[]{:S(2)}, u32[]{:S(2)}) collective-permute-start(bf16[512,512]{1,0:T(8,128)(2,1)S(1)} %collective-permute-done.8.refs_1_), channel_id=1, source_target_pairs={{0,4},{4,0},{8,12},{12,8},{1,5},{5,1},{9,13},{13,9},{2,6},{6,2},{1... | collective-permute-start | bytes 1572872 | tf_op jit(solution)/shard_map/ppermute | solution.py:175
